TPU v7x, 256 devices: a whole 4x4x8 slice. The times are simulated.
256 devices in a mesh: dp: 16 (over y, z_lo, core), tensor: 16 (over z_hi, x).
Axes of the slice: x: 4, y: 4, z: 8 (z_hi: 4, z_lo: 2; z = z_hi * 2 + z_lo), core: 2. Of those that a mesh axis runs over, the one named last changes fastest.
Arguments:
- normed: bfloat16 [18432, 1536], P(('dp', 'tensor')), may hold values from -24 to 24
- out_grad: bfloat16 [18432, 1536], P(('dp', 'tensor')), may hold values from -24 to 24
- gate_weight: bfloat16 [1536, 8960], P(None, 'tensor'), may hold values from -0.15625 to 0.15625
- up_weight: bfloat16 [1536, 8960], P(None, 'tensor'), may hold values from -0.15625 to 0.15625
- down_weight: bfloat16 [8960, 1536], P('tensor'), may hold values from -0.0625 to 0.0625
Outputs:
- grad_input: bfloat16 [18432, 1536], P(('dp', 'tensor'))
- grad_gate: float32 [1536, 8960], P('dp', 'tensor')
- grad_up: float32 [1536, 8960], P('dp', 'tensor')
- grad_down: float32 [8960, 1536], P('tensor', 'dp')
All inputs are finite; a program needn't handle non-finite values.
Results may differ from a plain program's by a relative error of at most 0.0049.
Values may be sent and summed in bfloat16 or wider, within the bound.
No kernel may reach another device: no remote copies, remote signals or barrier semaphores. Data moves between devices by JAX's collectives and lax.ppermute only.
A program may use at most 128 MiB of HBM per device.

v0:
```python
import functools

import jax
import jax.numpy as jnp
from jax import lax
from jax.experimental import pallas as pl
from jax.experimental.pallas import tpu as pltpu
from jax.sharding import PartitionSpec as P

F32, BF16 = jnp.float32, jnp.bfloat16
VMEM = pl.BlockSpec(memory_space=pltpu.VMEM)
ANY = pl.BlockSpec(memory_space=pl.ANY)
LIMIT = 40 << 20
SHORT = pl.CostEstimate(flops=0, bytes_accessed=0, transcendentals=0)


def contract(left, right, left_dim, right_dim):
    return lax.dot_general(
        left, right, (((left_dim,), (right_dim,)), ((), ())), preferred_element_type=F32
    )


def along_x(value, step):
    return lax.ppermute(value, "tensor", [(i, i // 4 * 4 + (i + step) % 4) for i in range(16)])


def along_z(value, step):
    return lax.ppermute(value, "tensor", [(i, (i + 4 * step) % 16) for i in range(16)])


def along_y(value, step):
    return lax.ppermute(value, "dp", [(i, (i + 4 * step) % 16) for i in range(16)])


def other_z_lo(value):
    return lax.ppermute(value, "dp", [(i, i ^ 2) for i in range(16)])


def other_core(value):
    return lax.ppermute(value, "dp", [(i, i ^ 1) for i in range(16)])


def pack_body(rows, grads, after, out):
    out[0], out[1] = rows[...], grads[...]


def pack(rows, grads, after):
    return pl.pallas_call(
        pack_body,
        out_shape=jax.ShapeDtypeStruct((2, *rows.shape), rows.dtype),
        in_specs=[VMEM, VMEM, ANY],
        out_specs=VMEM,
        cost_estimate=pl.CostEstimate(flops=0, bytes_accessed=1 << 20, transcendentals=0),
        name="pack",
    )(rows, grads, after)


def partials(both, weight, outs, g):
    tokens = outs[0].shape[1]
    grad = jnp.dot(both, weight[...], preferred_element_type=F32)
    outs[0][g] = grad[:tokens]
    for i in range(1, 4):
        outs[i][g] = grad[i * tokens : (i + 1) * tokens].astype(BF16)


def partial_shapes(groups, tokens, model):
    shape = jax.ShapeDtypeStruct
    return [shape((groups, tokens, model), F32)] + [shape((groups, tokens, model), BF16)] * 3


def stage_body(groups, send, *refs):
    blocks, (weight, down), outs = refs[: 4 * groups], refs[4 * groups : 4 * groups + 2], refs[4 * groups + 2 :]
    rows_out, grads_out, both_out, hidden_out = outs[:4]
    tokens, hidden_units = blocks[0].shape[1], down.shape[0]
    for i, block in enumerate(blocks):
        rows_out[i * tokens : (i + 1) * tokens, :] = block[0]
        grads_out[i * tokens : (i + 1) * tokens, :] = block[1]
    for g in range(groups):
        part_of = pl.ds(g * 4 * tokens, 4 * tokens)
        gate_up = contract(rows_out[part_of, :], weight[...], 1, 1)
        part = contract(grads_out[part_of, :], down[...], 1, 1)
        gate, up = gate_up[:, :hidden_units], gate_up[:, hidden_units:]
        sig = jax.nn.sigmoid(gate)
        act = gate * sig
        hidden_out[part_of, :] = (act * up).astype(BF16)
        dgate = (part * up * sig * (1.0 + gate * (1.0 - sig))).astype(BF16)
        dup = (part * act).astype(BF16)
        both = jnp.concatenate((dgate, dup), axis=1)
        both_out[part_of, :] = both
        if send:
            partials(both, weight, outs[4:], g)


def stage(blocks, weight, down, send):
    groups = len(blocks) // 4
    tokens, model = blocks[0].shape[1:]
    hidden_units = down.shape[0]
    m = len(blocks) * tokens
    shape = jax.ShapeDtypeStruct
    outs = [shape((m, model), BF16)] * 2 + [shape((m, 2 * hidden_units), BF16), shape((m, hidden_units), BF16)]
    if send:
        outs += partial_shapes(groups, tokens, model)
    return pl.pallas_call(
        functools.partial(stage_body, groups, send),
        out_shape=outs,
        in_specs=[VMEM] * (len(blocks) + 2),
        out_specs=[VMEM] * len(outs),
        compiler_params=pltpu.CompilerParams(vmem_limit_bytes=LIMIT),
        cost_estimate=pl.CostEstimate(
            flops=10 * m * model * hidden_units, bytes_accessed=groups * (6 << 20), transcendentals=m * hidden_units
        ),
        name="stage",
    )(*blocks, weight, down)


def late_body(groups, *refs):
    outs = refs[-4:]
    for g in range(groups):
        partials(refs[g][...], refs[groups], outs, g)


def late_partials(both, weight, *after):
    groups, m, model = len(both), both[0].shape[0], weight.shape[1]
    return pl.pallas_call(
        functools.partial(late_body, groups),
        out_shape=partial_shapes(groups, m // 4, model),
        in_specs=[VMEM] * (groups + 1) + [ANY] * len(after),
        out_specs=[VMEM] * 4,
        compiler_params=pltpu.CompilerParams(vmem_limit_bytes=LIMIT),
        cost_estimate=SHORT,
        name="late_partials",
    )(*both, weight, *after)


def weight_body(has_total, n_args, last, place, *refs):
    left, right = refs[0], refs[1]
    total = contract(left[...], right[...], 0, 0)
    if has_total:
        total = total + refs[2][...]
    outs = refs[n_args:]
    if not last:
        outs[0][...] = total
        return
    send, keep, held = outs
    core, part = place[0], keep.shape[2]
    held[...] = total
    for z in range(2):
        mine = pl.ds(pl.multiple_of(z * 2 * part + core * part, 32), part)
        others = pl.ds(pl.multiple_of(z * 2 * part + (1 - core) * part, 32), part)
        keep[0, z] = held[mine, :]
        send[0, z] = held[others, :].astype(BF16)


def weight_grad(place, left, right, total, last, after=None):
    m, model = left.shape
    n = right.shape[1]
    chunk, part = model // 4, model // 16
    shape = jax.ShapeDtypeStruct

    in_specs = [
        pl.BlockSpec((m, chunk), lambda r, place: (0, r)),
        pl.BlockSpec((m, n), lambda r, place: (0, 0)),
    ]
    args = [left, right]
    if total is not None:
        in_specs.append(pl.BlockSpec((chunk, n), lambda r, place: (r, 0)))
        args.append(total)
    if after is not None:
        in_specs.append(ANY)
        args.append(after)
    if last:
        out_specs = [pl.BlockSpec((1, 2, part, n), lambda r, place: (r, 0, 0, 0))] * 2
        out_shape = [shape((4, 2, part, n), BF16), shape((4, 2, part, n), F32)]
        scratch = [pltpu.VMEM((chunk, n), F32)]
    else:
        out_specs = [pl.BlockSpec((chunk, n), lambda r, place: (r, 0))]
        out_shape = [shape((model, n), F32)]
        scratch = []
    return pl.pallas_call(
        functools.partial(weight_body, total is not None, len(args), last),
        grid_spec=pltpu.PrefetchScalarGridSpec(
            num_scalar_prefetch=1, grid=(4,), in_specs=in_specs, out_specs=out_specs, scratch_shapes=scratch
        ),
        out_shape=out_shape,
        compiler_params=pltpu.CompilerParams(vmem_limit_bytes=LIMIT),
        cost_estimate=SHORT if last else pl.CostEstimate(flops=2 * m * model * n, bytes_accessed=8 * model * n, transcendentals=0),
        name="weight_grad",
    )(place, *args)


def add_body(place, got, mine_out, others_out):
    z_lo = place[1]
    for out, z in ((mine_out, z_lo), (others_out, 1 - z_lo)):
        total = got[0, z].astype(F32)
        for y in range(1, 4):
            total = total + got[y, z].astype(F32)
        out[...] = total.astype(out.dtype)


def add_chunks(place, got):
    part, n = got.shape[2:]
    shape = jax.ShapeDtypeStruct
    return pl.pallas_call(
        add_body,
        out_shape=[shape((part, n), F32), shape((part, n), BF16)],
        in_specs=[pl.BlockSpec(memory_space=pltpu.SMEM), VMEM],
        out_specs=[VMEM] * 2,
        compiler_params=pltpu.CompilerParams(vmem_limit_bytes=LIMIT),
        cost_estimate=SHORT,
        name="add_chunks",
    )(place, got)


def cores_body(keep, got, *refs):
    refs[-1][...] = (keep[...] + got[...].astype(F32)).astype(BF16)


def over_cores(send, keep, *after):
    got = other_core(send)
    part, n = keep.shape[2:]
    block = pl.BlockSpec((1, 2, part, n), lambda y: (y, 0, 0, 0))
    return pl.pallas_call(
        cores_body,
        grid=(4,),
        out_shape=jax.ShapeDtypeStruct(keep.shape, BF16),
        in_specs=[block, block] + [ANY] * len(after),
        out_specs=block,
        compiler_params=pltpu.CompilerParams(vmem_limit_bytes=LIMIT),
        cost_estimate=SHORT,
        name="over_cores",
    )(keep, got, *after)


def over_y(sums):
    groups = [[y * 4 + j for y in range(4)] for j in range(4)]
    return lax.all_to_all(sums, "dp", 0, 0, axis_index_groups=groups, tiled=True)


def over_rest(got, place):
    mine, others = add_chunks(place, got)
    return mine + other_z_lo(others).astype(F32)


def add_parts_body(groups, own, left, right, far, *refs):
    for g, out in enumerate(refs[-groups:]):
        total = own[g] + left[g].astype(F32) + right[g].astype(F32) + far[g].astype(F32)
        out[...] = total.astype(out.dtype)


def scatter_x(own, to_left, to_right, to_far, types, *after):
    got = along_x(to_left, -1), along_x(to_right, 1), along_x(to_far, 2)
    return pl.pallas_call(
        functools.partial(add_parts_body, len(types)),
        out_shape=[jax.ShapeDtypeStruct(own.shape[1:], kind) for kind in types],
        in_specs=[VMEM] * 4 + [ANY] * len(after),
        out_specs=[VMEM] * len(types),
        compiler_params=pltpu.CompilerParams(vmem_limit_bytes=LIMIT),
        cost_estimate=SHORT,
        name="add_parts",
    )(own, *got, *after)


def on_device(normed, out_grad, gate_weight, up_weight, down_weight):
    replicas = lax.axis_size("dp")
    dp = lax.axis_index("dp")
    place = jnp.stack((dp % 2, dp // 2 % 2)).astype(jnp.int32)
    weight = jnp.concatenate((gate_weight.T, up_weight.T), axis=0)
    own = jnp.stack((normed, out_grad))

    below, above = along_z(own, 1), along_z(own, -1)
    left, right = along_x(own, 1), along_x(own, -1)
    again = pack(normed, out_grad, left)
    home = [own, left, right, along_x(again, 2)]
    far = along_z(again, 2)
    b_left, b_right = along_x(below, 1), along_x(below, -1)
    a_left, a_right = along_x(above, 1), along_x(above, -1)
    b_far, a_far = along_x(b_left, 1), along_x(a_right, -1)
    near = [below, b_left, b_right, b_far, above, a_left, a_right, a_far]
    away = [far, along_x(far, 1), along_x(far, -1), along_x(far, 2)]

    home = stage(home, weight, down_weight, False)
    pair, down = weight_grad(place, home[0], home[2], None, False), weight_grad(place, home[1], home[3], None, False)
    near = stage(near, weight, down_weight, True)
    pair = weight_grad(place, near[0], near[2], pair[0], False)
    down = weight_grad(place, near[1], near[3], down[0], False)
    away = stage(away, weight, down_weight, False)
    pair = weight_grad(place, away[0], away[2], pair[0], True)
    late = late_partials([away[2], home[2]], weight, pair[0])
    pair = over_cores(*pair, late[0])
    down = weight_grad(place, away[1], away[3], down[0], True, pair)
    below, above = scatter_x(*near[4:], (BF16, BF16), down[0])
    from_below, from_above = along_z(above, 1), along_z(below, -1)
    pair = over_y(pair)
    down = over_cores(*down, pair)
    far, mine = scatter_x(*late, (BF16, F32), below)
    down = over_y(down)
    from_far = along_z(far, 2)
    grad_input = mine + from_below.astype(F32) + from_above.astype(F32) + from_far.astype(F32)

    grad_pair = over_rest(pair, place) / replicas
    grad_down = over_rest(down, place) / replicas
    half = gate_weight.shape[1]
    return grad_input.astype(BF16), grad_pair[:, :half], grad_pair[:, half:], grad_down.T


def solution(mesh):
    return jax.shard_map(
        on_device,
        mesh=mesh,
        in_specs=(
            P(("dp", "tensor"), None),
            P(("dp", "tensor"), None),
            P(None, "tensor"),
            P(None, "tensor"),
            P("tensor", None),
        ),
        out_specs=(
            P(("dp", "tensor"), None),
            P("dp", "tensor"),
            P("dp", "tensor"),
            P("tensor", "dp"),
        ),
        check_vma=False,
    )
```

profile of v0, /device:TPU:8, one launch (start us, length us, event | category | flops | bytes accessed | tf_op | source)
XLA Modules:
  0.0 196.5 jit_solution(10560151693025525178)
XLA Ops:
  0.6 1.1 pad_maximum_fusion.1.refs_0_
  1.7 1.6 collective-permute-start
  3.3 3.3 %collective-permute-start.7 = (bf16[2,72,1536]{2,1,0:T(8,128)(2,1)S(1)}, bf16[2,72,1536]{2,1,0:T(8,128)(2,1)}, u32[]{:S(2)}, u32[]{:S(2)}) collective-permute-start(bf16[2,72,1536]{2,1,0:T(8,128)(2,1)S(1)} %pad_maximum_fusion.1.refs_0_), channel_id=1, source_target_pairs={{0,4},{1,5},{2,6},{3,7},{4,8},{5,9},{6,10},{7,11},{8,12},{9,13},{1... | collective-permute-start | bytes 1327112 | tf_op jit(solution)/shard_map/ppermute | solution.py:28
  6.6 3.0 %collective-permute-start.11 = (bf16[2,72,1536]{2,1,0:T(8,128)(2,1)S(1)}, bf16[2,72,1536]{2,1,0:T(8,128)(2,1)}, u32[]{:S(2)}, u32[]{:S(2)}) collective-permute-start(bf16[2,72,1536]{2,1,0:T(8,128)(2,1)S(1)} %pad_maximum_fusion.1.refs_0_), channel_id=1, source_target_pairs={{0,12},{1,13},{2,14},{3,15},{4,0},{5,1},{6,2},{7,3},{8,4},{9,5},{1... | collective-permute-start | bytes 1327112 | tf_op jit(solution)/shard_map/ppermute | solution.py:28
  9.6 1.7 collective-permute-start.5
  11.3 3.6 %collective-permute-done.after.refs_1_ = bf16[2,72,1536]{2,1,0:T(8,128)(2,1)S(1)} collective-permute-done((bf16[2,72,1536]{2,1,0:T(8,128)(2,1)S(1)}, bf16[2,72,1536]{2,1,0:T(8,128)(2,1)S(1)}, u32[]{:S(2)}, u32[]{:S(2)}) %collective-permute-start) | collective-permute-done | bytes 442400 | tf_op jit(solution)/shard_map/ppermute | solution.py:24
  15.7 1.9 pack.1
  17.6 1.8 collective-permute-start.6
  19.4 3.7 %collective-permute-done.7.refs_0_ = bf16[2,72,1536]{2,1,0:T(8,128)(2,1)} collective-permute-done((bf16[2,72,1536]{2,1,0:T(8,128)(2,1)S(1)}, bf16[2,72,1536]{2,1,0:T(8,128)(2,1)}, u32[]{:S(2)}, u32[]{:S(2)}) %collective-permute-start.7) | collective-permute-done | bytes 442400 | tf_op jit(solution)/shard_map/ppermute | solution.py:28
  23.0 1.5 collective-permute-start.8
  24.5 5.7 %collective-permute-done.11.refs_4_ = bf16[2,72,1536]{2,1,0:T(8,128)(2,1)} collective-permute-done((bf16[2,72,1536]{2,1,0:T(8,128)(2,1)S(1)}, bf16[2,72,1536]{2,1,0:T(8,128)(2,1)}, u32[]{:S(2)}, u32[]{:S(2)}) %collective-permute-start.11) | collective-permute-done | bytes 442400 | tf_op jit(solution)/shard_map/ppermute | solution.py:28
  30.2 1.7 collective-permute-start.13
  32.0 5.0 %collective-permute-start.1 = (bf16[2,72,1536]{2,1,0:T(8,128)(2,1)}, bf16[2,72,1536]{2,1,0:T(8,128)(2,1)}, u32[]{:S(2)}, u32[]{:S(2)}) collective-permute-start(bf16[2,72,1536]{2,1,0:T(8,128)(2,1)} %pack.1), channel_id=1, source_target_pairs={{0,8},{1,9},{2,10},{3,11},{4,12},{5,13},{6,14},{7,15},{8,0},{9,1},... | collective-permute-start | bytes 1327112 | tf_op jit(solution)/shard_map/ppermute | solution.py:28
  38.8 3.0 %collective-permute-start.9 = (bf16[2,72,1536]{2,1,0:T(8,128)(2,1)}, bf16[2,72,1536]{2,1,0:T(8,128)(2,1)}, u32[]{:S(2)}, u32[]{:S(2)}) collective-permute-start(bf16[2,72,1536]{2,1,0:T(8,128)(2,1)} %collective-permute-done.7.refs_0_), channel_id=1, source_target_pairs={{0,3},{1,0},{2,1},{3,2},{4,7},{5,4},{6,5},{7,6},{8,11},{9,8},{10,9... | collective-permute-start | bytes 1327112 | tf_op jit(solution)/shard_map/ppermute | solution.py:24
  41.7 1.9 collective-permute-done.13.refs_6_
  43.7 2.5 %collective-permute-start.14 = (bf16[2,72,1536]{2,1,0:T(8,128)(2,1)}, bf16[2,72,1536]{2,1,0:T(8,128)(2,1)}, u32[]{:S(2)}, u32[]{:S(2)}) collective-permute-start(bf16[2,72,1536]{2,1,0:T(8,128)(2,1)} %collective-permute-done.13.refs_6_), channel_id=1, source_target_pairs={{0,3},{1,0},{2,1},{3,2},{4,7},{5,4},{6,5},{7,6},{8,11},{9,8},{10,9... | collective-permute-start | bytes 1327112 | tf_op jit(solution)/shard_map/ppermute | solution.py:24
  46.2 2.2 %pad_maximum_fusion.refs_4_.refs_8_.refs_2_ = bf16[1120,1536]{1,0:T(8,128)(2,1)S(1)} fusion(bf16[560,1536]{1,0:T(8,128)(2,1)} %bitcast.8, bf16[560,1536]{1,0:T(8,128)(2,1)} %bitcast.9), kind=kLoop, calls=%fused_computation | loop fusion | flops 6881280 | bytes 6881280 | tf_op jit(solution)/shard_map/concatenate | solution.py:267
  48.5 5.9 %collective-permute-done.1.refs_0_ = bf16[2,72,1536]{2,1,0:T(8,128)(2,1)} collective-permute-done((bf16[2,72,1536]{2,1,0:T(8,128)(2,1)}, bf16[2,72,1536]{2,1,0:T(8,128)(2,1)}, u32[]{:S(2)}, u32[]{:S(2)}) %collective-permute-start.1) | collective-permute-done | bytes 442400 | tf_op jit(solution)/shard_map/ppermute | solution.py:28
  54.7 1.0 copy-done.17
  55.7 1.0 copy-done.19
  56.7 1.5 copy-done.24
  58.2 1.0 copy-done.27
  59.2 1.0 copy-done.29
  60.2 2.2 %stage.4 = (bf16[288,1536]{1,0:T(8,128)(2,1)S(1)}, bf16[288,1536]{1,0:T(8,128)(2,1)S(1)}, bf16[288,1120]{1,0:T(8,128)(2,1)S(1)}, bf16[288,560]{1,0:T(8,128)(2,1)S(1)}) custom-call(bf16[2,72,1536]{2,1,0:T(8,128)(2,1)S(1)} %copy-done.17, bf16[2,72,1536]{2,1,0:T(8,128)(2,1)S(1)} %copy-done.19, bf16[2,72,1536]{2,1,0:T(8,128)(2,1)S(1)} %copy-done.27, ...), custom_call_target="tpu_custom_call" | custom-call | flops 2477260800 | bytes 6291456 | tf_op jit(solution)/shard_map/stage/pallas_call | solution.py:103
  62.4 0.9 copy-done.10
  64.1 3.5 %weight_grad.6.refs_2_ = f32[1536,1120]{1,0:T(8,128)S(1)} custom-call(s32[2]{0:T(128)S(1)} %pad_add_fusion.place, bf16[288,1536]{1,0:T(8,128)(2,1)S(1)} %get-tuple-element.41.refs_0_, bf16[288,1120]{1,0:T(8,128)(2,1)S(1)} %get-tuple-element.37.refs_1_), custom_call_target="tpu_custom_call" | custom-call | flops 990904320 | bytes 13762560 | tf_op jit(solution)/shard_map/weight_grad/pallas_call | solution.py:179
  67.6 2.8 %copy-done = f32[1536,1120]{1,0:T(8,128)} copy-done((f32[1536,1120]{1,0:T(8,128)}, f32[1536,1120]{1,0:T(8,128)S(1)}, u32[]{:S(2)}) %copy-start) | copy-done | bytes 6881304
  70.4 3.0 %collective-permute-start.3 = (bf16[2,72,1536]{2,1,0:T(8,128)(2,1)}, bf16[2,72,1536]{2,1,0:T(8,128)(2,1)S(1)}, u32[]{:S(2)}, u32[]{:S(2)}) collective-permute-start(bf16[2,72,1536]{2,1,0:T(8,128)(2,1)} %collective-permute-done.1.refs_0_), channel_id=1, source_target_pairs={{0,3},{1,0},{2,1},{3,2},{4,7},{5,4},{6,5},{7,6},{8,11},{9,8},{10,9... | collective-permute-start | bytes 1327112 | tf_op jit(solution)/shard_map/ppermute | solution.py:24
  73.4 9.6 %stage.5 = (bf16[576,1536]{1,0:T(8,128)(2,1)S(1)}, bf16[576,1536]{1,0:T(8,128)(2,1)S(1)}, bf16[576,1120]{1,0:T(8,128)(2,1)S(1)}, bf16[576,560]{1,0:T(8,128)(2,1)...) custom-call(bf16[2,72,1536]{2,1,0:T(8,128)(2,1)} %collective-permute, ...), custom_call_target="tpu_custom_call" | custom-call | flops 4954521600 | bytes 12582912 | tf_op jit(solution)/shard_map/stage/pallas_call | solution.py:103
  83.1 0.9 copy-done.14
  84.0 8.1 %weight_grad.7.refs_2_ = f32[1536,1120]{1,0:T(8,128)S(1)} custom-call(s32[2]{0:T(128)S(1)} %pad_add_fusion.place, bf16[576,1536]{1,0:T(8,128)(2,1)S(1)} %get-tuple-element.39.refs_0_, bf16[576,1120]{1,0:T(8,128)(2,1)S(1)} %get-tuple-element.40.refs_1_, f32[1536,1120]{1,0:T(8,128)} %copy-done), custom_call_target="tpu_custom_call" | custom-call | flops 1981808640 | bytes 13762560 | tf_op jit(solution)/shard_map/weight_grad/pallas_call | solution.py:179
  92.2 3.2 %stage.3 = (bf16[288,1536]{1,0:T(8,128)(2,1)S(1)}, bf16[288,1536]{1,0:T(8,128)(2,1)S(1)}, bf16[288,1120]{1,0:T(8,128)(2,1)S(1)}, bf16[288,560]{1,0:T(8,128)(2,1)S(1)}) custom-call(bf16[2,72,1536]{2,1,0:T(8,128)(2,1)} %collective-permute-done.1.refs_0_, bf16[2,72,1536]{2,1,0:T(8,128)(2,1)S(1)} %collective-permute-done.2.refs_1_, ...), custom_call_target="tpu_custom_call" | custom-call | flops 2477260800 | bytes 6291456 | tf_op jit(solution)/shard_map/stage/pallas_call | solution.py:103
  95.4 1.0 copy-done.12
  96.4 3.9 %weight_grad.8 = (bf16[4,2,96,1120]{3,2,1,0:T(8,128)(2,1)S(1)}, f32[4,2,96,1120]{3,2,1,0:T(8,128)S(1)}) custom-call(s32[2]{0:T(128)S(1)} %pad_add_fusion.place, bf16[288,1536]{1,0:T(8,128)(2,1)S(1)} %get-tuple-element.38.refs_0_, bf16[288,1120]{1,0:T(8,128)(2,1)S(1)} %get-tuple-element.36.refs_1_.refs_0_, f32[1536,1120]{1,0:T(8,128)S(1)} %weight_grad.7.refs_2_), custom_call_target="tpu_custom_call" | custom-call | tf_op jit(solution)/shard_map/weight_grad/pallas_call | solution.py:179
  100.5 2.5 %late_partials.1 = (f32[2,72,1536]{2,1,0:T(8,128)S(1)}, bf16[2,72,1536]{2,1,0:T(8,128)(2,1)S(1)}, bf16[2,72,1536]{2,1,0:T(8,128)(2,1)S(1)}, bf16[2,72,1536]{2,1,0:T(8,128)(2,1)S(1)}) custom-call(bf16[288,1120]{1,0:T(8,128)(2,1)S(1)} %get-tuple-element.36.refs_1_.refs_0_, bf16[288,1120]{1,0:T(8,128)(2,1)S(1)} %get-tuple-element.37.refs_1_, ...), custom_call_target="tpu_custom_call" | custom-call | tf_op jit(solution)/shard_map/late_partials/pallas_call | solution.py:124
  105.4 1.9 over_cores.2.refs_3_
  107.2 4.9 %all-to-all-start = ((bf16[4,2,96,1120]{3,2,1,0:T(8,128)(2,1)}), bf16[4,2,96,1120]{3,2,1,0:T(8,128)(2,1)S(1)}, u32[]{:S(2)}, u32[]{:S(2)}) async-start(bf16[4,2,96,1120]{3,2,1,0:T(8,128)(2,1)} %over_cores.2.refs_3_), calls=%async_computation | async-start | bytes 3538944 | tf_op jit(solution)/shard_map/all_to_all | solution.py:236
  112.1 1.7 collective-permute-start.18
  114.2 1.2 copy-done.11
  115.3 1.0 copy-done.23
  116.3 2.7 %weight_grad.9.refs_2_ = f32[1536,560]{1,0:T(8,128)S(1)} custom-call(s32[2]{0:T(128)S(1)} %pad_add_fusion.place, bf16[288,1536]{1,0:T(8,128)(2,1)S(1)} %copy-done.11, bf16[288,560]{1,0:T(8,128)(2,1)S(1)} %copy-done.23), custom_call_target="tpu_custom_call" | custom-call | flops 495452160 | bytes 6881280 | tf_op jit(solution)/shard_map/weight_grad/pallas_call | solution.py:179
  119.1 3.4 %weight_grad.10.refs_2_ = f32[1536,560]{1,0:T(8,128)S(1)} custom-call(s32[2]{0:T(128)S(1)} %pad_add_fusion.place, bf16[576,1536]{1,0:T(8,128)(2,1)S(1)} %copy-done.7, bf16[576,560]{1,0:T(8,128)(2,1)S(1)} %copy-done.15, f32[1536,560]{1,0:T(8,128)S(1)} %weight_grad.9.refs_2_), custom_call_target="tpu_custom_call" | custom-call | flops 990904320 | bytes 6881280 | tf_op jit(solution)/shard_map/weight_grad/pallas_call | solution.py:179
  122.5 3.0 %weight_grad.11 = (bf16[4,2,96,560]{3,2,1,0:T(8,128)(2,1)S(1)}, f32[4,2,96,560]{3,2,1,0:T(8,128)S(1)}) custom-call(s32[2]{0:T(128)S(1)} %pad_add_fusion.place, bf16[288,1536]{1,0:T(8,128)(2,1)S(1)} %copy-done.13, bf16[288,560]{1,0:T(8,128)(2,1)S(1)} %copy-done.21, f32[1536,560]{1,0:T(8,128)S(1)} %weight_grad.10.refs_2_, ...), custom_call_target="tpu_custom_call" | custom-call | tf_op jit(solution)/shard_map/weight_grad/pallas_call | solution.py:179
  125.6 3.6 %collective-permute-start.20 = (bf16[2,72,1536]{2,1,0:T(8,128)(2,1)S(1)}, bf16[2,72,1536]{2,1,0:T(8,128)(2,1)S(1)}, u32[]{:S(2)}, u32[]{:S(2)}) collective-permute-start(bf16[2,72,1536]{2,1,0:T(8,128)(2,1)S(1)} %copy-done.31), channel_id=1, source_target_pairs={{0,2},{1,3},{2,0},{3,1},{4,6},{5,7},{6,4},{7,5},{8,10},{9,11},{10,... | collective-permute-start | bytes 1327112 | tf_op jit(solution)/shard_map/ppermute | solution.py:24
  129.8 1.5 collective-permute-start.16
  131.7 8.6 %collective-permute-done.20.far = bf16[2,72,1536]{2,1,0:T(8,128)(2,1)S(1)} collective-permute-done((bf16[2,72,1536]{2,1,0:T(8,128)(2,1)S(1)}, bf16[2,72,1536]{2,1,0:T(8,128)(2,1)S(1)}, u32[]{:S(2)}, u32[]{:S(2)}) %collective-permute-start.20) | collective-permute-done | bytes 442400 | tf_op jit(solution)/shard_map/ppermute | solution.py:24
  140.3 0.9 add_parts.2
  141.2 8.8 %collective-permute-done.15.left = bf16[2,72,1536]{2,1,0:T(8,128)(2,1)S(1)} collective-permute-done((bf16[2,72,1536]{2,1,0:T(8,128)(2,1)S(1)}, bf16[2,72,1536]{2,1,0:T(8,128)(2,1)S(1)}, u32[]{:S(2)}, u32[]{:S(2)}) %collective-permute-start.15) | collective-permute-done | bytes 442400 | tf_op jit(solution)/shard_map/ppermute | solution.py:24
  150.0 9.0 %collective-permute-done.17.far = bf16[2,72,1536]{2,1,0:T(8,128)(2,1)S(1)} collective-permute-done((bf16[2,72,1536]{2,1,0:T(8,128)(2,1)S(1)}, bf16[2,72,1536]{2,1,0:T(8,128)(2,1)S(1)}, u32[]{:S(2)}, u32[]{:S(2)}) %collective-permute-start.17) | collective-permute-done | bytes 442400 | tf_op jit(solution)/shard_map/ppermute | solution.py:24
  159.2 4.6 %collective-permute-start.24 = (bf16[72,1536]{1,0:T(8,128)(2,1)S(1)}, bf16[72,1536]{1,0:T(8,128)(2,1)}, u32[]{:S(2)}, u32[]{:S(2)}) collective-permute-start(bf16[72,1536]{1,0:T(8,128)(2,1)S(1)} %get-tuple-element.62), channel_id=1, source_target_pairs={{0,8},{1,9},{2,10},{3,11},{4,12},{5,13},{6,14},{7,15},{8,0},{9,1},... | collective-permute-start | bytes 663560 | tf_op jit(solution)/shard_map/ppermute | solution.py:28
  163.8 3.1 %collective-permute-start.22 = (bf16[72,1536]{1,0:T(8,128)(2,1)}, bf16[72,1536]{1,0:T(8,128)(2,1)}, u32[]{:S(2)}, u32[]{:S(2)}) collective-permute-start(bf16[72,1536]{1,0:T(8,128)(2,1)} %get-tuple-element.61), channel_id=1, source_target_pairs={{0,4},{1,5},{2,6},{3,7},{4,8},{5,9},{6,10},{7,11},{8,12},{9,13},{1... | collective-permute-start | bytes 663560 | tf_op jit(solution)/shard_map/ppermute | solution.py:28
  166.9 1.3 collective-permute-start.23
  168.2 1.0 copy-done.8
  169.2 1.5 copy-done.5
  170.7 1.2 copy-done.9
  172.1 1.0 copy-done.3
  173.1 4.8 %all-to-all-start.1 = ((bf16[4,2,96,560]{3,2,1,0:T(8,128)(2,1)}), bf16[4,2,96,560]{3,2,1,0:T(8,128)(2,1)S(1)}, u32[]{:S(2)}, u32[]{:S(2)}) async-start(bf16[4,2,96,560]{3,2,1,0:T(8,128)(2,1)} %copy-done.3), calls=%async_computation.1 | async-start | bytes 1966080 | tf_op jit(solution)/shard_map/all_to_all | solution.py:236
  178.7 1.3 collective-permute-start.25
  180.5 3.6 %collective-permute-done.23 = bf16[72,1536]{1,0:T(8,128)(2,1)} collective-permute-done((bf16[72,1536]{1,0:T(8,128)(2,1)}, bf16[72,1536]{1,0:T(8,128)(2,1)}, u32[]{:S(2)}, u32[]{:S(2)}) %collective-permute-start.23) | collective-permute-done | bytes 221216 | tf_op jit(solution)/shard_map/ppermute | solution.py:28
  184.0 1.9 add_convert_fusion
  186.0 2.3 %collective-permute-done.25 = bf16[96,1120]{1,0:T(8,128)(2,1)S(1)} collective-permute-done((bf16[96,1120]{1,0:T(8,128)(2,1)S(1)}, bf16[96,1120]{1,0:T(8,128)(2,1)S(1)}, u32[]{:S(2)}, u32[]{:S(2)}) %collective-permute-start.25) | collective-permute-done | bytes 215072 | tf_op jit(solution)/shard_map/ppermute | solution.py:36
  188.4 1.7 all-to-all-done.1.got
  190.8 1.0 collective-permute-start.27
  192.6 3.2 %collective-permute-done.27 = bf16[96,560]{1,0:T(8,128)(2,1)S(1)} collective-permute-done((bf16[96,560]{1,0:T(8,128)(2,1)S(1)}, bf16[96,560]{1,0:T(8,128)(2,1)S(1)}, u32[]{:S(2)}, u32[]{:S(2)}) %collective-permute-start.27) | collective-permute-done | bytes 107552 | tf_op jit(solution)/shard_map/ppermute | solution.py:36
  (100 shorter events, 11.6 us)
Async XLA Ops:
  1.7 44.4 %copy-start.16 = (bf16[2,72,1536]{2,1,0:T(8,128)(2,1)}, bf16[2,72,1536]{2,1,0:T(8,128)(2,1)S(1)}, u32[]{:S(2)}) copy-start(bf16[2,72,1536]{2,1,0:T(8,128)(2,1)S(1)} %pad_maximum_fusion.1.refs_0_) | copy-start | bytes 1327108
  1.7 13.2 %collective-permute-start = (bf16[2,72,1536]{2,1,0:T(8,128)(2,1)S(1)}, bf16[2,72,1536]{2,1,0:T(8,128)(2,1)S(1)}, u32[]{:S(2)}, u32[]{:S(2)}) collective-permute-start(bf16[2,72,1536]{2,1,0:T(8,128)(2,1)S(1)} %pad_maximum_fusion.1.refs_0_), channel_id=1, source_target_pairs={{0,1},{1,2},{2,3},{3,0},{4,5},{5,6},{6,7},{7,4},{8,9},{9,10},{10,1... | collective-permute-start | bytes 1327112 | tf_op jit(solution)/shard_map/ppermute | solution.py:24
  3.3 19.7 %collective-permute-start.7 = (bf16[2,72,1536]{2,1,0:T(8,128)(2,1)S(1)}, bf16[2,72,1536]{2,1,0:T(8,128)(2,1)}, u32[]{:S(2)}, u32[]{:S(2)}) collective-permute-start(bf16[2,72,1536]{2,1,0:T(8,128)(2,1)S(1)} %pad_maximum_fusion.1.refs_0_), channel_id=1, source_target_pairs={{0,4},{1,5},{2,6},{3,7},{4,8},{5,9},{6,10},{7,11},{8,12},{9,13},{1... | collective-permute-start | bytes 1327112 | tf_op jit(solution)/shard_map/ppermute | solution.py:28
  6.6 23.7 %collective-permute-start.11 = (bf16[2,72,1536]{2,1,0:T(8,128)(2,1)S(1)}, bf16[2,72,1536]{2,1,0:T(8,128)(2,1)}, u32[]{:S(2)}, u32[]{:S(2)}) collective-permute-start(bf16[2,72,1536]{2,1,0:T(8,128)(2,1)S(1)} %pad_maximum_fusion.1.refs_0_), channel_id=1, source_target_pairs={{0,12},{1,13},{2,14},{3,15},{4,0},{5,1},{6,2},{7,3},{8,4},{9,5},{1... | collective-permute-start | bytes 1327112 | tf_op jit(solution)/shard_map/ppermute | solution.py:28
  9.6 27.4 %collective-permute-start.5 = (bf16[2,72,1536]{2,1,0:T(8,128)(2,1)S(1)}, bf16[2,72,1536]{2,1,0:T(8,128)(2,1)S(1)}, u32[]{:S(2)}, u32[]{:S(2)}) collective-permute-start(bf16[2,72,1536]{2,1,0:T(8,128)(2,1)S(1)} %pad_maximum_fusion.1.refs_0_), channel_id=1, source_target_pairs={{0,3},{1,0},{2,1},{3,2},{4,7},{5,4},{6,5},{7,6},{8,11},{9,8},{10,9... | collective-permute-start | bytes 1327112 | tf_op jit(solution)/shard_map/ppermute | solution.py:24
  17.6 20.4 %collective-permute-start.6 = (bf16[2,72,1536]{2,1,0:T(8,128)(2,1)}, bf16[2,72,1536]{2,1,0:T(8,128)(2,1)S(1)}, u32[]{:S(2)}, u32[]{:S(2)}) collective-permute-start(bf16[2,72,1536]{2,1,0:T(8,128)(2,1)} %pack.1), channel_id=1, source_target_pairs={{0,2},{1,3},{2,0},{3,1},{4,6},{5,7},{6,4},{7,5},{8,10},{9,11},{10,... | collective-permute-start | bytes 1327112 | tf_op jit(solution)/shard_map/ppermute | solution.py:24
  23.0 18.7 %collective-permute-start.8 = (bf16[2,72,1536]{2,1,0:T(8,128)(2,1)}, bf16[2,72,1536]{2,1,0:T(8,128)(2,1)}, u32[]{:S(2)}, u32[]{:S(2)}) collective-permute-start(bf16[2,72,1536]{2,1,0:T(8,128)(2,1)} %collective-permute-done.7.refs_0_), channel_id=1, source_target_pairs={{0,1},{1,2},{2,3},{3,0},{4,5},{5,6},{6,7},{7,4},{8,9},{9,10},{10,1... | collective-permute-start | bytes 1327112 | tf_op jit(solution)/shard_map/ppermute | solution.py:24
  30.2 13.4 %collective-permute-start.13 = (bf16[2,72,1536]{2,1,0:T(8,128)(2,1)}, bf16[2,72,1536]{2,1,0:T(8,128)(2,1)}, u32[]{:S(2)}, u32[]{:S(2)}) collective-permute-start(bf16[2,72,1536]{2,1,0:T(8,128)(2,1)} %collective-permute-done.11.refs_4_), channel_id=1, source_target_pairs={{0,3},{1,0},{2,1},{3,2},{4,7},{5,4},{6,5},{7,6},{8,11},{9,8},{10,9... | collective-permute-start | bytes 1327112 | tf_op jit(solution)/shard_map/ppermute | solution.py:24
  32.0 22.4 %collective-permute-start.1 = (bf16[2,72,1536]{2,1,0:T(8,128)(2,1)}, bf16[2,72,1536]{2,1,0:T(8,128)(2,1)}, u32[]{:S(2)}, u32[]{:S(2)}) collective-permute-start(bf16[2,72,1536]{2,1,0:T(8,128)(2,1)} %pack.1), channel_id=1, source_target_pairs={{0,8},{1,9},{2,10},{3,11},{4,12},{5,13},{6,14},{7,15},{8,0},{9,1},... | collective-permute-start | bytes 1327112 | tf_op jit(solution)/shard_map/ppermute | solution.py:28
  37.7 32.7 %collective-permute-start.12 = (bf16[2,72,1536]{2,1,0:T(8,128)(2,1)}, bf16[2,72,1536]{2,1,0:T(8,128)(2,1)}, u32[]{:S(2)}, u32[]{:S(2)}) collective-permute-start(bf16[2,72,1536]{2,1,0:T(8,128)(2,1)} %collective-permute-done.11.refs_4_), channel_id=1, source_target_pairs={{0,1},{1,2},{2,3},{3,0},{4,5},{5,6},{6,7},{7,4},{8,9},{9,10},{10,1... | collective-permute-start | bytes 1327112 | tf_op jit(solution)/shard_map/ppermute | solution.py:24
  38.8 34.6 %collective-permute-start.9 = (bf16[2,72,1536]{2,1,0:T(8,128)(2,1)}, bf16[2,72,1536]{2,1,0:T(8,128)(2,1)}, u32[]{:S(2)}, u32[]{:S(2)}) collective-permute-start(bf16[2,72,1536]{2,1,0:T(8,128)(2,1)} %collective-permute-done.7.refs_0_), channel_id=1, source_target_pairs={{0,3},{1,0},{2,1},{3,2},{4,7},{5,4},{6,5},{7,6},{8,11},{9,8},{10,9... | collective-permute-start | bytes 1327112 | tf_op jit(solution)/shard_map/ppermute | solution.py:24
  41.7 31.7 %collective-permute-start.10 = (bf16[2,72,1536]{2,1,0:T(8,128)(2,1)}, bf16[2,72,1536]{2,1,0:T(8,128)(2,1)}, u32[]{:S(2)}, u32[]{:S(2)}) collective-permute-start(bf16[2,72,1536]{2,1,0:T(8,128)(2,1)} %collective-permute-done.8.refs_1_), channel_id=1, source_target_pairs={{0,1},{1,2},{2,3},{3,0},{4,5},{5,6},{6,7},{7,4},{8,9},{9,10},{10,1... | collective-permute-start | bytes 1327112 | tf_op jit(solution)/shard_map/ppermute | solution.py:24
  43.7 29.7 %collective-permute-start.14 = (bf16[2,72,1536]{2,1,0:T(8,128)(2,1)}, bf16[2,72,1536]{2,1,0:T(8,128)(2,1)}, u32[]{:S(2)}, u32[]{:S(2)}) collective-permute-start(bf16[2,72,1536]{2,1,0:T(8,128)(2,1)} %collective-permute-done.13.refs_6_), channel_id=1, source_target_pairs={{0,3},{1,0},{2,1},{3,2},{4,7},{5,4},{6,5},{7,6},{8,11},{9,8},{10,9... | collective-permute-start | bytes 1327112 | tf_op jit(solution)/shard_map/ppermute | solution.py:24
  48.4 14.0 %copy-start.1 = (bf16[1120,1536]{1,0:T(8,128)(2,1)}, bf16[1120,1536]{1,0:T(8,128)(2,1)S(1)}, u32[]{:S(2)}) copy-start(bf16[1120,1536]{1,0:T(8,128)(2,1)S(1)} %pad_maximum_fusion.refs_4_.refs_8_.refs_2_) | copy-start | bytes 10321924
  54.4 37.7 %collective-permute-start.2 = (bf16[2,72,1536]{2,1,0:T(8,128)(2,1)}, bf16[2,72,1536]{2,1,0:T(8,128)(2,1)S(1)}, u32[]{:S(2)}, u32[]{:S(2)}) collective-permute-start(bf16[2,72,1536]{2,1,0:T(8,128)(2,1)} %collective-permute-done.1.refs_0_), channel_id=1, source_target_pairs={{0,1},{1,2},{2,3},{3,0},{4,5},{5,6},{6,7},{7,4},{8,9},{9,10},{10,1... | collective-permute-start | bytes 1327112 | tf_op jit(solution)/shard_map/ppermute | solution.py:24
  54.7 1.0 copy-start.17
  55.7 1.0 copy-start.19
  56.7 1.5 copy-start.24
  58.2 1.0 copy-start.27
  59.2 1.0 copy-start.29
  62.4 0.9 copy-start.10
  64.1 9.4 %copy-start.25 = (bf16[560,1536]{1,0:T(8,128)(2,1)S(1)}, bf16[560,1536]{1,0:T(8,128)(2,1)}, u32[]{:S(2)}) copy-start(bf16[560,1536]{1,0:T(8,128)(2,1)} %refs_9_.1) | copy-start | bytes 5160964
  67.6 2.8 %copy-start = (f32[1536,1120]{1,0:T(8,128)}, f32[1536,1120]{1,0:T(8,128)S(1)}, u32[]{:S(2)}) copy-start(f32[1536,1120]{1,0:T(8,128)S(1)} %weight_grad.6.refs_2_) | copy-start | bytes 20643844
  70.4 21.7 %collective-permute-start.3 = (bf16[2,72,1536]{2,1,0:T(8,128)(2,1)}, bf16[2,72,1536]{2,1,0:T(8,128)(2,1)S(1)}, u32[]{:S(2)}, u32[]{:S(2)}) collective-permute-start(bf16[2,72,1536]{2,1,0:T(8,128)(2,1)} %collective-permute-done.1.refs_0_), channel_id=1, source_target_pairs={{0,3},{1,0},{2,1},{3,2},{4,7},{5,4},{6,5},{7,6},{8,11},{9,8},{10,9... | collective-permute-start | bytes 1327112 | tf_op jit(solution)/shard_map/ppermute | solution.py:24
  73.4 18.8 %collective-permute-start.4 = (bf16[2,72,1536]{2,1,0:T(8,128)(2,1)}, bf16[2,72,1536]{2,1,0:T(8,128)(2,1)S(1)}, u32[]{:S(2)}, u32[]{:S(2)}) collective-permute-start(bf16[2,72,1536]{2,1,0:T(8,128)(2,1)} %collective-permute-done.1.refs_0_), channel_id=1, source_target_pairs={{0,2},{1,3},{2,0},{3,1},{4,6},{5,7},{6,4},{7,5},{8,10},{9,11},{10,... | collective-permute-start | bytes 1327112 | tf_op jit(solution)/shard_map/ppermute | solution.py:24
  83.0 0.9 copy-start.14
  83.9 8.2 %copy-start.6 = (bf16[576,1536]{1,0:T(8,128)(2,1)}, bf16[576,1536]{1,0:T(8,128)(2,1)S(1)}, u32[]{:S(2)}) copy-start(bf16[576,1536]{1,0:T(8,128)(2,1)S(1)} %get-tuple-element.53.refs_0_) | copy-start | bytes 5308420
  83.9 8.2 %copy-start.30 = (bf16[2,72,1536]{2,1,0:T(8,128)(2,1)}, bf16[2,72,1536]{2,1,0:T(8,128)(2,1)S(1)}, u32[]{:S(2)}) copy-start(bf16[2,72,1536]{2,1,0:T(8,128)(2,1)S(1)} %get-tuple-element.50) | copy-start | bytes 1327108
  83.9 8.2 %copy-start.32 = (bf16[2,72,1536]{2,1,0:T(8,128)(2,1)}, bf16[2,72,1536]{2,1,0:T(8,128)(2,1)S(1)}, u32[]{:S(2)}) copy-start(bf16[2,72,1536]{2,1,0:T(8,128)(2,1)S(1)} %get-tuple-element.49) | copy-start | bytes 1327108
  83.9 8.2 %copy-start.33 = (bf16[2,72,1536]{2,1,0:T(8,128)(2,1)}, bf16[2,72,1536]{2,1,0:T(8,128)(2,1)S(1)}, u32[]{:S(2)}) copy-start(bf16[2,72,1536]{2,1,0:T(8,128)(2,1)S(1)} %get-tuple-element.48) | copy-start | bytes 1327108
  83.9 8.2 %copy-start.2 = (bf16[1120,1536]{1,0:T(8,128)(2,1)S(1)}, bf16[1120,1536]{1,0:T(8,128)(2,1)}, u32[]{:S(2)}) copy-start(bf16[1120,1536]{1,0:T(8,128)(2,1)} %copy-done.1) | copy-start | bytes 10321924
  95.4 1.0 copy-start.12
  96.4 4.0 %copy-start.20 = (bf16[288,560]{1,0:T(8,128)(2,1)}, bf16[288,560]{1,0:T(8,128)(2,1)S(1)}, u32[]{:S(2)}) copy-start(bf16[288,560]{1,0:T(8,128)(2,1)S(1)} %get-tuple-element.52.refs_1_) | copy-start | bytes 967684
  100.4 5.0 %collective-permute-start.21 = (bf16[4,2,96,1120]{3,2,1,0:T(8,128)(2,1)S(1)}, bf16[4,2,96,1120]{3,2,1,0:T(8,128)(2,1)S(1)}, u32[]{:S(2)}, u32[]{:S(2)}) collective-permute-start(bf16[4,2,96,1120]{3,2,1,0:T(8,128)(2,1)S(1)} %get-tuple-element.42.refs_3_), channel_id=1, source_target_pairs={{0,16},{16,0},{32,48},{48,32},{64,80},{80,64},{96,112},{112,96},{1... | collective-permute-start | bytes 5160968 | tf_op jit(solution)/shard_map/ppermute | solution.py:40
  104.5 0.8 copy-start.38
  107.2 61.9 %all-to-all-start = ((bf16[4,2,96,1120]{3,2,1,0:T(8,128)(2,1)}), bf16[4,2,96,1120]{3,2,1,0:T(8,128)(2,1)S(1)}, u32[]{:S(2)}, u32[]{:S(2)}) async-start(bf16[4,2,96,1120]{3,2,1,0:T(8,128)(2,1)} %over_cores.2.refs_3_), calls=%async_computation | async-start | bytes 3538944 | tf_op jit(solution)/shard_map/all_to_all | solution.py:236
  112.1 17.7 %collective-permute-start.18 = (bf16[2,72,1536]{2,1,0:T(8,128)(2,1)}, bf16[2,72,1536]{2,1,0:T(8,128)(2,1)S(1)}, u32[]{:S(2)}, u32[]{:S(2)}) collective-permute-start(bf16[2,72,1536]{2,1,0:T(8,128)(2,1)} %copy-done.33), channel_id=1, source_target_pairs={{0,3},{1,0},{2,1},{3,2},{4,7},{5,4},{6,5},{7,6},{8,11},{9,8},{10,9... | collective-permute-start | bytes 1327112 | tf_op jit(solution)/shard_map/ppermute | solution.py:24
  113.9 17.4 %collective-permute-start.19 = (bf16[2,72,1536]{2,1,0:T(8,128)(2,1)}, bf16[2,72,1536]{2,1,0:T(8,128)(2,1)S(1)}, u32[]{:S(2)}, u32[]{:S(2)}) collective-permute-start(bf16[2,72,1536]{2,1,0:T(8,128)(2,1)} %copy-done.32), channel_id=1, source_target_pairs={{0,1},{1,2},{2,3},{3,0},{4,5},{5,6},{6,7},{7,4},{8,9},{9,10},{10,1... | collective-permute-start | bytes 1327112 | tf_op jit(solution)/shard_map/ppermute | solution.py:24
  114.2 1.2 copy-start.11
  115.3 1.0 copy-start.23
  116.3 2.7 %copy-start.7 = (bf16[576,1536]{1,0:T(8,128)(2,1)S(1)}, bf16[576,1536]{1,0:T(8,128)(2,1)}, u32[]{:S(2)}) copy-start(bf16[576,1536]{1,0:T(8,128)(2,1)} %copy-done.6) | copy-start | bytes 5308420
  116.3 2.7 %copy-start.15 = (bf16[576,560]{1,0:T(8,128)(2,1)S(1)}, bf16[576,560]{1,0:T(8,128)(2,1)}, u32[]{:S(2)}) copy-start(bf16[576,560]{1,0:T(8,128)(2,1)} %copy-done.14) | copy-start | bytes 1935364
  119.1 3.4 %copy-start.13 = (bf16[288,1536]{1,0:T(8,128)(2,1)S(1)}, bf16[288,1536]{1,0:T(8,128)(2,1)}, u32[]{:S(2)}) copy-start(bf16[288,1536]{1,0:T(8,128)(2,1)} %copy-done.12) | copy-start | bytes 2654212
  119.1 3.4 %copy-start.21 = (bf16[288,560]{1,0:T(8,128)(2,1)S(1)}, bf16[288,560]{1,0:T(8,128)(2,1)}, u32[]{:S(2)}) copy-start(bf16[288,560]{1,0:T(8,128)(2,1)} %copy-done.20) | copy-start | bytes 967684
  122.5 3.1 %copy-start.31 = (bf16[2,72,1536]{2,1,0:T(8,128)(2,1)S(1)}, bf16[2,72,1536]{2,1,0:T(8,128)(2,1)}, u32[]{:S(2)}) copy-start(bf16[2,72,1536]{2,1,0:T(8,128)(2,1)} %copy-done.30) | copy-start | bytes 1327108
  122.5 6.7 %copy-start.39 = (bf16[2,72,1536]{2,1,0:T(8,128)(2,1)S(1)}, bf16[2,72,1536]{2,1,0:T(8,128)(2,1)}, u32[]{:S(2)}) copy-start(bf16[2,72,1536]{2,1,0:T(8,128)(2,1)} %copy-done.38) | copy-start | bytes 1327108
  122.5 7.3 %copy-start.37 = (bf16[2,72,1536]{2,1,0:T(8,128)(2,1)S(1)}, bf16[2,72,1536]{2,1,0:T(8,128)(2,1)}, u32[]{:S(2)}) copy-start(bf16[2,72,1536]{2,1,0:T(8,128)(2,1)} %copy-done.36) | copy-start | bytes 1327108
  122.5 8.7 %copy-start.35 = (bf16[2,72,1536]{2,1,0:T(8,128)(2,1)S(1)}, bf16[2,72,1536]{2,1,0:T(8,128)(2,1)}, u32[]{:S(2)}) copy-start(bf16[2,72,1536]{2,1,0:T(8,128)(2,1)} %copy-done.34) | copy-start | bytes 1327108
  125.5 33.6 %copy-start.4 = (f32[4,2,96,560]{3,2,1,0:T(8,128)}, f32[4,2,96,560]{3,2,1,0:T(8,128)S(1)}, u32[]{:S(2)}) copy-start(f32[4,2,96,560]{3,2,1,0:T(8,128)S(1)} %get-tuple-element.65.keep) | copy-start | bytes 5160964
  125.5 42.7 %collective-permute-start.26 = (bf16[4,2,96,560]{3,2,1,0:T(8,128)(2,1)S(1)}, bf16[4,2,96,560]{3,2,1,0:T(8,128)(2,1)S(1)}, u32[]{:S(2)}, u32[]{:S(2)}) collective-permute-start(bf16[4,2,96,560]{3,2,1,0:T(8,128)(2,1)S(1)} %get-tuple-element.58.refs_0_), channel_id=1, source_target_pairs={{0,16},{16,0},{32,48},{48,32},{64,80},{80,64},{96,112},{112,96},{1... | collective-permute-start | bytes 2580488 | tf_op jit(solution)/shard_map/ppermute | solution.py:40
  125.6 14.7 %collective-permute-start.20 = (bf16[2,72,1536]{2,1,0:T(8,128)(2,1)S(1)}, bf16[2,72,1536]{2,1,0:T(8,128)(2,1)S(1)}, u32[]{:S(2)}, u32[]{:S(2)}) collective-permute-start(bf16[2,72,1536]{2,1,0:T(8,128)(2,1)S(1)} %copy-done.31), channel_id=1, source_target_pairs={{0,2},{1,3},{2,0},{3,1},{4,6},{5,7},{6,4},{7,5},{8,10},{9,11},{10,... | collective-permute-start | bytes 1327112 | tf_op jit(solution)/shard_map/ppermute | solution.py:24
  129.2 20.7 %collective-permute-start.15 = (bf16[2,72,1536]{2,1,0:T(8,128)(2,1)S(1)}, bf16[2,72,1536]{2,1,0:T(8,128)(2,1)S(1)}, u32[]{:S(2)}, u32[]{:S(2)}) collective-permute-start(bf16[2,72,1536]{2,1,0:T(8,128)(2,1)S(1)} %copy-done.39), channel_id=1, source_target_pairs={{0,3},{1,0},{2,1},{3,2},{4,7},{5,4},{6,5},{7,6},{8,11},{9,8},{10,9... | collective-permute-start | bytes 1327112 | tf_op jit(solution)/shard_map/ppermute | solution.py:24
  129.8 20.2 %collective-permute-start.16 = (bf16[2,72,1536]{2,1,0:T(8,128)(2,1)S(1)}, bf16[2,72,1536]{2,1,0:T(8,128)(2,1)S(1)}, u32[]{:S(2)}, u32[]{:S(2)}) collective-permute-start(bf16[2,72,1536]{2,1,0:T(8,128)(2,1)S(1)} %copy-done.37), channel_id=1, source_target_pairs={{0,1},{1,2},{2,3},{3,0},{4,5},{5,6},{6,7},{7,4},{8,9},{9,10},{10,1... | collective-permute-start | bytes 1327112 | tf_op jit(solution)/shard_map/ppermute | solution.py:24
  131.3 27.7 %collective-permute-start.17 = (bf16[2,72,1536]{2,1,0:T(8,128)(2,1)S(1)}, bf16[2,72,1536]{2,1,0:T(8,128)(2,1)S(1)}, u32[]{:S(2)}, u32[]{:S(2)}) collective-permute-start(bf16[2,72,1536]{2,1,0:T(8,128)(2,1)S(1)} %copy-done.35), channel_id=1, source_target_pairs={{0,2},{1,3},{2,0},{3,1},{4,6},{5,7},{6,4},{7,5},{8,10},{9,11},{10,... | collective-permute-start | bytes 1327112 | tf_op jit(solution)/shard_map/ppermute | solution.py:24
  159.2 20.8 %collective-permute-start.24 = (bf16[72,1536]{1,0:T(8,128)(2,1)S(1)}, bf16[72,1536]{1,0:T(8,128)(2,1)}, u32[]{:S(2)}, u32[]{:S(2)}) collective-permute-start(bf16[72,1536]{1,0:T(8,128)(2,1)S(1)} %get-tuple-element.62), channel_id=1, source_target_pairs={{0,8},{1,9},{2,10},{3,11},{4,12},{5,13},{6,14},{7,15},{8,0},{9,1},... | collective-permute-start | bytes 663560 | tf_op jit(solution)/shard_map/ppermute | solution.py:28
  163.8 16.7 %collective-permute-start.22 = (bf16[72,1536]{1,0:T(8,128)(2,1)}, bf16[72,1536]{1,0:T(8,128)(2,1)}, u32[]{:S(2)}, u32[]{:S(2)}) collective-permute-start(bf16[72,1536]{1,0:T(8,128)(2,1)} %get-tuple-element.61), channel_id=1, source_target_pairs={{0,4},{1,5},{2,6},{3,7},{4,8},{5,9},{6,10},{7,11},{8,12},{9,13},{1... | collective-permute-start | bytes 663560 | tf_op jit(solution)/shard_map/ppermute | solution.py:28
  166.9 17.2 %collective-permute-start.23 = (bf16[72,1536]{1,0:T(8,128)(2,1)}, bf16[72,1536]{1,0:T(8,128)(2,1)}, u32[]{:S(2)}, u32[]{:S(2)}) collective-permute-start(bf16[72,1536]{1,0:T(8,128)(2,1)} %get-tuple-element.59.refs_0_), channel_id=1, source_target_pairs={{0,12},{1,13},{2,14},{3,15},{4,0},{5,1},{6,2},{7,3},{8,4},{9,5},{1... | collective-permute-start | bytes 663560 | tf_op jit(solution)/shard_map/ppermute | solution.py:28
  168.2 1.0 copy-start.8
  169.2 1.5 copy-start.5
  170.7 1.2 copy-start.9
  172.1 1.0 copy-start.3
  173.1 17.0 %all-to-all-start.1 = ((bf16[4,2,96,560]{3,2,1,0:T(8,128)(2,1)}), bf16[4,2,96,560]{3,2,1,0:T(8,128)(2,1)S(1)}, u32[]{:S(2)}, u32[]{:S(2)}) async-start(bf16[4,2,96,560]{3,2,1,0:T(8,128)(2,1)} %copy-done.3), calls=%async_computation.1 | async-start | bytes 1966080 | tf_op jit(solution)/shard_map/all_to_all | solution.py:236
  178.7 9.6 %collective-permute-start.25 = (bf16[96,1120]{1,0:T(8,128)(2,1)S(1)}, bf16[96,1120]{1,0:T(8,128)(2,1)S(1)}, u32[]{:S(2)}, u32[]{:S(2)}) collective-permute-start(bf16[96,1120]{1,0:T(8,128)(2,1)S(1)} %get-tuple-element.64), channel_id=1, source_target_pairs={{0,32},{16,48},{32,0},{48,16},{64,96},{80,112},{96,64},{112,80},{1... | collective-permute-start | bytes 645128 | tf_op jit(solution)/shard_map/ppermute | solution.py:36
  190.8 5.0 %collective-permute-start.27 = (bf16[96,560]{1,0:T(8,128)(2,1)S(1)}, bf16[96,560]{1,0:T(8,128)(2,1)S(1)}, u32[]{:S(2)}, u32[]{:S(2)}) collective-permute-start(bf16[96,560]{1,0:T(8,128)(2,1)S(1)} %get-tuple-element.67), channel_id=1, source_target_pairs={{0,32},{16,48},{32,0},{48,16},{64,96},{80,112},{96,64},{112,80},{1... | collective-permute-start | bytes 322568 | tf_op jit(solution)/shard_map/ppermute | solution.py:36
  (6 other events, 4.6 us)
where the time goes:
time: 199 us; the launch traced here: 196 us
  waiting for transfers between devices  58.6 us (29%)
  starting transfers between devices  57.8 us (29%)
  Pallas kernels  48.6 us (24%)
  local copies, waits for them, and re-layouts  24.2 us (12%)
  other arithmetic  6.07 us (3%)
    ppermute x18, waiting for transfers between devices, along_x(): lax.ppermute(value, 'tensor', [(i, i // 4 * 4 + (i + step) % 4) for i in...  31.9 us
    ppermute x18, starting transfers between devices, along_x(): lax.ppermute(value, 'tensor', [(i, i // 4 * 4 + (i + step) % 4) for i in...  25.4 us
    pallas_call x6, Pallas kernels, weight_grad(): pl.pallas_call(functools.partial(weight_body, total is not None, len(args...  24.7 us
    unnamed x80, local copies, waits for them, and re-layouts  23.4 us
    ppermute x6, starting transfers between devices, along_z(): lax.ppermute(value, 'tensor', [(i, (i + 4 * step) % 16) for i in range(16)])  20.3 us
    ppermute x6, waiting for transfers between devices, along_z(): lax.ppermute(value, 'tensor', [(i, (i + 4 * step) % 16) for i in range(16)])  19.4 us
    pallas_call x3, Pallas kernels, stage(): pl.pallas_call(functools.partial(stage_body, groups, send), out_shape=out...  15 us
    all_to_all x2, starting transfers between devices, over_y(): lax.all_to_all(sums, 'dp', 0, 0, axis_index_groups=groups, tiled=True)  9.72 us
  transfers between devices with their start and end apart: 30, of which 13 were waited for; matrix products, arithmetic and copies ran while one was open for 3% of the time, Pallas kernels for 20%

commit v1 on v0

--- a/solution.py
+++ b/solution.py
@@ -106,7 +106,7 @@
         in_specs=[VMEM] * (len(blocks) + 2),
         out_specs=[VMEM] * len(outs),
         compiler_params=pltpu.CompilerParams(vmem_limit_bytes=LIMIT),
-        cost_estimate=pl.CostEstimate(
+        cost_estimate=SHORT if groups == 1 else pl.CostEstimate(
             flops=10 * m * model * hidden_units, bytes_accessed=groups * (6 << 20), transcendentals=m * hidden_units
         ),
         name="stage",
@@ -183,7 +183,7 @@
         ),
         out_shape=out_shape,
         compiler_params=pltpu.CompilerParams(vmem_limit_bytes=LIMIT),
-        cost_estimate=SHORT if last else pl.CostEstimate(flops=2 * m * model * n, bytes_accessed=8 * model * n, transcendentals=0),
+        cost_estimate=SHORT if last or total is None else pl.CostEstimate(flops=2 * m * model * n, bytes_accessed=8 * model * n, transcendentals=0),
         name="weight_grad",
     )(place, *args)
 
@@ -292,7 +292,7 @@
     from_below, from_above = along_z(above, 1), along_z(below, -1)
     pair = over_y(pair)
     down = over_cores(*down, pair)
-    far, mine = scatter_x(*late, (BF16, F32), below)
+    far, mine = scatter_x(*late, (BF16, F32), down, from_below, from_above)
     down = over_y(down)
     from_far = along_z(far, 2)
     grad_input = mine + from_below.astype(F32) + from_above.astype(F32) + from_far.astype(F32)

time: 199 us -> 186 us (0.935)
  local copies, waits for them, and re-layouts: 24.2 us -> 12.9 us
  waiting for transfers between devices: 58.6 us -> 48.7 us
  Pallas kernels: 48.6 us -> 53.3 us
  starting transfers between devices: 57.8 us -> 62.3 us
    unnamed x80 -> x70, local copies, waits for them, and re-layouts: 23.4 us -> 12.1 us
    ppermute x6, waiting for transfers between devices: 19.4 us -> 11.5 us  [along_z(): lax.ppermute(value, 'tensor', [(i, (i + 4 * step) % 16) for i in range(16)])]
    ppermute x2, waiting for transfers between devices: 5.5 us -> 1.48 us  [other_z_lo(): return lax.ppermute(value, 'dp', [(i, i ^ 2) for i in range(16)])]
    pallas_call x2, Pallas kernels: 2.1 us -> 5.27 us  [over_cores(): pl.pallas_call(cores_body, grid=(4,), out_shape=jax.ShapeDtypeStruct(keep...]
    ppermute x2, starting transfers between devices: 2.23 us -> 5.35 us  [other_z_lo(): return lax.ppermute(value, 'dp', [(i, i ^ 2) for i in range(16)])]
    ppermute x18, starting transfers between devices: 25.4 us -> 28.2 us  [along_x(): lax.ppermute(value, 'tensor', [(i, i // 4 * 4 + (i + step) % 4) for i in...]
    pallas_call x3, Pallas kernels: 15 us -> 12.8 us  [stage(): pl.pallas_call(functools.partial(stage_body, groups, send), out_shape=out...]
  transfers between devices with their start and end apart: 30 -> 30, of which waited for: 13 -> 11; matrix products, arithmetic and copies ran while one was open for 3% -> 3% of each run, Pallas kernels for 20% -> 25%
where the time goes in v1:
time: 186 us; the launch traced here: 184 us
  starting transfers between devices  62.3 us (33%)
  Pallas kernels  53.3 us (29%)
  waiting for transfers between devices  48.7 us (26%)
  local copies, waits for them, and re-layouts  12.9 us (7%)
  other arithmetic  6.01 us (3%)
    ppermute x18, waiting for transfers between devices, along_x(): lax.ppermute(value, 'tensor', [(i, i // 4 * 4 + (i + step) % 4) for i in...  33.8 us
    ppermute x18, starting transfers between devices, along_x(): lax.ppermute(value, 'tensor', [(i, i // 4 * 4 + (i + step) % 4) for i in...  28.2 us
    pallas_call x6, Pallas kernels, weight_grad(): pl.pallas_call(functools.partial(weight_body, total is not None, len(args...  25.7 us
    ppermute x6, starting transfers between devices, along_z(): lax.ppermute(value, 'tensor', [(i, (i + 4 * step) % 16) for i in range(16)])  18.9 us
    pallas_call x3, Pallas kernels, stage(): pl.pallas_call(functools.partial(stage_body, groups, send), out_shape=out...  12.8 us
    unnamed x70, local copies, waits for them, and re-layouts  12.1 us
    ppermute x6, waiting for transfers between devices, along_z(): lax.ppermute(value, 'tensor', [(i, (i + 4 * step) % 16) for i in range(16)])  11.5 us
    all_to_all x2, starting transfers between devices, over_y(): lax.all_to_all(sums, 'dp', 0, 0, axis_index_groups=groups, tiled=True)  9.83 us
  transfers between devices with their start and end apart: 30, of which 11 were waited for; matrix products, arithmetic and copies ran while one was open for 3% of the time, Pallas kernels for 25%

profile of v1, /device:TPU:8, one launch (start us, length us, event | category | flops | bytes accessed | tf_op | source)
XLA Modules:
  0.0 184.3 jit_solution(15017348163089554415)
XLA Ops:
  0.6 1.1 pad_maximum_fusion.1.refs_0_
  1.7 1.6 collective-permute-start
  3.3 3.3 %collective-permute-start.7 = (bf16[2,72,1536]{2,1,0:T(8,128)(2,1)S(1)}, bf16[2,72,1536]{2,1,0:T(8,128)(2,1)S(1)}, u32[]{:S(2)}, u32[]{:S(2)}) collective-permute-start(bf16[2,72,1536]{2,1,0:T(8,128)(2,1)S(1)} %pad_maximum_fusion.1.refs_0_), channel_id=1, source_target_pairs={{0,4},{1,5},{2,6},{3,7},{4,8},{5,9},{6,10},{7,11},{8,12},{9,13},{1... | collective-permute-start | bytes 1327112 | tf_op jit(solution)/shard_map/ppermute | solution.py:28
  6.6 3.0 %collective-permute-start.11 = (bf16[2,72,1536]{2,1,0:T(8,128)(2,1)S(1)}, bf16[2,72,1536]{2,1,0:T(8,128)(2,1)S(1)}, u32[]{:S(2)}, u32[]{:S(2)}) collective-permute-start(bf16[2,72,1536]{2,1,0:T(8,128)(2,1)S(1)} %pad_maximum_fusion.1.refs_0_), channel_id=1, source_target_pairs={{0,12},{1,13},{2,14},{3,15},{4,0},{5,1},{6,2},{7,3},{8,4},{9,5},{1... | collective-permute-start | bytes 1327112 | tf_op jit(solution)/shard_map/ppermute | solution.py:28
  9.6 1.7 collective-permute-start.5
  11.3 3.6 %collective-permute-done.after.refs_1_ = bf16[2,72,1536]{2,1,0:T(8,128)(2,1)S(1)} collective-permute-done((bf16[2,72,1536]{2,1,0:T(8,128)(2,1)S(1)}, bf16[2,72,1536]{2,1,0:T(8,128)(2,1)S(1)}, u32[]{:S(2)}, u32[]{:S(2)}) %collective-permute-start) | collective-permute-done | bytes 442400 | tf_op jit(solution)/shard_map/ppermute | solution.py:24
  14.9 0.8 copy-done.9
  15.7 1.9 %pack.1 = bf16[2,72,1536]{2,1,0:T(8,128)(2,1)} custom-call(bf16[72,1536]{1,0:T(8,128)(2,1)} %rows.1, bf16[72,1536]{1,0:T(8,128)(2,1)} %grads.1, bf16[2,72,1536]{2,1,0:T(8,128)(2,1)} %copy-done.9), custom_call_target="tpu_custom_call" | custom-call | bytes 1048576 | tf_op jit(solution)/shard_map/pack/pallas_call | solution.py:48
  17.5 1.8 collective-permute-start.6
  19.4 3.6 %collective-permute-done.7.refs_0_ = bf16[2,72,1536]{2,1,0:T(8,128)(2,1)S(1)} collective-permute-done((bf16[2,72,1536]{2,1,0:T(8,128)(2,1)S(1)}, bf16[2,72,1536]{2,1,0:T(8,128)(2,1)S(1)}, u32[]{:S(2)}, u32[]{:S(2)}) %collective-permute-start.7) | collective-permute-done | bytes 442400 | tf_op jit(solution)/shard_map/ppermute | solution.py:28
  22.9 1.5 collective-permute-start.8
  24.4 5.7 %collective-permute-done.11.refs_4_ = bf16[2,72,1536]{2,1,0:T(8,128)(2,1)S(1)} collective-permute-done((bf16[2,72,1536]{2,1,0:T(8,128)(2,1)S(1)}, bf16[2,72,1536]{2,1,0:T(8,128)(2,1)S(1)}, u32[]{:S(2)}, u32[]{:S(2)}) %collective-permute-start.11) | collective-permute-done | bytes 442400 | tf_op jit(solution)/shard_map/ppermute | solution.py:28
  30.1 1.7 collective-permute-start.13
  31.9 5.0 %collective-permute-start.1 = (bf16[2,72,1536]{2,1,0:T(8,128)(2,1)}, bf16[2,72,1536]{2,1,0:T(8,128)(2,1)S(1)}, u32[]{:S(2)}, u32[]{:S(2)}) collective-permute-start(bf16[2,72,1536]{2,1,0:T(8,128)(2,1)} %pack.1), channel_id=1, source_target_pairs={{0,8},{1,9},{2,10},{3,11},{4,12},{5,13},{6,14},{7,15},{8,0},{9,1},... | collective-permute-start | bytes 1327112 | tf_op jit(solution)/shard_map/ppermute | solution.py:28
  37.2 3.0 %collective-permute-start.9 = (bf16[2,72,1536]{2,1,0:T(8,128)(2,1)S(1)}, bf16[2,72,1536]{2,1,0:T(8,128)(2,1)S(1)}, u32[]{:S(2)}, u32[]{:S(2)}) collective-permute-start(bf16[2,72,1536]{2,1,0:T(8,128)(2,1)S(1)} %collective-permute-done.7.refs_0_), channel_id=1, source_target_pairs={{0,3},{1,0},{2,1},{3,2},{4,7},{5,4},{6,5},{7,6},{8,11},{9,8},{10,9... | collective-permute-start | bytes 1327112 | tf_op jit(solution)/shard_map/ppermute | solution.py:24
  40.2 1.8 collective-permute-start.10
  42.0 1.2 collective-permute-done.13.refs_6_
  43.2 3.0 %collective-permute-start.14 = (bf16[2,72,1536]{2,1,0:T(8,128)(2,1)S(1)}, bf16[2,72,1536]{2,1,0:T(8,128)(2,1)S(1)}, u32[]{:S(2)}, u32[]{:S(2)}) collective-permute-start(bf16[2,72,1536]{2,1,0:T(8,128)(2,1)S(1)} %collective-permute-done.13.refs_6_), channel_id=1, source_target_pairs={{0,3},{1,0},{2,1},{3,2},{4,7},{5,4},{6,5},{7,6},{8,11},{9,8},{10,9... | collective-permute-start | bytes 1327112 | tf_op jit(solution)/shard_map/ppermute | solution.py:24
  46.2 2.3 %pad_maximum_fusion.refs_4_.refs_8_.refs_2_ = bf16[1120,1536]{1,0:T(8,128)(2,1)S(1)} fusion(bf16[560,1536]{1,0:T(8,128)(2,1)} %bitcast.8, bf16[560,1536]{1,0:T(8,128)(2,1)} %bitcast.9), kind=kLoop, calls=%fused_computation | loop fusion | flops 6881280 | bytes 6881280 | tf_op jit(solution)/shard_map/concatenate | solution.py:267
  48.8 2.2 %stage.4 = (bf16[288,1536]{1,0:T(8,128)(2,1)S(1)}, bf16[288,1536]{1,0:T(8,128)(2,1)S(1)}, bf16[288,1120]{1,0:T(8,128)(2,1)S(1)}, bf16[288,560]{1,0:T(8,128)(2,1)S(1)}) custom-call(bf16[2,72,1536]{2,1,0:T(8,128)(2,1)S(1)} %pad_maximum_fusion.1.refs_0_, bf16[2,72,1536]{2,1,0:T(8,128)(2,1)S(1)} %copy-done.10, ...), custom_call_target="tpu_custom_call" | custom-call | tf_op jit(solution)/shard_map/stage/pallas_call | solution.py:103
  51.0 0.9 copy-done.15
  51.9 3.5 %weight_grad.6.refs_2_ = f32[1536,1120]{1,0:T(8,128)S(1)} custom-call(s32[2]{0:T(128)S(1)} %pad_add_fusion.place, bf16[288,1536]{1,0:T(8,128)(2,1)S(1)} %get-tuple-element.41.refs_0_, bf16[288,1120]{1,0:T(8,128)(2,1)S(1)} %get-tuple-element.37.refs_1_), custom_call_target="tpu_custom_call" | custom-call | tf_op jit(solution)/shard_map/weight_grad/pallas_call | solution.py:179
  55.4 2.8 %copy-done.2 = f32[1536,1120]{1,0:T(8,128)} copy-done((f32[1536,1120]{1,0:T(8,128)}, f32[1536,1120]{1,0:T(8,128)S(1)}, u32[]{:S(2)}) %copy-start.2) | copy-done | bytes 6881304
  58.3 3.2 %collective-permute-start.3 = (bf16[2,72,1536]{2,1,0:T(8,128)(2,1)S(1)}, bf16[2,72,1536]{2,1,0:T(8,128)(2,1)S(1)}, u32[]{:S(2)}, u32[]{:S(2)}) collective-permute-start(bf16[2,72,1536]{2,1,0:T(8,128)(2,1)S(1)} %collective-permute-done.1.refs_0_), channel_id=1, source_target_pairs={{0,3},{1,0},{2,1},{3,2},{4,7},{5,4},{6,5},{7,6},{8,11},{9,8},{10,9... | collective-permute-start | bytes 1327112 | tf_op jit(solution)/shard_map/ppermute | solution.py:24
  62.2 8.4 %stage.5 = (bf16[576,1536]{1,0:T(8,128)(2,1)S(1)}, bf16[576,1536]{1,0:T(8,128)(2,1)S(1)}, bf16[576,1120]{1,0:T(8,128)(2,1)S(1)}, bf16[576,560]{1,0:T(8,128)(2,1)...) custom-call(bf16[2,72,1536]{2,1,0:T(8,128)(2,1)S(1)} %collective-per, ...), custom_call_target="tpu_custom_call" | custom-call | flops 4954521600 | bytes 12582912 | tf_op jit(solution)/shard_map/stage/pallas_call | solution.py:103
  70.6 0.7 copy-done.27
  71.4 0.8 copy-done.29
  72.2 8.4 %weight_grad.7.refs_2_ = f32[1536,1120]{1,0:T(8,128)S(1)} custom-call(s32[2]{0:T(128)S(1)} %pad_add_fusion.place, bf16[576,1536]{1,0:T(8,128)(2,1)S(1)} %get-tuple-element.39.refs_0_, bf16[576,1120]{1,0:T(8,128)(2,1)S(1)} %get-tuple-element.40.refs_1_, f32[1536,1120]{1,0:T(8,128)} %copy-done.2), custom_call_target="tpu_custom_call" | custom-call | flops 1981808640 | bytes 13762560 | tf_op jit(solution)/shard_map/weight_grad/pallas_call | solution.py:179
  80.7 2.2 %stage.3 = (bf16[288,1536]{1,0:T(8,128)(2,1)S(1)}, bf16[288,1536]{1,0:T(8,128)(2,1)S(1)}, bf16[288,1120]{1,0:T(8,128)(2,1)S(1)}, bf16[288,560]{1,0:T(8,128)(2,1)S(1)}) custom-call(bf16[2,72,1536]{2,1,0:T(8,128)(2,1)S(1)} %collective-permute-done.1.refs_0_, bf16[2,72,1536]{2,1,0:T(8,128)(2,1)S(1)} %collective-permute-done.2.refs_1_, ...), custom_call_target="tpu_custom_call" | custom-call | tf_op jit(solution)/shard_map/stage/pallas_call | solution.py:103
  82.9 0.9 copy-done.17
  83.8 0.7 copy-done.23
  84.6 3.9 %weight_grad.8 = (bf16[4,2,96,1120]{3,2,1,0:T(8,128)(2,1)S(1)}, f32[4,2,96,1120]{3,2,1,0:T(8,128)S(1)}) custom-call(s32[2]{0:T(128)S(1)} %pad_add_fusion.place, bf16[288,1536]{1,0:T(8,128)(2,1)S(1)} %get-tuple-element.38.refs_0_, bf16[288,1120]{1,0:T(8,128)(2,1)S(1)} %get-tuple-element.36.refs_1_.refs_0_, f32[1536,1120]{1,0:T(8,128)S(1)} %weight_grad.7.refs_2_), custom_call_target="tpu_custom_call" | custom-call | tf_op jit(solution)/shard_map/weight_grad/pallas_call | solution.py:179
  88.6 3.3 %late_partials.1 = (f32[2,72,1536]{2,1,0:T(8,128)S(1)}, bf16[2,72,1536]{2,1,0:T(8,128)(2,1)S(1)}, bf16[2,72,1536]{2,1,0:T(8,128)(2,1)}, bf16[2,72,1536]{2,1,0:T(8,128)(2,1)}) custom-call(bf16[288,1120]{1,0:T(8,128)(2,1)S(1)} %get-tuple-element.36.refs_1_.refs_0_, bf16[288,1120]{1,0:T(8,128)(2,1)S(1)} %copy-done.6, bf16[1120,1536]{1,0:T(8,128)(2,1)S(1)} %copy-done.1, ...), custom_call_target="tpu_custom_call" | custom-call | tf_op jit(solution)/shard_map/late_partials/pallas_call | solution.py:124
  92.0 0.8 copy-done.33
  92.8 1.9 %over_cores.2.refs_3_ = bf16[4,2,96,1120]{3,2,1,0:T(8,128)(2,1)} custom-call(f32[4,2,96,1120]{3,2,1,0:T(8,128)S(1)} %get-tuple-element.53.keep, bf16[4,2,96,1120]{3,2,1,0:T(8,128)(2,1)S(1)} %collective-permute-done.18.got, f32[2,72,1536]{2,1,0:T(8,128)S(1)} %get-tuple-element.43.refs_0_.own), custom_call_target="tpu_custom_call" | custom-call | tf_op jit(solution)/shard_map/over_cores/pallas_call | solution.py:222
  94.6 5.0 %all-to-all-start = ((bf16[4,2,96,1120]{3,2,1,0:T(8,128)(2,1)}), bf16[4,2,96,1120]{3,2,1,0:T(8,128)(2,1)S(1)}, u32[]{:S(2)}, u32[]{:S(2)}) async-start(bf16[4,2,96,1120]{3,2,1,0:T(8,128)(2,1)} %over_cores.2.refs_3_), calls=%async_computation | async-start | bytes 3538944 | tf_op jit(solution)/shard_map/all_to_all | solution.py:236
  99.7 1.0 copy-done.26
  100.6 2.7 %weight_grad.9.refs_2_ = f32[1536,560]{1,0:T(8,128)S(1)} custom-call(s32[2]{0:T(128)S(1)} %pad_add_fusion.place, bf16[288,1536]{1,0:T(8,128)(2,1)S(1)} %copy-done.16, bf16[288,560]{1,0:T(8,128)(2,1)S(1)} %copy-done.26), custom_call_target="tpu_custom_call" | custom-call | tf_op jit(solution)/shard_map/weight_grad/pallas_call | solution.py:179
  103.4 3.4 %weight_grad.10.refs_2_ = f32[1536,560]{1,0:T(8,128)S(1)} custom-call(s32[2]{0:T(128)S(1)} %pad_add_fusion.place, bf16[576,1536]{1,0:T(8,128)(2,1)S(1)} %copy-done.12, bf16[576,560]{1,0:T(8,128)(2,1)S(1)} %copy-done.20, f32[1536,560]{1,0:T(8,128)S(1)} %weight_grad.9.refs_2_), custom_call_target="tpu_custom_call" | custom-call | flops 990904320 | bytes 6881280 | tf_op jit(solution)/shard_map/weight_grad/pallas_call | solution.py:179
  106.9 3.8 %weight_grad.11 = (bf16[4,2,96,560]{3,2,1,0:T(8,128)(2,1)}, f32[4,2,96,560]{3,2,1,0:T(8,128)S(1)}) custom-call(s32[2]{0:T(128)S(1)} %pad_add_fusion.place, bf16[288,1536]{1,0:T(8,128)(2,1)S(1)} %copy-done.18, bf16[288,560]{1,0:T(8,128)(2,1)S(1)} %copy-done.24, f32[1536,560]{1,0:T(8,128)S(1)} %weight_grad.10.refs_2_, bf16[4,2,96,1120]{3,2,1,0:T(8,128)(2,1)} %over_cores.2.refs_3_), custom_call_target="tpu_custom_call" | custom-call | tf_op jit(solution)/shard_map/weight_grad/pallas_call | solution.py:179
  110.6 3.0 %collective-permute-start.20 = (bf16[2,72,1536]{2,1,0:T(8,128)(2,1)S(1)}, bf16[2,72,1536]{2,1,0:T(8,128)(2,1)S(1)}, u32[]{:S(2)}, u32[]{:S(2)}) collective-permute-start(bf16[2,72,1536]{2,1,0:T(8,128)(2,1)S(1)} %copy-done.32), channel_id=1, source_target_pairs={{0,3},{1,0},{2,1},{3,2},{4,7},{5,4},{6,5},{7,6},{8,11},{9,8},{10,9... | collective-permute-start | bytes 1327112 | tf_op jit(solution)/shard_map/ppermute | solution.py:24
  113.7 1.9 %collective-permute-start.22 = (bf16[2,72,1536]{2,1,0:T(8,128)(2,1)S(1)}, bf16[2,72,1536]{2,1,0:T(8,128)(2,1)S(1)}, u32[]{:S(2)}, u32[]{:S(2)}) collective-permute-start(bf16[2,72,1536]{2,1,0:T(8,128)(2,1)S(1)} %copy-done.28), channel_id=1, source_target_pairs={{0,2},{1,3},{2,0},{3,1},{4,6},{5,7},{6,4},{7,5},{8,10},{9,11},{10,... | collective-permute-start | bytes 1327112 | tf_op jit(solution)/shard_map/ppermute | solution.py:24
  115.6 1.4 collective-permute-start.15
  117.0 16.6 %collective-permute-done.20.left = bf16[2,72,1536]{2,1,0:T(8,128)(2,1)S(1)} collective-permute-done((bf16[2,72,1536]{2,1,0:T(8,128)(2,1)S(1)}, bf16[2,72,1536]{2,1,0:T(8,128)(2,1)S(1)}, u32[]{:S(2)}, u32[]{:S(2)}) %collective-permute-start.20) | collective-permute-done | bytes 442400 | tf_op jit(solution)/shard_map/ppermute | solution.py:24
  133.6 3.0 %collective-permute-done.21.right = bf16[2,72,1536]{2,1,0:T(8,128)(2,1)S(1)} collective-permute-done((bf16[2,72,1536]{2,1,0:T(8,128)(2,1)S(1)}, bf16[2,72,1536]{2,1,0:T(8,128)(2,1)S(1)}, u32[]{:S(2)}, u32[]{:S(2)}) %collective-permute-start.21) | collective-permute-done | bytes 442400 | tf_op jit(solution)/shard_map/ppermute | solution.py:24
  136.6 2.2 %collective-permute-start.17 = (bf16[2,72,1536]{2,1,0:T(8,128)(2,1)}, bf16[2,72,1536]{2,1,0:T(8,128)(2,1)}, u32[]{:S(2)}, u32[]{:S(2)}) collective-permute-start(bf16[2,72,1536]{2,1,0:T(8,128)(2,1)} %get-tuple-element.46), channel_id=1, source_target_pairs={{0,2},{1,3},{2,0},{3,1},{4,6},{5,7},{6,4},{7,5},{8,10},{9,11},{10,... | collective-permute-start | bytes 1327112 | tf_op jit(solution)/shard_map/ppermute | solution.py:24
  138.8 0.9 add_parts.2
  139.7 3.8 %collective-permute-start.23 = (bf16[72,1536]{1,0:T(8,128)(2,1)}, bf16[72,1536]{1,0:T(8,128)(2,1)S(1)}, u32[]{:S(2)}, u32[]{:S(2)}) collective-permute-start(bf16[72,1536]{1,0:T(8,128)(2,1)} %get-tuple-element.60), channel_id=1, source_target_pairs={{0,4},{1,5},{2,6},{3,7},{4,8},{5,9},{6,10},{7,11},{8,12},{9,13},{1... | collective-permute-start | bytes 663560 | tf_op jit(solution)/shard_map/ppermute | solution.py:28
  143.4 8.7 %collective-permute-done.15.left = bf16[2,72,1536]{2,1,0:T(8,128)(2,1)S(1)} collective-permute-done((bf16[2,72,1536]{2,1,0:T(8,128)(2,1)S(1)}, bf16[2,72,1536]{2,1,0:T(8,128)(2,1)S(1)}, u32[]{:S(2)}, u32[]{:S(2)}) %collective-permute-start.15) | collective-permute-done | bytes 442400 | tf_op jit(solution)/shard_map/ppermute | solution.py:24
  152.1 1.3 add_chunks.2
  153.5 0.8 copy-done.21
  154.3 3.6 %collective-permute-start.26 = (bf16[96,1120]{1,0:T(8,128)(2,1)}, bf16[96,1120]{1,0:T(8,128)(2,1)}, u32[]{:S(2)}, u32[]{:S(2)}) collective-permute-start(bf16[96,1120]{1,0:T(8,128)(2,1)} %get-tuple-element.65), channel_id=1, source_target_pairs={{0,32},{16,48},{32,0},{48,16},{64,96},{80,112},{96,64},{112,80},{1... | collective-permute-start | bytes 645128 | tf_op jit(solution)/shard_map/ppermute | solution.py:36
  157.8 1.5 copy-done.8
  159.4 3.4 %over_cores.3.refs_0_ = bf16[4,2,96,560]{3,2,1,0:T(8,128)(2,1)} custom-call(f32[4,2,96,560]{3,2,1,0:T(8,128)S(1)} %copy-done.8, bf16[4,2,96,560]{3,2,1,0:T(8,128)(2,1)} %collective-permute-done.19.got, bf16[4,2,96,1120]{3,2,1,0:T(8,128)(2,1)S(1)} %all-to-all-done.refs_0_.got), custom_call_target="tpu_custom_call" | custom-call | tf_op jit(solution)/shard_map/over_cores/pallas_call | solution.py:222
  162.8 4.8 %all-to-all-start.1 = ((bf16[4,2,96,560]{3,2,1,0:T(8,128)(2,1)}), bf16[4,2,96,560]{3,2,1,0:T(8,128)(2,1)S(1)}, u32[]{:S(2)}, u32[]{:S(2)}) async-start(bf16[4,2,96,560]{3,2,1,0:T(8,128)(2,1)} %over_cores.3.refs_0_), calls=%async_computation.1 | async-start | bytes 1966080 | tf_op jit(solution)/shard_map/all_to_all | solution.py:236
  167.6 1.4 add_parts.3
  169.0 3.8 %collective-permute-start.25 = (bf16[72,1536]{1,0:T(8,128)(2,1)S(1)}, bf16[72,1536]{1,0:T(8,128)(2,1)S(1)}, u32[]{:S(2)}, u32[]{:S(2)}) collective-permute-start(bf16[72,1536]{1,0:T(8,128)(2,1)S(1)} %get-tuple-element.63), channel_id=1, source_target_pairs={{0,8},{1,9},{2,10},{3,11},{4,12},{5,13},{6,14},{7,15},{8,0},{9,1},... | collective-permute-start | bytes 663560 | tf_op jit(solution)/shard_map/ppermute | solution.py:28
  172.9 1.0 add_multiply_fusion
  173.9 0.8 fusion
  174.7 2.0 %all-to-all-done.1.got = bf16[4,2,96,560]{3,2,1,0:T(8,128)(2,1)S(1)} async-done(((bf16[4,2,96,560]{3,2,1,0:T(8,128)(2,1)}), bf16[4,2,96,560]{3,2,1,0:T(8,128)(2,1)S(1)}, u32[]{:S(2)}, u32[]{:S(2)}) %all-to-all-start.1) | async-done | bytes 860192 | tf_op jit(solution)/shard_map/all_to_all | solution.py:236
  177.3 1.8 collective-permute-start.27
  179.1 2.2 %collective-permute-done.25 = bf16[72,1536]{1,0:T(8,128)(2,1)S(1)} collective-permute-done((bf16[72,1536]{1,0:T(8,128)(2,1)S(1)}, bf16[72,1536]{1,0:T(8,128)(2,1)S(1)}, u32[]{:S(2)}, u32[]{:S(2)}) %collective-permute-start.25) | collective-permute-done | bytes 221216 | tf_op jit(solution)/shard_map/ppermute | solution.py:28
  181.3 0.8 add_convert_fusion
  182.1 1.5 collective-permute-done.27
  (90 shorter events, 2.9 us)
Async XLA Ops:
  1.7 13.2 %collective-permute-start = (bf16[2,72,1536]{2,1,0:T(8,128)(2,1)S(1)}, bf16[2,72,1536]{2,1,0:T(8,128)(2,1)S(1)}, u32[]{:S(2)}, u32[]{:S(2)}) collective-permute-start(bf16[2,72,1536]{2,1,0:T(8,128)(2,1)S(1)} %pad_maximum_fusion.1.refs_0_), channel_id=1, source_target_pairs={{0,1},{1,2},{2,3},{3,0},{4,5},{5,6},{6,7},{7,4},{8,9},{9,10},{10,1... | collective-permute-start | bytes 1327112 | tf_op jit(solution)/shard_map/ppermute | solution.py:24
  3.3 19.6 %collective-permute-start.7 = (bf16[2,72,1536]{2,1,0:T(8,128)(2,1)S(1)}, bf16[2,72,1536]{2,1,0:T(8,128)(2,1)S(1)}, u32[]{:S(2)}, u32[]{:S(2)}) collective-permute-start(bf16[2,72,1536]{2,1,0:T(8,128)(2,1)S(1)} %pad_maximum_fusion.1.refs_0_), channel_id=1, source_target_pairs={{0,4},{1,5},{2,6},{3,7},{4,8},{5,9},{6,10},{7,11},{8,12},{9,13},{1... | collective-permute-start | bytes 1327112 | tf_op jit(solution)/shard_map/ppermute | solution.py:28
  6.6 23.6 %collective-permute-start.11 = (bf16[2,72,1536]{2,1,0:T(8,128)(2,1)S(1)}, bf16[2,72,1536]{2,1,0:T(8,128)(2,1)S(1)}, u32[]{:S(2)}, u32[]{:S(2)}) collective-permute-start(bf16[2,72,1536]{2,1,0:T(8,128)(2,1)S(1)} %pad_maximum_fusion.1.refs_0_), channel_id=1, source_target_pairs={{0,12},{1,13},{2,14},{3,15},{4,0},{5,1},{6,2},{7,3},{8,4},{9,5},{1... | collective-permute-start | bytes 1327112 | tf_op jit(solution)/shard_map/ppermute | solution.py:28
  9.6 27.3 %collective-permute-start.5 = (bf16[2,72,1536]{2,1,0:T(8,128)(2,1)S(1)}, bf16[2,72,1536]{2,1,0:T(8,128)(2,1)S(1)}, u32[]{:S(2)}, u32[]{:S(2)}) collective-permute-start(bf16[2,72,1536]{2,1,0:T(8,128)(2,1)S(1)} %pad_maximum_fusion.1.refs_0_), channel_id=1, source_target_pairs={{0,3},{1,0},{2,1},{3,2},{4,7},{5,4},{6,5},{7,6},{8,11},{9,8},{10,9... | collective-permute-start | bytes 1327112 | tf_op jit(solution)/shard_map/ppermute | solution.py:24
  14.9 0.8 copy-start.9
  17.5 19.7 %collective-permute-start.6 = (bf16[2,72,1536]{2,1,0:T(8,128)(2,1)}, bf16[2,72,1536]{2,1,0:T(8,128)(2,1)S(1)}, u32[]{:S(2)}, u32[]{:S(2)}) collective-permute-start(bf16[2,72,1536]{2,1,0:T(8,128)(2,1)} %pack.1), channel_id=1, source_target_pairs={{0,2},{1,3},{2,0},{3,1},{4,6},{5,7},{6,4},{7,5},{8,10},{9,11},{10,... | collective-permute-start | bytes 1327112 | tf_op jit(solution)/shard_map/ppermute | solution.py:24
  22.9 17.3 %collective-permute-start.8 = (bf16[2,72,1536]{2,1,0:T(8,128)(2,1)S(1)}, bf16[2,72,1536]{2,1,0:T(8,128)(2,1)S(1)}, u32[]{:S(2)}, u32[]{:S(2)}) collective-permute-start(bf16[2,72,1536]{2,1,0:T(8,128)(2,1)S(1)} %collective-permute-done.7.refs_0_), channel_id=1, source_target_pairs={{0,1},{1,2},{2,3},{3,0},{4,5},{5,6},{6,7},{7,4},{8,9},{9,10},{10,1... | collective-permute-start | bytes 1327112 | tf_op jit(solution)/shard_map/ppermute | solution.py:24
  30.1 13.1 %collective-permute-start.13 = (bf16[2,72,1536]{2,1,0:T(8,128)(2,1)S(1)}, bf16[2,72,1536]{2,1,0:T(8,128)(2,1)S(1)}, u32[]{:S(2)}, u32[]{:S(2)}) collective-permute-start(bf16[2,72,1536]{2,1,0:T(8,128)(2,1)S(1)} %collective-permute-done.11.refs_4_), channel_id=1, source_target_pairs={{0,3},{1,0},{2,1},{3,2},{4,7},{5,4},{6,5},{7,6},{8,11},{9,8},{10,9... | collective-permute-start | bytes 1327112 | tf_op jit(solution)/shard_map/ppermute | solution.py:24
  31.9 26.3 %collective-permute-start.1 = (bf16[2,72,1536]{2,1,0:T(8,128)(2,1)}, bf16[2,72,1536]{2,1,0:T(8,128)(2,1)S(1)}, u32[]{:S(2)}, u32[]{:S(2)}) collective-permute-start(bf16[2,72,1536]{2,1,0:T(8,128)(2,1)} %pack.1), channel_id=1, source_target_pairs={{0,8},{1,9},{2,10},{3,11},{4,12},{5,13},{6,14},{7,15},{8,0},{9,1},... | collective-permute-start | bytes 1327112 | tf_op jit(solution)/shard_map/ppermute | solution.py:28
  36.9 21.3 %collective-permute-start.12 = (bf16[2,72,1536]{2,1,0:T(8,128)(2,1)S(1)}, bf16[2,72,1536]{2,1,0:T(8,128)(2,1)S(1)}, u32[]{:S(2)}, u32[]{:S(2)}) collective-permute-start(bf16[2,72,1536]{2,1,0:T(8,128)(2,1)S(1)} %collective-permute-done.11.refs_4_), channel_id=1, source_target_pairs={{0,1},{1,2},{2,3},{3,0},{4,5},{5,6},{6,7},{7,4},{8,9},{9,10},{10,1... | collective-permute-start | bytes 1327112 | tf_op jit(solution)/shard_map/ppermute | solution.py:24
  37.2 24.3 %collective-permute-start.9 = (bf16[2,72,1536]{2,1,0:T(8,128)(2,1)S(1)}, bf16[2,72,1536]{2,1,0:T(8,128)(2,1)S(1)}, u32[]{:S(2)}, u32[]{:S(2)}) collective-permute-start(bf16[2,72,1536]{2,1,0:T(8,128)(2,1)S(1)} %collective-permute-done.7.refs_0_), channel_id=1, source_target_pairs={{0,3},{1,0},{2,1},{3,2},{4,7},{5,4},{6,5},{7,6},{8,11},{9,8},{10,9... | collective-permute-start | bytes 1327112 | tf_op jit(solution)/shard_map/ppermute | solution.py:24
  40.2 21.3 %collective-permute-start.10 = (bf16[2,72,1536]{2,1,0:T(8,128)(2,1)S(1)}, bf16[2,72,1536]{2,1,0:T(8,128)(2,1)S(1)}, u32[]{:S(2)}, u32[]{:S(2)}) collective-permute-start(bf16[2,72,1536]{2,1,0:T(8,128)(2,1)S(1)} %collective-permute-done.8.refs_1_), channel_id=1, source_target_pairs={{0,1},{1,2},{2,3},{3,0},{4,5},{5,6},{6,7},{7,4},{8,9},{9,10},{10,1... | collective-permute-start | bytes 1327112 | tf_op jit(solution)/shard_map/ppermute | solution.py:24
  43.2 19.0 %collective-permute-start.14 = (bf16[2,72,1536]{2,1,0:T(8,128)(2,1)S(1)}, bf16[2,72,1536]{2,1,0:T(8,128)(2,1)S(1)}, u32[]{:S(2)}, u32[]{:S(2)}) collective-permute-start(bf16[2,72,1536]{2,1,0:T(8,128)(2,1)S(1)} %collective-permute-done.13.refs_6_), channel_id=1, source_target_pairs={{0,3},{1,0},{2,1},{3,2},{4,7},{5,4},{6,5},{7,6},{8,11},{9,8},{10,9... | collective-permute-start | bytes 1327112 | tf_op jit(solution)/shard_map/ppermute | solution.py:24
  46.2 2.5 %copy-start.3 = (bf16[560,1536]{1,0:T(8,128)(2,1)S(1)}, bf16[560,1536]{1,0:T(8,128)(2,1)}, u32[]{:S(2)}) copy-start(bf16[560,1536]{1,0:T(8,128)(2,1)} %refs_9_.1) | copy-start | bytes 5160964
  46.2 2.6 %copy-start.10 = (bf16[2,72,1536]{2,1,0:T(8,128)(2,1)S(1)}, bf16[2,72,1536]{2,1,0:T(8,128)(2,1)}, u32[]{:S(2)}) copy-start(bf16[2,72,1536]{2,1,0:T(8,128)(2,1)} %copy-done.9) | copy-start | bytes 1327108
  48.7 2.2 %copy-start = (bf16[1120,1536]{1,0:T(8,128)(2,1)}, bf16[1120,1536]{1,0:T(8,128)(2,1)S(1)}, u32[]{:S(2)}) copy-start(bf16[1120,1536]{1,0:T(8,128)(2,1)S(1)} %pad_maximum_fusion.refs_4_.refs_8_.refs_2_) | copy-start | bytes 10321924
  50.9 0.9 copy-start.15
  51.9 3.5 %copy-start.5 = (bf16[288,1120]{1,0:T(8,128)(2,1)}, bf16[288,1120]{1,0:T(8,128)(2,1)S(1)}, u32[]{:S(2)}) copy-start(bf16[288,1120]{1,0:T(8,128)(2,1)S(1)} %get-tuple-element.37.refs_1_) | copy-start | bytes 1935364
  51.9 3.6 %copy-start.25 = (bf16[288,560]{1,0:T(8,128)(2,1)}, bf16[288,560]{1,0:T(8,128)(2,1)S(1)}, u32[]{:S(2)}) copy-start(bf16[288,560]{1,0:T(8,128)(2,1)S(1)} %get-tuple-element.52.refs_1_) | copy-start | bytes 967684
  55.4 2.8 %copy-start.2 = (f32[1536,1120]{1,0:T(8,128)}, f32[1536,1120]{1,0:T(8,128)S(1)}, u32[]{:S(2)}) copy-start(f32[1536,1120]{1,0:T(8,128)S(1)} %weight_grad.6.refs_2_) | copy-start | bytes 20643844
  58.3 22.4 %collective-permute-start.2 = (bf16[2,72,1536]{2,1,0:T(8,128)(2,1)S(1)}, bf16[2,72,1536]{2,1,0:T(8,128)(2,1)S(1)}, u32[]{:S(2)}, u32[]{:S(2)}) collective-permute-start(bf16[2,72,1536]{2,1,0:T(8,128)(2,1)S(1)} %collective-permute-done.1.refs_0_), channel_id=1, source_target_pairs={{0,1},{1,2},{2,3},{3,0},{4,5},{5,6},{6,7},{7,4},{8,9},{9,10},{10,1... | collective-permute-start | bytes 1327112 | tf_op jit(solution)/shard_map/ppermute | solution.py:24
  58.3 22.4 %collective-permute-start.3 = (bf16[2,72,1536]{2,1,0:T(8,128)(2,1)S(1)}, bf16[2,72,1536]{2,1,0:T(8,128)(2,1)S(1)}, u32[]{:S(2)}, u32[]{:S(2)}) collective-permute-start(bf16[2,72,1536]{2,1,0:T(8,128)(2,1)S(1)} %collective-permute-done.1.refs_0_), channel_id=1, source_target_pairs={{0,3},{1,0},{2,1},{3,2},{4,7},{5,4},{6,5},{7,6},{8,11},{9,8},{10,9... | collective-permute-start | bytes 1327112 | tf_op jit(solution)/shard_map/ppermute | solution.py:24
  61.5 19.1 %collective-permute-start.4 = (bf16[2,72,1536]{2,1,0:T(8,128)(2,1)S(1)}, bf16[2,72,1536]{2,1,0:T(8,128)(2,1)S(1)}, u32[]{:S(2)}, u32[]{:S(2)}) collective-permute-start(bf16[2,72,1536]{2,1,0:T(8,128)(2,1)S(1)} %collective-permute-done.1.refs_0_), channel_id=1, source_target_pairs={{0,2},{1,3},{2,0},{3,1},{4,6},{5,7},{6,4},{7,5},{8,10},{9,11},{10,... | collective-permute-start | bytes 1327112 | tf_op jit(solution)/shard_map/ppermute | solution.py:24
  70.6 0.8 copy-start.27
  71.4 0.8 copy-start.29
  72.2 8.4 %copy-start.11 = (bf16[576,1536]{1,0:T(8,128)(2,1)}, bf16[576,1536]{1,0:T(8,128)(2,1)S(1)}, u32[]{:S(2)}) copy-start(bf16[576,1536]{1,0:T(8,128)(2,1)S(1)} %get-tuple-element.49.refs_0_) | copy-start | bytes 5308420
  72.2 8.4 %copy-start.13 = (f32[2,72,1536]{2,1,0:T(8,128)}, f32[2,72,1536]{2,1,0:T(8,128)S(1)}, u32[]{:S(2)}) copy-start(f32[2,72,1536]{2,1,0:T(8,128)S(1)} %get-tuple-element.56.own) | copy-start | bytes 2654212
  72.2 8.5 %copy-start.19 = (bf16[576,560]{1,0:T(8,128)(2,1)}, bf16[576,560]{1,0:T(8,128)(2,1)S(1)}, u32[]{:S(2)}) copy-start(bf16[576,560]{1,0:T(8,128)(2,1)S(1)} %get-tuple-element.50.refs_1_) | copy-start | bytes 1935364
  72.2 8.5 %copy-start.31 = (bf16[2,72,1536]{2,1,0:T(8,128)(2,1)}, bf16[2,72,1536]{2,1,0:T(8,128)(2,1)S(1)}, u32[]{:S(2)}) copy-start(bf16[2,72,1536]{2,1,0:T(8,128)(2,1)S(1)} %get-tuple-element.57) | copy-start | bytes 1327108
  72.2 8.5 %copy-start.1 = (bf16[1120,1536]{1,0:T(8,128)(2,1)S(1)}, bf16[1120,1536]{1,0:T(8,128)(2,1)}, u32[]{:S(2)}) copy-start(bf16[1120,1536]{1,0:T(8,128)(2,1)} %copy-done) | copy-start | bytes 10321924
  72.2 8.5 %copy-start.4 = (bf16[560,1536]{1,0:T(8,128)(2,1)S(1)}, bf16[560,1536]{1,0:T(8,128)(2,1)}, u32[]{:S(2)}) copy-start(bf16[560,1536]{1,0:T(8,128)(2,1)} %refs_9_.1) | copy-start | bytes 5160964
  82.9 1.0 copy-start.17
  84.6 4.1 %copy-start.6 = (bf16[288,1120]{1,0:T(8,128)(2,1)S(1)}, bf16[288,1120]{1,0:T(8,128)(2,1)}, u32[]{:S(2)}) copy-start(bf16[288,1120]{1,0:T(8,128)(2,1)} %copy-done.5) | copy-start | bytes 1935364
  88.5 4.2 %collective-permute-start.18 = (bf16[4,2,96,1120]{3,2,1,0:T(8,128)(2,1)S(1)}, bf16[4,2,96,1120]{3,2,1,0:T(8,128)(2,1)S(1)}, u32[]{:S(2)}, u32[]{:S(2)}) collective-permute-start(bf16[4,2,96,1120]{3,2,1,0:T(8,128)(2,1)S(1)} %get-tuple-element.42.refs_3_), channel_id=1, source_target_pairs={{0,16},{16,0},{32,48},{48,32},{64,80},{80,64},{96,112},{112,96},{1... | collective-permute-start | bytes 5160968 | tf_op jit(solution)/shard_map/ppermute | solution.py:40
  92.0 0.8 copy-start.33
  94.6 5.0 %copy-start.16 = (bf16[288,1536]{1,0:T(8,128)(2,1)S(1)}, bf16[288,1536]{1,0:T(8,128)(2,1)}, u32[]{:S(2)}) copy-start(bf16[288,1536]{1,0:T(8,128)(2,1)} %copy-done.15) | copy-start | bytes 2654212
  94.6 57.5 %all-to-all-start = ((bf16[4,2,96,1120]{3,2,1,0:T(8,128)(2,1)}), bf16[4,2,96,1120]{3,2,1,0:T(8,128)(2,1)S(1)}, u32[]{:S(2)}, u32[]{:S(2)}) async-start(bf16[4,2,96,1120]{3,2,1,0:T(8,128)(2,1)} %over_cores.2.refs_3_), calls=%async_computation | async-start | bytes 3538944 | tf_op jit(solution)/shard_map/all_to_all | solution.py:236
  99.7 1.0 copy-start.26
  100.6 2.7 %copy-start.12 = (bf16[576,1536]{1,0:T(8,128)(2,1)S(1)}, bf16[576,1536]{1,0:T(8,128)(2,1)}, u32[]{:S(2)}) copy-start(bf16[576,1536]{1,0:T(8,128)(2,1)} %copy-done.11) | copy-start | bytes 5308420
  100.6 2.7 %copy-start.20 = (bf16[576,560]{1,0:T(8,128)(2,1)S(1)}, bf16[576,560]{1,0:T(8,128)(2,1)}, u32[]{:S(2)}) copy-start(bf16[576,560]{1,0:T(8,128)(2,1)} %copy-done.19) | copy-start | bytes 1935364
  103.4 3.4 %copy-start.18 = (bf16[288,1536]{1,0:T(8,128)(2,1)S(1)}, bf16[288,1536]{1,0:T(8,128)(2,1)}, u32[]{:S(2)}) copy-start(bf16[288,1536]{1,0:T(8,128)(2,1)} %copy-done.17) | copy-start | bytes 2654212
  103.4 3.4 %copy-start.24 = (bf16[288,560]{1,0:T(8,128)(2,1)S(1)}, bf16[288,560]{1,0:T(8,128)(2,1)}, u32[]{:S(2)}) copy-start(bf16[288,560]{1,0:T(8,128)(2,1)} %copy-done.23) | copy-start | bytes 967684
  106.8 3.8 %copy-start.32 = (bf16[2,72,1536]{2,1,0:T(8,128)(2,1)S(1)}, bf16[2,72,1536]{2,1,0:T(8,128)(2,1)}, u32[]{:S(2)}) copy-start(bf16[2,72,1536]{2,1,0:T(8,128)(2,1)} %copy-done.31) | copy-start | bytes 1327108
  106.8 6.8 %copy-start.30 = (bf16[2,72,1536]{2,1,0:T(8,128)(2,1)S(1)}, bf16[2,72,1536]{2,1,0:T(8,128)(2,1)}, u32[]{:S(2)}) copy-start(bf16[2,72,1536]{2,1,0:T(8,128)(2,1)} %copy-done.29) | copy-start | bytes 1327108
  106.8 6.8 %copy-start.28 = (bf16[2,72,1536]{2,1,0:T(8,128)(2,1)S(1)}, bf16[2,72,1536]{2,1,0:T(8,128)(2,1)}, u32[]{:S(2)}) copy-start(bf16[2,72,1536]{2,1,0:T(8,128)(2,1)} %copy-done.27) | copy-start | bytes 1327108
  106.8 8.8 %copy-start.34 = (bf16[2,72,1536]{2,1,0:T(8,128)(2,1)S(1)}, bf16[2,72,1536]{2,1,0:T(8,128)(2,1)}, u32[]{:S(2)}) copy-start(bf16[2,72,1536]{2,1,0:T(8,128)(2,1)} %copy-done.33) | copy-start | bytes 1327108
  106.8 31.9 %copy-start.14 = (f32[2,72,1536]{2,1,0:T(8,128)S(1)}, f32[2,72,1536]{2,1,0:T(8,128)}, u32[]{:S(2)}) copy-start(f32[2,72,1536]{2,1,0:T(8,128)} %copy-done.13) | copy-start | bytes 2654212
  110.6 41.5 %copy-start.7 = (f32[4,2,96,560]{3,2,1,0:T(8,128)}, f32[4,2,96,560]{3,2,1,0:T(8,128)S(1)}, u32[]{:S(2)}) copy-start(f32[4,2,96,560]{3,2,1,0:T(8,128)S(1)} %get-tuple-element.54.keep) | copy-start | bytes 5160964
  110.6 43.6 %collective-permute-start.19 = (bf16[4,2,96,560]{3,2,1,0:T(8,128)(2,1)}, bf16[4,2,96,560]{3,2,1,0:T(8,128)(2,1)}, u32[]{:S(2)}, u32[]{:S(2)}) collective-permute-start(bf16[4,2,96,560]{3,2,1,0:T(8,128)(2,1)} %get-tuple-element.55.refs_0_), channel_id=1, source_target_pairs={{0,16},{16,0},{32,48},{48,32},{64,80},{80,64},{96,112},{112,96},{1... | collective-permute-start | bytes 2580488 | tf_op jit(solution)/shard_map/ppermute | solution.py:40
  110.6 23.0 %collective-permute-start.20 = (bf16[2,72,1536]{2,1,0:T(8,128)(2,1)S(1)}, bf16[2,72,1536]{2,1,0:T(8,128)(2,1)S(1)}, u32[]{:S(2)}, u32[]{:S(2)}) collective-permute-start(bf16[2,72,1536]{2,1,0:T(8,128)(2,1)S(1)} %copy-done.32), channel_id=1, source_target_pairs={{0,3},{1,0},{2,1},{3,2},{4,7},{5,4},{6,5},{7,6},{8,11},{9,8},{10,9... | collective-permute-start | bytes 1327112 | tf_op jit(solution)/shard_map/ppermute | solution.py:24
  113.7 22.9 %collective-permute-start.21 = (bf16[2,72,1536]{2,1,0:T(8,128)(2,1)S(1)}, bf16[2,72,1536]{2,1,0:T(8,128)(2,1)S(1)}, u32[]{:S(2)}, u32[]{:S(2)}) collective-permute-start(bf16[2,72,1536]{2,1,0:T(8,128)(2,1)S(1)} %copy-done.30), channel_id=1, source_target_pairs={{0,1},{1,2},{2,3},{3,0},{4,5},{5,6},{6,7},{7,4},{8,9},{9,10},{10,1... | collective-permute-start | bytes 1327112 | tf_op jit(solution)/shard_map/ppermute | solution.py:24
  113.7 25.1 %collective-permute-start.22 = (bf16[2,72,1536]{2,1,0:T(8,128)(2,1)S(1)}, bf16[2,72,1536]{2,1,0:T(8,128)(2,1)S(1)}, u32[]{:S(2)}, u32[]{:S(2)}) collective-permute-start(bf16[2,72,1536]{2,1,0:T(8,128)(2,1)S(1)} %copy-done.28), channel_id=1, source_target_pairs={{0,2},{1,3},{2,0},{3,1},{4,6},{5,7},{6,4},{7,5},{8,10},{9,11},{10,... | collective-permute-start | bytes 1327112 | tf_op jit(solution)/shard_map/ppermute | solution.py:24
  115.6 36.5 %collective-permute-start.15 = (bf16[2,72,1536]{2,1,0:T(8,128)(2,1)S(1)}, bf16[2,72,1536]{2,1,0:T(8,128)(2,1)S(1)}, u32[]{:S(2)}, u32[]{:S(2)}) collective-permute-start(bf16[2,72,1536]{2,1,0:T(8,128)(2,1)S(1)} %copy-done.34), channel_id=1, source_target_pairs={{0,3},{1,0},{2,1},{3,2},{4,7},{5,4},{6,5},{7,6},{8,11},{9,8},{10,9... | collective-permute-start | bytes 1327112 | tf_op jit(solution)/shard_map/ppermute | solution.py:24
  133.6 34.0 %collective-permute-start.16 = (bf16[2,72,1536]{2,1,0:T(8,128)(2,1)}, bf16[2,72,1536]{2,1,0:T(8,128)(2,1)}, u32[]{:S(2)}, u32[]{:S(2)}) collective-permute-start(bf16[2,72,1536]{2,1,0:T(8,128)(2,1)} %get-tuple-element.45), channel_id=1, source_target_pairs={{0,1},{1,2},{2,3},{3,0},{4,5},{5,6},{6,7},{7,4},{8,9},{9,10},{10,1... | collective-permute-start | bytes 1327112 | tf_op jit(solution)/shard_map/ppermute | solution.py:24
  136.6 31.0 %collective-permute-start.17 = (bf16[2,72,1536]{2,1,0:T(8,128)(2,1)}, bf16[2,72,1536]{2,1,0:T(8,128)(2,1)}, u32[]{:S(2)}, u32[]{:S(2)}) collective-permute-start(bf16[2,72,1536]{2,1,0:T(8,128)(2,1)} %get-tuple-element.46), channel_id=1, source_target_pairs={{0,2},{1,3},{2,0},{3,1},{4,6},{5,7},{6,4},{7,5},{8,10},{9,11},{10,... | collective-permute-start | bytes 1327112 | tf_op jit(solution)/shard_map/ppermute | solution.py:24
  139.7 27.9 %collective-permute-start.23 = (bf16[72,1536]{1,0:T(8,128)(2,1)}, bf16[72,1536]{1,0:T(8,128)(2,1)S(1)}, u32[]{:S(2)}, u32[]{:S(2)}) collective-permute-start(bf16[72,1536]{1,0:T(8,128)(2,1)} %get-tuple-element.60), channel_id=1, source_target_pairs={{0,4},{1,5},{2,6},{3,7},{4,8},{5,9},{6,10},{7,11},{8,12},{9,13},{1... | collective-permute-start | bytes 663560 | tf_op jit(solution)/shard_map/ppermute | solution.py:28
  152.1 15.5 %collective-permute-start.24 = (bf16[72,1536]{1,0:T(8,128)(2,1)}, bf16[72,1536]{1,0:T(8,128)(2,1)S(1)}, u32[]{:S(2)}, u32[]{:S(2)}) collective-permute-start(bf16[72,1536]{1,0:T(8,128)(2,1)} %get-tuple-element.61), channel_id=1, source_target_pairs={{0,12},{1,13},{2,14},{3,15},{4,0},{5,1},{6,2},{7,3},{8,4},{9,5},{1... | collective-permute-start | bytes 663560 | tf_op jit(solution)/shard_map/ppermute | solution.py:28
  153.5 0.8 copy-start.21
  154.3 18.6 %collective-permute-start.26 = (bf16[96,1120]{1,0:T(8,128)(2,1)}, bf16[96,1120]{1,0:T(8,128)(2,1)}, u32[]{:S(2)}, u32[]{:S(2)}) collective-permute-start(bf16[96,1120]{1,0:T(8,128)(2,1)} %get-tuple-element.65), channel_id=1, source_target_pairs={{0,32},{16,48},{32,0},{48,16},{64,96},{80,112},{96,64},{112,80},{1... | collective-permute-start | bytes 645128 | tf_op jit(solution)/shard_map/ppermute | solution.py:36
  157.8 1.5 copy-start.8
  162.8 13.9 %all-to-all-start.1 = ((bf16[4,2,96,560]{3,2,1,0:T(8,128)(2,1)}), bf16[4,2,96,560]{3,2,1,0:T(8,128)(2,1)S(1)}, u32[]{:S(2)}, u32[]{:S(2)}) async-start(bf16[4,2,96,560]{3,2,1,0:T(8,128)(2,1)} %over_cores.3.refs_0_), calls=%async_computation.1 | async-start | bytes 1966080 | tf_op jit(solution)/shard_map/all_to_all | solution.py:236
  167.6 5.3 %copy-start.22 = (f32[96,1120]{1,0:T(8,128)S(1)}, f32[96,1120]{1,0:T(8,128)}, u32[]{:S(2)}) copy-start(f32[96,1120]{1,0:T(8,128)} %copy-done.21) | copy-start | bytes 1290244
  169.0 12.3 %collective-permute-start.25 = (bf16[72,1536]{1,0:T(8,128)(2,1)S(1)}, bf16[72,1536]{1,0:T(8,128)(2,1)S(1)}, u32[]{:S(2)}, u32[]{:S(2)}) collective-permute-start(bf16[72,1536]{1,0:T(8,128)(2,1)S(1)} %get-tuple-element.63), channel_id=1, source_target_pairs={{0,8},{1,9},{2,10},{3,11},{4,12},{5,13},{6,14},{7,15},{8,0},{9,1},... | collective-permute-start | bytes 663560 | tf_op jit(solution)/shard_map/ppermute | solution.py:28
  177.3 6.2 %collective-permute-start.27 = (bf16[96,560]{1,0:T(8,128)(2,1)S(1)}, bf16[96,560]{1,0:T(8,128)(2,1)S(1)}, u32[]{:S(2)}, u32[]{:S(2)}) collective-permute-start(bf16[96,560]{1,0:T(8,128)(2,1)S(1)} %get-tuple-element.67), channel_id=1, source_target_pairs={{0,32},{16,48},{32,0},{48,16},{64,96},{80,112},{96,64},{112,80},{1... | collective-permute-start | bytes 322568 | tf_op jit(solution)/shard_map/ppermute | solution.py:36
  (1 other events, 0.7 us)

commit v2 on v1

--- a/solution.py
+++ b/solution.py
@@ -183,7 +183,7 @@
         ),
         out_shape=out_shape,
         compiler_params=pltpu.CompilerParams(vmem_limit_bytes=LIMIT),
-        cost_estimate=SHORT if last or total is None else pl.CostEstimate(flops=2 * m * model * n, bytes_accessed=8 * model * n, transcendentals=0),
+        cost_estimate=SHORT,
         name="weight_grad",
     )(place, *args)
 
@@ -287,8 +287,8 @@
     pair = weight_grad(place, away[0], away[2], pair[0], True)
     late = late_partials([away[2], home[2]], weight, pair[0])
     pair = over_cores(*pair, late[0])
-    down = weight_grad(place, away[1], away[3], down[0], True, pair)
-    below, above = scatter_x(*near[4:], (BF16, BF16), down[0])
+    below, above = scatter_x(*near[4:], (BF16, BF16), pair)
+    down = weight_grad(place, away[1], away[3], down[0], True, below)
     from_below, from_above = along_z(above, 1), along_z(below, -1)
     pair = over_y(pair)
     down = over_cores(*down, pair)

time: 186 us -> 169 us (0.909)
  waiting for transfers between devices: 48.7 us -> 33.1 us
  Pallas kernels: 53.3 us -> 55.4 us
    ppermute x18, waiting for transfers between devices: 33.8 us -> 15.3 us  [along_x(): lax.ppermute(value, 'tensor', [(i, i // 4 * 4 + (i + step) % 4) for i in...]
    all_to_all x2, waiting for transfers between devices: 1.98 us -> 5.28 us  [over_y(): lax.all_to_all(sums, 'dp', 0, 0, axis_index_groups=groups, tiled=True)]
    ppermute x2, starting transfers between devices: 5.35 us -> 2.11 us  [other_z_lo(): return lax.ppermute(value, 'dp', [(i, i ^ 2) for i in range(16)])]
    ppermute x6, starting transfers between devices: 18.9 us -> 21.3 us  [along_z(): lax.ppermute(value, 'tensor', [(i, (i + 4 * step) % 16) for i in range(16)])]
    unnamed x70 -> x58, local copies, waits for them, and re-layouts: 12.1 us -> 11.9 us
  transfers between devices with their start and end apart: 30 -> 30, of which waited for: 11 -> 10; matrix products, arithmetic and copies ran while one was open for 3% -> 3% of each run, Pallas kernels for 25% -> 29%
where the time goes in v2:
time: 169 us
  starting transfers between devices  60.6 us (36%)
  Pallas kernels  55.4 us (33%)
  waiting for transfers between devices  33.1 us (20%)
  local copies, waits for them, and re-layouts  12.7 us (8%)
  other arithmetic  6.01 us (4%)
    ppermute x18, starting transfers between devices, along_x(): lax.ppermute(value, 'tensor', [(i, i // 4 * 4 + (i + step) % 4) for i in...  27.1 us
    pallas_call x6, Pallas kernels, weight_grad(): pl.pallas_call(functools.partial(weight_body, total is not None, len(args...  25.5 us
    ppermute x6, starting transfers between devices, along_z(): lax.ppermute(value, 'tensor', [(i, (i + 4 * step) % 16) for i in range(16)])  21.3 us
    ppermute x18, waiting for transfers between devices, along_x(): lax.ppermute(value, 'tensor', [(i, i // 4 * 4 + (i + step) % 4) for i in...  15.3 us
    pallas_call x3, Pallas kernels, stage(): pl.pallas_call(functools.partial(stage_body, groups, send), out_shape=out...  13.8 us
    unnamed x58, local copies, waits for them, and re-layouts  11.9 us
    ppermute x6, waiting for transfers between devices, along_z(): lax.ppermute(value, 'tensor', [(i, (i + 4 * step) % 16) for i in range(16)])  11.7 us
    all_to_all x2, starting transfers between devices, over_y(): lax.all_to_all(sums, 'dp', 0, 0, axis_index_groups=groups, tiled=True)  9.95 us
  transfers between devices with their start and end apart: 30, of which 10 were waited for; matrix products, arithmetic and copies ran while one was open for 3% of the time, Pallas kernels for 29%

profile of v2, /device:TPU:8, one launch (start us, length us, event | category | flops | bytes accessed | tf_op | source)
XLA Modules:
  0.0 168.8 jit_solution(16899631202595137577)
XLA Ops:
  0.6 1.1 pad_maximum_fusion.1.refs_0_
  1.7 1.6 collective-permute-start
  3.3 3.3 %collective-permute-start.7 = (bf16[2,72,1536]{2,1,0:T(8,128)(2,1)S(1)}, bf16[2,72,1536]{2,1,0:T(8,128)(2,1)S(1)}, u32[]{:S(2)}, u32[]{:S(2)}) collective-permute-start(bf16[2,72,1536]{2,1,0:T(8,128)(2,1)S(1)} %pad_maximum_fusion.1.refs_0_), channel_id=1, source_target_pairs={{0,4},{1,5},{2,6},{3,7},{4,8},{5,9},{6,10},{7,11},{8,12},{9,13},{1... | collective-permute-start | bytes 1327112 | tf_op jit(solution)/shard_map/ppermute | solution.py:28
  6.6 3.0 %collective-permute-start.11 = (bf16[2,72,1536]{2,1,0:T(8,128)(2,1)S(1)}, bf16[2,72,1536]{2,1,0:T(8,128)(2,1)S(1)}, u32[]{:S(2)}, u32[]{:S(2)}) collective-permute-start(bf16[2,72,1536]{2,1,0:T(8,128)(2,1)S(1)} %pad_maximum_fusion.1.refs_0_), channel_id=1, source_target_pairs={{0,12},{1,13},{2,14},{3,15},{4,0},{5,1},{6,2},{7,3},{8,4},{9,5},{1... | collective-permute-start | bytes 1327112 | tf_op jit(solution)/shard_map/ppermute | solution.py:28
  9.6 1.7 %collective-permute-start.5 = (bf16[2,72,1536]{2,1,0:T(8,128)(2,1)S(1)}, bf16[2,72,1536]{2,1,0:T(8,128)(2,1)S(1)}, u32[]{:S(2)}, u32[]{:S(2)}) collective-permute-start(bf16[2,72,1536]{2,1,0:T(8,128)(2,1)S(1)} %pad_maximum_fusion.1.refs_0_), channel_id=1, source_target_pairs={{0,3},{1,0},{2,1},{3,2},{4,7},{5,4},{6,5},{7,6},{8,11},{9,8},{10,9... | collective-permute-start | bytes 1327112 | tf_op jit(solution)/shard_map/ppermute | solution.py:24
  11.3 3.6 %collective-permute-done.after.refs_1_ = bf16[2,72,1536]{2,1,0:T(8,128)(2,1)S(1)} collective-permute-done((bf16[2,72,1536]{2,1,0:T(8,128)(2,1)S(1)}, bf16[2,72,1536]{2,1,0:T(8,128)(2,1)S(1)}, u32[]{:S(2)}, u32[]{:S(2)}) %collective-permute-start) | collective-permute-done | bytes 442400 | tf_op jit(solution)/shard_map/ppermute | solution.py:24
  14.9 0.8 copy-done.9
  15.7 1.8 %pack.1 = bf16[2,72,1536]{2,1,0:T(8,128)(2,1)} custom-call(bf16[72,1536]{1,0:T(8,128)(2,1)} %rows.1, bf16[72,1536]{1,0:T(8,128)(2,1)} %grads.1, bf16[2,72,1536]{2,1,0:T(8,128)(2,1)} %copy-done.9), custom_call_target="tpu_custom_call" | custom-call | bytes 1048576 | tf_op jit(solution)/shard_map/pack/pallas_call | solution.py:48
  17.5 1.8 %collective-permute-start.6 = (bf16[2,72,1536]{2,1,0:T(8,128)(2,1)}, bf16[2,72,1536]{2,1,0:T(8,128)(2,1)S(1)}, u32[]{:S(2)}, u32[]{:S(2)}) collective-permute-start(bf16[2,72,1536]{2,1,0:T(8,128)(2,1)} %pack.1), channel_id=1, source_target_pairs={{0,2},{1,3},{2,0},{3,1},{4,6},{5,7},{6,4},{7,5},{8,10},{9,11},{10,... | collective-permute-start | bytes 1327112 | tf_op jit(solution)/shard_map/ppermute | solution.py:24
  19.3 3.6 %collective-permute-done.7.refs_0_ = bf16[2,72,1536]{2,1,0:T(8,128)(2,1)S(1)} collective-permute-done((bf16[2,72,1536]{2,1,0:T(8,128)(2,1)S(1)}, bf16[2,72,1536]{2,1,0:T(8,128)(2,1)S(1)}, u32[]{:S(2)}, u32[]{:S(2)}) %collective-permute-start.7) | collective-permute-done | bytes 442400 | tf_op jit(solution)/shard_map/ppermute | solution.py:28
  22.9 1.5 collective-permute-start.8
  24.4 5.7 %collective-permute-done.11.refs_4_ = bf16[2,72,1536]{2,1,0:T(8,128)(2,1)S(1)} collective-permute-done((bf16[2,72,1536]{2,1,0:T(8,128)(2,1)S(1)}, bf16[2,72,1536]{2,1,0:T(8,128)(2,1)S(1)}, u32[]{:S(2)}, u32[]{:S(2)}) %collective-permute-start.11) | collective-permute-done | bytes 442400 | tf_op jit(solution)/shard_map/ppermute | solution.py:28
  30.1 1.7 %collective-permute-start.13 = (bf16[2,72,1536]{2,1,0:T(8,128)(2,1)S(1)}, bf16[2,72,1536]{2,1,0:T(8,128)(2,1)S(1)}, u32[]{:S(2)}, u32[]{:S(2)}) collective-permute-start(bf16[2,72,1536]{2,1,0:T(8,128)(2,1)S(1)} %collective-permute-done.11.refs_4_), channel_id=1, source_target_pairs={{0,3},{1,0},{2,1},{3,2},{4,7},{5,4},{6,5},{7,6},{8,11},{9,8},{10,9... | collective-permute-start | bytes 1327112 | tf_op jit(solution)/shard_map/ppermute | solution.py:24
  31.9 5.0 %collective-permute-start.1 = (bf16[2,72,1536]{2,1,0:T(8,128)(2,1)}, bf16[2,72,1536]{2,1,0:T(8,128)(2,1)S(1)}, u32[]{:S(2)}, u32[]{:S(2)}) collective-permute-start(bf16[2,72,1536]{2,1,0:T(8,128)(2,1)} %pack.1), channel_id=1, source_target_pairs={{0,8},{1,9},{2,10},{3,11},{4,12},{5,13},{6,14},{7,15},{8,0},{9,1},... | collective-permute-start | bytes 1327112 | tf_op jit(solution)/shard_map/ppermute | solution.py:28
  37.2 3.0 %collective-permute-start.9 = (bf16[2,72,1536]{2,1,0:T(8,128)(2,1)S(1)}, bf16[2,72,1536]{2,1,0:T(8,128)(2,1)S(1)}, u32[]{:S(2)}, u32[]{:S(2)}) collective-permute-start(bf16[2,72,1536]{2,1,0:T(8,128)(2,1)S(1)} %collective-permute-done.7.refs_0_), channel_id=1, source_target_pairs={{0,3},{1,0},{2,1},{3,2},{4,7},{5,4},{6,5},{7,6},{8,11},{9,8},{10,9... | collective-permute-start | bytes 1327112 | tf_op jit(solution)/shard_map/ppermute | solution.py:24
  40.2 1.8 %collective-permute-start.10 = (bf16[2,72,1536]{2,1,0:T(8,128)(2,1)S(1)}, bf16[2,72,1536]{2,1,0:T(8,128)(2,1)S(1)}, u32[]{:S(2)}, u32[]{:S(2)}) collective-permute-start(bf16[2,72,1536]{2,1,0:T(8,128)(2,1)S(1)} %collective-permute-done.8.refs_1_), channel_id=1, source_target_pairs={{0,1},{1,2},{2,3},{3,0},{4,5},{5,6},{6,7},{7,4},{8,9},{9,10},{10,1... | collective-permute-start | bytes 1327112 | tf_op jit(solution)/shard_map/ppermute | solution.py:24
  41.9 1.3 collective-permute-done.13.refs_6_
  43.2 3.0 %collective-permute-start.14 = (bf16[2,72,1536]{2,1,0:T(8,128)(2,1)S(1)}, bf16[2,72,1536]{2,1,0:T(8,128)(2,1)S(1)}, u32[]{:S(2)}, u32[]{:S(2)}) collective-permute-start(bf16[2,72,1536]{2,1,0:T(8,128)(2,1)S(1)} %collective-permute-done.13.refs_6_), channel_id=1, source_target_pairs={{0,3},{1,0},{2,1},{3,2},{4,7},{5,4},{6,5},{7,6},{8,11},{9,8},{10,9... | collective-permute-start | bytes 1327112 | tf_op jit(solution)/shard_map/ppermute | solution.py:24
  46.2 2.3 %pad_maximum_fusion.refs_4_.refs_8_.refs_2_ = bf16[1120,1536]{1,0:T(8,128)(2,1)S(1)} fusion(bf16[560,1536]{1,0:T(8,128)(2,1)} %bitcast.8, bf16[560,1536]{1,0:T(8,128)(2,1)} %bitcast.9), kind=kLoop, calls=%fused_computation | loop fusion | flops 6881280 | bytes 6881280 | tf_op jit(solution)/shard_map/concatenate | solution.py:267
  48.8 2.2 %stage.4 = (bf16[288,1536]{1,0:T(8,128)(2,1)S(1)}, bf16[288,1536]{1,0:T(8,128)(2,1)S(1)}, bf16[288,1120]{1,0:T(8,128)(2,1)S(1)}, bf16[288,560]{1,0:T(8,128)(2,1)S(1)}) custom-call(bf16[2,72,1536]{2,1,0:T(8,128)(2,1)S(1)} %pad_maximum_fusion.1.refs_0_, bf16[2,72,1536]{2,1,0:T(8,128)(2,1)S(1)} %copy-done.10, ...), custom_call_target="tpu_custom_call" | custom-call | tf_op jit(solution)/shard_map/stage/pallas_call | solution.py:103
  51.0 0.9 copy-done.15
  51.9 3.5 %weight_grad.6.refs_2_ = f32[1536,1120]{1,0:T(8,128)S(1)} custom-call(s32[2]{0:T(128)S(1)} %pad_add_fusion.place, bf16[288,1536]{1,0:T(8,128)(2,1)S(1)} %get-tuple-element.41.refs_0_, bf16[288,1120]{1,0:T(8,128)(2,1)S(1)} %get-tuple-element.37.refs_1_), custom_call_target="tpu_custom_call" | custom-call | tf_op jit(solution)/shard_map/weight_grad/pallas_call | solution.py:179
  55.4 2.8 %copy-done.2 = f32[1536,1120]{1,0:T(8,128)} copy-done((f32[1536,1120]{1,0:T(8,128)}, f32[1536,1120]{1,0:T(8,128)S(1)}, u32[]{:S(2)}) %copy-start.2) | copy-done | bytes 6881304
  58.3 3.2 %collective-permute-start.3 = (bf16[2,72,1536]{2,1,0:T(8,128)(2,1)S(1)}, bf16[2,72,1536]{2,1,0:T(8,128)(2,1)S(1)}, u32[]{:S(2)}, u32[]{:S(2)}) collective-permute-start(bf16[2,72,1536]{2,1,0:T(8,128)(2,1)S(1)} %collective-permute-done.1.refs_0_), channel_id=1, source_target_pairs={{0,3},{1,0},{2,1},{3,2},{4,7},{5,4},{6,5},{7,6},{8,11},{9,8},{10,9... | collective-permute-start | bytes 1327112 | tf_op jit(solution)/shard_map/ppermute | solution.py:24
  61.5 0.7 collective-permute-done.14.refs_7_
  62.2 9.5 %stage.5 = (bf16[576,1536]{1,0:T(8,128)(2,1)S(1)}, bf16[576,1536]{1,0:T(8,128)(2,1)S(1)}, bf16[576,1120]{1,0:T(8,128)(2,1)S(1)}, bf16[576,560]{1,0:T(8,128)(2,1)...) custom-call(bf16[2,72,1536]{2,1,0:T(8,128)(2,1)S(1)} %collective-per, ...), custom_call_target="tpu_custom_call" | custom-call | flops 4954521600 | bytes 12582912 | tf_op jit(solution)/shard_map/stage/pallas_call | solution.py:103
  71.7 8.2 %weight_grad.7.refs_2_ = f32[1536,1120]{1,0:T(8,128)S(1)} custom-call(s32[2]{0:T(128)S(1)} %pad_add_fusion.place, bf16[576,1536]{1,0:T(8,128)(2,1)S(1)} %get-tuple-element.39.refs_0_, bf16[576,1120]{1,0:T(8,128)(2,1)S(1)} %get-tuple-element.40.refs_1_, f32[1536,1120]{1,0:T(8,128)} %copy-done.2), custom_call_target="tpu_custom_call" | custom-call | tf_op jit(solution)/shard_map/weight_grad/pallas_call | solution.py:179
  80.0 2.2 %stage.3 = (bf16[288,1536]{1,0:T(8,128)(2,1)S(1)}, bf16[288,1536]{1,0:T(8,128)(2,1)S(1)}, bf16[288,1120]{1,0:T(8,128)(2,1)S(1)}, bf16[288,560]{1,0:T(8,128)(2,1)S(1)}) custom-call(bf16[2,72,1536]{2,1,0:T(8,128)(2,1)S(1)} %collective-permute-done.1.refs_0_, bf16[2,72,1536]{2,1,0:T(8,128)(2,1)S(1)} %collective-permute-done.2.refs_1_, ...), custom_call_target="tpu_custom_call" | custom-call | tf_op jit(solution)/shard_map/stage/pallas_call | solution.py:103
  82.1 1.0 copy-done.17
  83.1 0.8 copy-done.23
  83.9 3.9 %weight_grad.8 = (bf16[4,2,96,1120]{3,2,1,0:T(8,128)(2,1)S(1)}, f32[4,2,96,1120]{3,2,1,0:T(8,128)S(1)}) custom-call(s32[2]{0:T(128)S(1)} %pad_add_fusion.place, bf16[288,1536]{1,0:T(8,128)(2,1)S(1)} %get-tuple-element.38.refs_0_, bf16[288,1120]{1,0:T(8,128)(2,1)S(1)} %get-tuple-element.36.refs_1_.refs_0_, f32[1536,1120]{1,0:T(8,128)S(1)} %weight_grad.7.refs_2_), custom_call_target="tpu_custom_call" | custom-call | tf_op jit(solution)/shard_map/weight_grad/pallas_call | solution.py:179
  87.9 3.0 %collective-permute-start.18 = (bf16[2,72,1536]{2,1,0:T(8,128)(2,1)}, bf16[2,72,1536]{2,1,0:T(8,128)(2,1)}, u32[]{:S(2)}, u32[]{:S(2)}) collective-permute-start(bf16[2,72,1536]{2,1,0:T(8,128)(2,1)} %get-tuple-element.54), channel_id=1, source_target_pairs={{0,3},{1,0},{2,1},{3,2},{4,7},{5,4},{6,5},{7,6},{8,11},{9,8},{10,9... | collective-permute-start | bytes 1327112 | tf_op jit(solution)/shard_map/ppermute | solution.py:24
  91.0 1.9 %collective-permute-start.20 = (bf16[2,72,1536]{2,1,0:T(8,128)(2,1)}, bf16[2,72,1536]{2,1,0:T(8,128)(2,1)}, u32[]{:S(2)}, u32[]{:S(2)}) collective-permute-start(bf16[2,72,1536]{2,1,0:T(8,128)(2,1)} %get-tuple-element.56), channel_id=1, source_target_pairs={{0,2},{1,3},{2,0},{3,1},{4,6},{5,7},{6,4},{7,5},{8,10},{9,11},{10,... | collective-permute-start | bytes 1327112 | tf_op jit(solution)/shard_map/ppermute | solution.py:24
  92.9 3.3 %late_partials.1 = (f32[2,72,1536]{2,1,0:T(8,128)S(1)}, bf16[2,72,1536]{2,1,0:T(8,128)(2,1)S(1)}, bf16[2,72,1536]{2,1,0:T(8,128)(2,1)}, bf16[2,72,1536]{2,1,0:T(8,128)(2,1)}) custom-call(bf16[288,1120]{1,0:T(8,128)(2,1)S(1)} %get-tuple-element.36.refs_1_.refs_0_, bf16[288,1120]{1,0:T(8,128)(2,1)S(1)} %copy-done.6, bf16[1120,1536]{1,0:T(8,128)(2,1)S(1)} %copy-done.1, ...), custom_call_target="tpu_custom_call" | custom-call | tf_op jit(solution)/shard_map/late_partials/pallas_call | solution.py:124
  96.2 0.8 copy-done.27
  97.0 1.9 %over_cores.2.refs_0_ = bf16[4,2,96,1120]{3,2,1,0:T(8,128)(2,1)} custom-call(f32[4,2,96,1120]{3,2,1,0:T(8,128)S(1)} %get-tuple-element.57.keep, bf16[4,2,96,1120]{3,2,1,0:T(8,128)(2,1)S(1)} %collective-permute-done.21.got, f32[2,72,1536]{2,1,0:T(8,128)S(1)} %get-tuple-element.43.refs_0_.own), custom_call_target="tpu_custom_call" | custom-call | tf_op jit(solution)/shard_map/over_cores/pallas_call | solution.py:222
  98.9 5.0 %all-to-all-start = ((bf16[4,2,96,1120]{3,2,1,0:T(8,128)(2,1)}), bf16[4,2,96,1120]{3,2,1,0:T(8,128)(2,1)S(1)}, u32[]{:S(2)}, u32[]{:S(2)}) async-start(bf16[4,2,96,1120]{3,2,1,0:T(8,128)(2,1)} %over_cores.2.refs_0_), calls=%async_computation | async-start | bytes 3538944 | tf_op jit(solution)/shard_map/all_to_all | solution.py:236
  104.0 1.0 copy-done.26
  105.0 2.7 %weight_grad.9.refs_2_ = f32[1536,560]{1,0:T(8,128)S(1)} custom-call(s32[2]{0:T(128)S(1)} %pad_add_fusion.place, bf16[288,1536]{1,0:T(8,128)(2,1)S(1)} %copy-done.16, bf16[288,560]{1,0:T(8,128)(2,1)S(1)} %copy-done.26), custom_call_target="tpu_custom_call" | custom-call | tf_op jit(solution)/shard_map/weight_grad/pallas_call | solution.py:179
  107.7 3.4 %weight_grad.10.refs_2_ = f32[1536,560]{1,0:T(8,128)S(1)} custom-call(s32[2]{0:T(128)S(1)} %pad_add_fusion.place, bf16[576,1536]{1,0:T(8,128)(2,1)S(1)} %copy-done.12, bf16[576,560]{1,0:T(8,128)(2,1)S(1)} %copy-done.20, f32[1536,560]{1,0:T(8,128)S(1)} %weight_grad.9.refs_2_), custom_call_target="tpu_custom_call" | custom-call | tf_op jit(solution)/shard_map/weight_grad/pallas_call | solution.py:179
  111.1 3.1 %collective-permute-done.19.right = bf16[2,72,1536]{2,1,0:T(8,128)(2,1)} collective-permute-done((bf16[2,72,1536]{2,1,0:T(8,128)(2,1)}, bf16[2,72,1536]{2,1,0:T(8,128)(2,1)}, u32[]{:S(2)}, u32[]{:S(2)}) %collective-permute-start.19) | collective-permute-done | bytes 442400 | tf_op jit(solution)/shard_map/ppermute | solution.py:24
  114.2 2.3 %add_parts.2 = (bf16[72,1536]{1,0:T(8,128)(2,1)}, bf16[72,1536]{1,0:T(8,128)(2,1)}) custom-call(f32[2,72,1536]{2,1,0:T(8,128)S(1)} %copy-done.14, bf16[2,72,1536]{2,1,0:T(8,128)(2,1)} %collective-permute-done.18.left, bf16[2,72,1536]{2,1,0:T(8,128)(2,1)} %collective-permute-done.19.right, bf16[2,72,1536]{2,1,0:T(8,128)(2,1)} %collective-permute-done.20.far, ...), custom_call_target="tpu_custom_call" | custom-call | tf_op jit(solution)/shard_map/add_parts/pallas_call | solution.py:252
  116.5 3.7 %weight_grad.11 = (bf16[4,2,96,560]{3,2,1,0:T(8,128)(2,1)}, f32[4,2,96,560]{3,2,1,0:T(8,128)S(1)}) custom-call(s32[2]{0:T(128)S(1)} %pad_add_fusion.place, bf16[288,1536]{1,0:T(8,128)(2,1)S(1)} %copy-done.18, bf16[288,560]{1,0:T(8,128)(2,1)S(1)} %copy-done.24, f32[1536,560]{1,0:T(8,128)S(1)} %weight_grad.10.refs_2_, bf16[72,1536]{1,0:T(8,128)(2,1)} %get-tuple-element.58.refs_3_), custom_call_target="tpu_custom_call" | custom-call | tf_op jit(solution)/shard_map/weight_grad/pallas_call | solution.py:179
  120.2 1.3 copy-done.7
  121.8 1.7 %collective-permute-start.16 = (bf16[2,72,1536]{2,1,0:T(8,128)(2,1)}, bf16[2,72,1536]{2,1,0:T(8,128)(2,1)}, u32[]{:S(2)}, u32[]{:S(2)}) collective-permute-start(bf16[2,72,1536]{2,1,0:T(8,128)(2,1)} %get-tuple-element.45), channel_id=1, source_target_pairs={{0,1},{1,2},{2,3},{3,0},{4,5},{5,6},{6,7},{7,4},{8,9},{9,10},{10,1... | collective-permute-start | bytes 1327112 | tf_op jit(solution)/shard_map/ppermute | solution.py:24
  124.1 3.8 %collective-permute-start.23 = (bf16[72,1536]{1,0:T(8,128)(2,1)}, bf16[72,1536]{1,0:T(8,128)(2,1)S(1)}, u32[]{:S(2)}, u32[]{:S(2)}) collective-permute-start(bf16[72,1536]{1,0:T(8,128)(2,1)} %get-tuple-element.61), channel_id=1, source_target_pairs={{0,4},{1,5},{2,6},{3,7},{4,8},{5,9},{6,10},{7,11},{8,12},{9,13},{1... | collective-permute-start | bytes 663560 | tf_op jit(solution)/shard_map/ppermute | solution.py:28
  127.9 6.6 %collective-permute-done.15.left = bf16[2,72,1536]{2,1,0:T(8,128)(2,1)S(1)} collective-permute-done((bf16[2,72,1536]{2,1,0:T(8,128)(2,1)S(1)}, bf16[2,72,1536]{2,1,0:T(8,128)(2,1)S(1)}, u32[]{:S(2)}, u32[]{:S(2)}) %collective-permute-start.15) | collective-permute-done | bytes 442400 | tf_op jit(solution)/shard_map/ppermute | solution.py:24
  134.5 2.8 %collective-permute-start.24 = (bf16[72,1536]{1,0:T(8,128)(2,1)}, bf16[72,1536]{1,0:T(8,128)(2,1)S(1)}, u32[]{:S(2)}, u32[]{:S(2)}) collective-permute-start(bf16[72,1536]{1,0:T(8,128)(2,1)} %get-tuple-element.58.refs_3_), channel_id=1, source_target_pairs={{0,12},{1,13},{2,14},{3,15},{4,0},{5,1},{6,2},{7,3},{8,4},{9,5},{1... | collective-permute-start | bytes 663560 | tf_op jit(solution)/shard_map/ppermute | solution.py:28
  137.3 1.3 add_chunks.2
  138.7 0.8 copy-done.21
  139.4 1.1 collective-permute-start.26
  140.6 1.5 copy-done.8
  142.1 3.4 %over_cores.3.refs_0_ = bf16[4,2,96,560]{3,2,1,0:T(8,128)(2,1)} custom-call(f32[4,2,96,560]{3,2,1,0:T(8,128)S(1)} %copy-done.8, bf16[4,2,96,560]{3,2,1,0:T(8,128)(2,1)} %collective-permute-done.22.got, bf16[4,2,96,1120]{3,2,1,0:T(8,128)(2,1)S(1)} %all-to-all-done.refs_0_.got), custom_call_target="tpu_custom_call" | custom-call | tf_op jit(solution)/shard_map/over_cores/pallas_call | solution.py:222
  145.5 4.9 %all-to-all-start.1 = ((bf16[4,2,96,560]{3,2,1,0:T(8,128)(2,1)}), bf16[4,2,96,560]{3,2,1,0:T(8,128)(2,1)S(1)}, u32[]{:S(2)}, u32[]{:S(2)}) async-start(bf16[4,2,96,560]{3,2,1,0:T(8,128)(2,1)} %over_cores.3.refs_0_), calls=%async_computation.1 | async-start | bytes 1966080 | tf_op jit(solution)/shard_map/all_to_all | solution.py:236
  150.5 1.4 add_parts.3
  151.9 3.5 %collective-permute-start.25 = (bf16[72,1536]{1,0:T(8,128)(2,1)S(1)}, bf16[72,1536]{1,0:T(8,128)(2,1)S(1)}, u32[]{:S(2)}, u32[]{:S(2)}) collective-permute-start(bf16[72,1536]{1,0:T(8,128)(2,1)S(1)} %get-tuple-element.63), channel_id=1, source_target_pairs={{0,8},{1,9},{2,10},{3,11},{4,12},{5,13},{6,14},{7,15},{8,0},{9,1},... | collective-permute-start | bytes 663560 | tf_op jit(solution)/shard_map/ppermute | solution.py:28
  155.3 1.0 add_multiply_fusion
  156.3 0.8 fusion
  157.1 5.3 %all-to-all-done.1.got = bf16[4,2,96,560]{3,2,1,0:T(8,128)(2,1)S(1)} async-done(((bf16[4,2,96,560]{3,2,1,0:T(8,128)(2,1)}), bf16[4,2,96,560]{3,2,1,0:T(8,128)(2,1)S(1)}, u32[]{:S(2)}, u32[]{:S(2)}) %all-to-all-start.1) | async-done | bytes 860192 | tf_op jit(solution)/shard_map/all_to_all | solution.py:236
  163.1 1.0 collective-permute-start.27
  164.1 2.4 %collective-permute-done.25 = bf16[72,1536]{1,0:T(8,128)(2,1)S(1)} collective-permute-done((bf16[72,1536]{1,0:T(8,128)(2,1)S(1)}, bf16[72,1536]{1,0:T(8,128)(2,1)S(1)}, u32[]{:S(2)}, u32[]{:S(2)}) %collective-permute-start.25) | collective-permute-done | bytes 221216 | tf_op jit(solution)/shard_map/ppermute | solution.py:28
  166.4 0.8 add_convert_fusion
  167.2 0.8 collective-permute-done.27
  168.1 0.7 multiply_bitcast_fusion
  (78 shorter events, 2.3 us)
Async XLA Ops:
  1.7 13.2 %collective-permute-start = (bf16[2,72,1536]{2,1,0:T(8,128)(2,1)S(1)}, bf16[2,72,1536]{2,1,0:T(8,128)(2,1)S(1)}, u32[]{:S(2)}, u32[]{:S(2)}) collective-permute-start(bf16[2,72,1536]{2,1,0:T(8,128)(2,1)S(1)} %pad_maximum_fusion.1.refs_0_), channel_id=1, source_target_pairs={{0,1},{1,2},{2,3},{3,0},{4,5},{5,6},{6,7},{7,4},{8,9},{9,10},{10,1... | collective-permute-start | bytes 1327112 | tf_op jit(solution)/shard_map/ppermute | solution.py:24
  3.3 19.6 %collective-permute-start.7 = (bf16[2,72,1536]{2,1,0:T(8,128)(2,1)S(1)}, bf16[2,72,1536]{2,1,0:T(8,128)(2,1)S(1)}, u32[]{:S(2)}, u32[]{:S(2)}) collective-permute-start(bf16[2,72,1536]{2,1,0:T(8,128)(2,1)S(1)} %pad_maximum_fusion.1.refs_0_), channel_id=1, source_target_pairs={{0,4},{1,5},{2,6},{3,7},{4,8},{5,9},{6,10},{7,11},{8,12},{9,13},{1... | collective-permute-start | bytes 1327112 | tf_op jit(solution)/shard_map/ppermute | solution.py:28
  6.6 23.6 %collective-permute-start.11 = (bf16[2,72,1536]{2,1,0:T(8,128)(2,1)S(1)}, bf16[2,72,1536]{2,1,0:T(8,128)(2,1)S(1)}, u32[]{:S(2)}, u32[]{:S(2)}) collective-permute-start(bf16[2,72,1536]{2,1,0:T(8,128)(2,1)S(1)} %pad_maximum_fusion.1.refs_0_), channel_id=1, source_target_pairs={{0,12},{1,13},{2,14},{3,15},{4,0},{5,1},{6,2},{7,3},{8,4},{9,5},{1... | collective-permute-start | bytes 1327112 | tf_op jit(solution)/shard_map/ppermute | solution.py:28
  9.6 27.3 %collective-permute-start.5 = (bf16[2,72,1536]{2,1,0:T(8,128)(2,1)S(1)}, bf16[2,72,1536]{2,1,0:T(8,128)(2,1)S(1)}, u32[]{:S(2)}, u32[]{:S(2)}) collective-permute-start(bf16[2,72,1536]{2,1,0:T(8,128)(2,1)S(1)} %pad_maximum_fusion.1.refs_0_), channel_id=1, source_target_pairs={{0,3},{1,0},{2,1},{3,2},{4,7},{5,4},{6,5},{7,6},{8,11},{9,8},{10,9... | collective-permute-start | bytes 1327112 | tf_op jit(solution)/shard_map/ppermute | solution.py:24
  14.9 0.8 copy-start.9
  17.5 19.7 %collective-permute-start.6 = (bf16[2,72,1536]{2,1,0:T(8,128)(2,1)}, bf16[2,72,1536]{2,1,0:T(8,128)(2,1)S(1)}, u32[]{:S(2)}, u32[]{:S(2)}) collective-permute-start(bf16[2,72,1536]{2,1,0:T(8,128)(2,1)} %pack.1), channel_id=1, source_target_pairs={{0,2},{1,3},{2,0},{3,1},{4,6},{5,7},{6,4},{7,5},{8,10},{9,11},{10,... | collective-permute-start | bytes 1327112 | tf_op jit(solution)/shard_map/ppermute | solution.py:24
  22.9 17.3 %collective-permute-start.8 = (bf16[2,72,1536]{2,1,0:T(8,128)(2,1)S(1)}, bf16[2,72,1536]{2,1,0:T(8,128)(2,1)S(1)}, u32[]{:S(2)}, u32[]{:S(2)}) collective-permute-start(bf16[2,72,1536]{2,1,0:T(8,128)(2,1)S(1)} %collective-permute-done.7.refs_0_), channel_id=1, source_target_pairs={{0,1},{1,2},{2,3},{3,0},{4,5},{5,6},{6,7},{7,4},{8,9},{9,10},{10,1... | collective-permute-start | bytes 1327112 | tf_op jit(solution)/shard_map/ppermute | solution.py:24
  30.1 13.1 %collective-permute-start.13 = (bf16[2,72,1536]{2,1,0:T(8,128)(2,1)S(1)}, bf16[2,72,1536]{2,1,0:T(8,128)(2,1)S(1)}, u32[]{:S(2)}, u32[]{:S(2)}) collective-permute-start(bf16[2,72,1536]{2,1,0:T(8,128)(2,1)S(1)} %collective-permute-done.11.refs_4_), channel_id=1, source_target_pairs={{0,3},{1,0},{2,1},{3,2},{4,7},{5,4},{6,5},{7,6},{8,11},{9,8},{10,9... | collective-permute-start | bytes 1327112 | tf_op jit(solution)/shard_map/ppermute | solution.py:24
  31.9 26.3 %collective-permute-start.1 = (bf16[2,72,1536]{2,1,0:T(8,128)(2,1)}, bf16[2,72,1536]{2,1,0:T(8,128)(2,1)S(1)}, u32[]{:S(2)}, u32[]{:S(2)}) collective-permute-start(bf16[2,72,1536]{2,1,0:T(8,128)(2,1)} %pack.1), channel_id=1, source_target_pairs={{0,8},{1,9},{2,10},{3,11},{4,12},{5,13},{6,14},{7,15},{8,0},{9,1},... | collective-permute-start | bytes 1327112 | tf_op jit(solution)/shard_map/ppermute | solution.py:28
  36.9 21.3 %collective-permute-start.12 = (bf16[2,72,1536]{2,1,0:T(8,128)(2,1)S(1)}, bf16[2,72,1536]{2,1,0:T(8,128)(2,1)S(1)}, u32[]{:S(2)}, u32[]{:S(2)}) collective-permute-start(bf16[2,72,1536]{2,1,0:T(8,128)(2,1)S(1)} %collective-permute-done.11.refs_4_), channel_id=1, source_target_pairs={{0,1},{1,2},{2,3},{3,0},{4,5},{5,6},{6,7},{7,4},{8,9},{9,10},{10,1... | collective-permute-start | bytes 1327112 | tf_op jit(solution)/shard_map/ppermute | solution.py:24
  37.2 24.3 %collective-permute-start.9 = (bf16[2,72,1536]{2,1,0:T(8,128)(2,1)S(1)}, bf16[2,72,1536]{2,1,0:T(8,128)(2,1)S(1)}, u32[]{:S(2)}, u32[]{:S(2)}) collective-permute-start(bf16[2,72,1536]{2,1,0:T(8,128)(2,1)S(1)} %collective-permute-done.7.refs_0_), channel_id=1, source_target_pairs={{0,3},{1,0},{2,1},{3,2},{4,7},{5,4},{6,5},{7,6},{8,11},{9,8},{10,9... | collective-permute-start | bytes 1327112 | tf_op jit(solution)/shard_map/ppermute | solution.py:24
  40.2 21.3 %collective-permute-start.10 = (bf16[2,72,1536]{2,1,0:T(8,128)(2,1)S(1)}, bf16[2,72,1536]{2,1,0:T(8,128)(2,1)S(1)}, u32[]{:S(2)}, u32[]{:S(2)}) collective-permute-start(bf16[2,72,1536]{2,1,0:T(8,128)(2,1)S(1)} %collective-permute-done.8.refs_1_), channel_id=1, source_target_pairs={{0,1},{1,2},{2,3},{3,0},{4,5},{5,6},{6,7},{7,4},{8,9},{9,10},{10,1... | collective-permute-start | bytes 1327112 | tf_op jit(solution)/shard_map/ppermute | solution.py:24
  43.2 19.0 %collective-permute-start.14 = (bf16[2,72,1536]{2,1,0:T(8,128)(2,1)S(1)}, bf16[2,72,1536]{2,1,0:T(8,128)(2,1)S(1)}, u32[]{:S(2)}, u32[]{:S(2)}) collective-permute-start(bf16[2,72,1536]{2,1,0:T(8,128)(2,1)S(1)} %collective-permute-done.13.refs_6_), channel_id=1, source_target_pairs={{0,3},{1,0},{2,1},{3,2},{4,7},{5,4},{6,5},{7,6},{8,11},{9,8},{10,9... | collective-permute-start | bytes 1327112 | tf_op jit(solution)/shard_map/ppermute | solution.py:24
  46.2 2.5 %copy-start.3 = (bf16[560,1536]{1,0:T(8,128)(2,1)S(1)}, bf16[560,1536]{1,0:T(8,128)(2,1)}, u32[]{:S(2)}) copy-start(bf16[560,1536]{1,0:T(8,128)(2,1)} %refs_9_.1) | copy-start | bytes 5160964
  46.2 2.6 %copy-start.10 = (bf16[2,72,1536]{2,1,0:T(8,128)(2,1)S(1)}, bf16[2,72,1536]{2,1,0:T(8,128)(2,1)}, u32[]{:S(2)}) copy-start(bf16[2,72,1536]{2,1,0:T(8,128)(2,1)} %copy-done.9) | copy-start | bytes 1327108
  48.7 2.2 %copy-start = (bf16[1120,1536]{1,0:T(8,128)(2,1)}, bf16[1120,1536]{1,0:T(8,128)(2,1)S(1)}, u32[]{:S(2)}) copy-start(bf16[1120,1536]{1,0:T(8,128)(2,1)S(1)} %pad_maximum_fusion.refs_4_.refs_8_.refs_2_) | copy-start | bytes 10321924
  50.9 0.9 copy-start.15
  51.9 3.5 %copy-start.5 = (bf16[288,1120]{1,0:T(8,128)(2,1)}, bf16[288,1120]{1,0:T(8,128)(2,1)S(1)}, u32[]{:S(2)}) copy-start(bf16[288,1120]{1,0:T(8,128)(2,1)S(1)} %get-tuple-element.37.refs_1_) | copy-start | bytes 1935364
  51.9 3.6 %copy-start.25 = (bf16[288,560]{1,0:T(8,128)(2,1)}, bf16[288,560]{1,0:T(8,128)(2,1)S(1)}, u32[]{:S(2)}) copy-start(bf16[288,560]{1,0:T(8,128)(2,1)S(1)} %get-tuple-element.52.refs_1_) | copy-start | bytes 967684
  55.4 2.8 %copy-start.2 = (f32[1536,1120]{1,0:T(8,128)}, f32[1536,1120]{1,0:T(8,128)S(1)}, u32[]{:S(2)}) copy-start(f32[1536,1120]{1,0:T(8,128)S(1)} %weight_grad.6.refs_2_) | copy-start | bytes 20643844
  58.3 21.7 %collective-permute-start.2 = (bf16[2,72,1536]{2,1,0:T(8,128)(2,1)S(1)}, bf16[2,72,1536]{2,1,0:T(8,128)(2,1)S(1)}, u32[]{:S(2)}, u32[]{:S(2)}) collective-permute-start(bf16[2,72,1536]{2,1,0:T(8,128)(2,1)S(1)} %collective-permute-done.1.refs_0_), channel_id=1, source_target_pairs={{0,1},{1,2},{2,3},{3,0},{4,5},{5,6},{6,7},{7,4},{8,9},{9,10},{10,1... | collective-permute-start | bytes 1327112 | tf_op jit(solution)/shard_map/ppermute | solution.py:24
  58.3 21.7 %collective-permute-start.3 = (bf16[2,72,1536]{2,1,0:T(8,128)(2,1)S(1)}, bf16[2,72,1536]{2,1,0:T(8,128)(2,1)S(1)}, u32[]{:S(2)}, u32[]{:S(2)}) collective-permute-start(bf16[2,72,1536]{2,1,0:T(8,128)(2,1)S(1)} %collective-permute-done.1.refs_0_), channel_id=1, source_target_pairs={{0,3},{1,0},{2,1},{3,2},{4,7},{5,4},{6,5},{7,6},{8,11},{9,8},{10,9... | collective-permute-start | bytes 1327112 | tf_op jit(solution)/shard_map/ppermute | solution.py:24
  61.5 18.4 %collective-permute-start.4 = (bf16[2,72,1536]{2,1,0:T(8,128)(2,1)S(1)}, bf16[2,72,1536]{2,1,0:T(8,128)(2,1)S(1)}, u32[]{:S(2)}, u32[]{:S(2)}) collective-permute-start(bf16[2,72,1536]{2,1,0:T(8,128)(2,1)S(1)} %collective-permute-done.1.refs_0_), channel_id=1, source_target_pairs={{0,2},{1,3},{2,0},{3,1},{4,6},{5,7},{6,4},{7,5},{8,10},{9,11},{10,... | collective-permute-start | bytes 1327112 | tf_op jit(solution)/shard_map/ppermute | solution.py:24
  71.7 8.2 %copy-start.11 = (bf16[576,1536]{1,0:T(8,128)(2,1)}, bf16[576,1536]{1,0:T(8,128)(2,1)S(1)}, u32[]{:S(2)}) copy-start(bf16[576,1536]{1,0:T(8,128)(2,1)S(1)} %get-tuple-element.49.refs_0_) | copy-start | bytes 5308420
  71.7 8.2 %copy-start.13 = (f32[2,72,1536]{2,1,0:T(8,128)}, f32[2,72,1536]{2,1,0:T(8,128)S(1)}, u32[]{:S(2)}) copy-start(f32[2,72,1536]{2,1,0:T(8,128)S(1)} %get-tuple-element.53.own) | copy-start | bytes 2654212
  71.7 8.2 %copy-start.19 = (bf16[576,560]{1,0:T(8,128)(2,1)}, bf16[576,560]{1,0:T(8,128)(2,1)S(1)}, u32[]{:S(2)}) copy-start(bf16[576,560]{1,0:T(8,128)(2,1)S(1)} %get-tuple-element.50.refs_1_) | copy-start | bytes 1935364
  71.7 8.3 %copy-start.1 = (bf16[1120,1536]{1,0:T(8,128)(2,1)S(1)}, bf16[1120,1536]{1,0:T(8,128)(2,1)}, u32[]{:S(2)}) copy-start(bf16[1120,1536]{1,0:T(8,128)(2,1)} %copy-done) | copy-start | bytes 10321924
  71.7 8.3 %copy-start.4 = (bf16[560,1536]{1,0:T(8,128)(2,1)S(1)}, bf16[560,1536]{1,0:T(8,128)(2,1)}, u32[]{:S(2)}) copy-start(bf16[560,1536]{1,0:T(8,128)(2,1)} %refs_9_.1) | copy-start | bytes 5160964
  82.1 1.0 copy-start.17
  83.1 0.8 copy-start.23
  83.9 9.0 %copy-start.6 = (bf16[288,1120]{1,0:T(8,128)(2,1)S(1)}, bf16[288,1120]{1,0:T(8,128)(2,1)}, u32[]{:S(2)}) copy-start(bf16[288,1120]{1,0:T(8,128)(2,1)} %copy-done.5) | copy-start | bytes 1935364
  87.8 9.2 %collective-permute-start.21 = (bf16[4,2,96,1120]{3,2,1,0:T(8,128)(2,1)S(1)}, bf16[4,2,96,1120]{3,2,1,0:T(8,128)(2,1)S(1)}, u32[]{:S(2)}, u32[]{:S(2)}) collective-permute-start(bf16[4,2,96,1120]{3,2,1,0:T(8,128)(2,1)S(1)} %get-tuple-element.42.refs_3_), channel_id=1, source_target_pairs={{0,16},{16,0},{32,48},{48,32},{64,80},{80,64},{96,112},{112,96},{1... | collective-permute-start | bytes 5160968 | tf_op jit(solution)/shard_map/ppermute | solution.py:40
  87.9 23.2 %collective-permute-start.18 = (bf16[2,72,1536]{2,1,0:T(8,128)(2,1)}, bf16[2,72,1536]{2,1,0:T(8,128)(2,1)}, u32[]{:S(2)}, u32[]{:S(2)}) collective-permute-start(bf16[2,72,1536]{2,1,0:T(8,128)(2,1)} %get-tuple-element.54), channel_id=1, source_target_pairs={{0,3},{1,0},{2,1},{3,2},{4,7},{5,4},{6,5},{7,6},{8,11},{9,8},{10,9... | collective-permute-start | bytes 1327112 | tf_op jit(solution)/shard_map/ppermute | solution.py:24
  91.0 23.2 %collective-permute-start.19 = (bf16[2,72,1536]{2,1,0:T(8,128)(2,1)}, bf16[2,72,1536]{2,1,0:T(8,128)(2,1)}, u32[]{:S(2)}, u32[]{:S(2)}) collective-permute-start(bf16[2,72,1536]{2,1,0:T(8,128)(2,1)} %get-tuple-element.55), channel_id=1, source_target_pairs={{0,1},{1,2},{2,3},{3,0},{4,5},{5,6},{6,7},{7,4},{8,9},{9,10},{10,1... | collective-permute-start | bytes 1327112 | tf_op jit(solution)/shard_map/ppermute | solution.py:24
  91.0 23.2 %collective-permute-start.20 = (bf16[2,72,1536]{2,1,0:T(8,128)(2,1)}, bf16[2,72,1536]{2,1,0:T(8,128)(2,1)}, u32[]{:S(2)}, u32[]{:S(2)}) collective-permute-start(bf16[2,72,1536]{2,1,0:T(8,128)(2,1)} %get-tuple-element.56), channel_id=1, source_target_pairs={{0,2},{1,3},{2,0},{3,1},{4,6},{5,7},{6,4},{7,5},{8,10},{9,11},{10,... | collective-permute-start | bytes 1327112 | tf_op jit(solution)/shard_map/ppermute | solution.py:24
  96.2 0.8 copy-start.27
  98.9 5.0 %copy-start.16 = (bf16[288,1536]{1,0:T(8,128)(2,1)S(1)}, bf16[288,1536]{1,0:T(8,128)(2,1)}, u32[]{:S(2)}) copy-start(bf16[288,1536]{1,0:T(8,128)(2,1)} %copy-done.15) | copy-start | bytes 2654212
  98.9 38.4 %all-to-all-start = ((bf16[4,2,96,1120]{3,2,1,0:T(8,128)(2,1)}), bf16[4,2,96,1120]{3,2,1,0:T(8,128)(2,1)S(1)}, u32[]{:S(2)}, u32[]{:S(2)}) async-start(bf16[4,2,96,1120]{3,2,1,0:T(8,128)(2,1)} %over_cores.2.refs_0_), calls=%async_computation | async-start | bytes 3538944 | tf_op jit(solution)/shard_map/all_to_all | solution.py:236
  104.0 1.0 copy-start.26
  105.0 2.7 %copy-start.12 = (bf16[576,1536]{1,0:T(8,128)(2,1)S(1)}, bf16[576,1536]{1,0:T(8,128)(2,1)}, u32[]{:S(2)}) copy-start(bf16[576,1536]{1,0:T(8,128)(2,1)} %copy-done.11) | copy-start | bytes 5308420
  105.0 2.7 %copy-start.20 = (bf16[576,560]{1,0:T(8,128)(2,1)S(1)}, bf16[576,560]{1,0:T(8,128)(2,1)}, u32[]{:S(2)}) copy-start(bf16[576,560]{1,0:T(8,128)(2,1)} %copy-done.19) | copy-start | bytes 1935364
  107.7 6.5 %copy-start.14 = (f32[2,72,1536]{2,1,0:T(8,128)S(1)}, f32[2,72,1536]{2,1,0:T(8,128)}, u32[]{:S(2)}) copy-start(f32[2,72,1536]{2,1,0:T(8,128)} %copy-done.13) | copy-start | bytes 2654212
  114.2 2.3 %copy-start.18 = (bf16[288,1536]{1,0:T(8,128)(2,1)S(1)}, bf16[288,1536]{1,0:T(8,128)(2,1)}, u32[]{:S(2)}) copy-start(bf16[288,1536]{1,0:T(8,128)(2,1)} %copy-done.17) | copy-start | bytes 2654212
  114.2 2.3 %copy-start.24 = (bf16[288,560]{1,0:T(8,128)(2,1)S(1)}, bf16[288,560]{1,0:T(8,128)(2,1)}, u32[]{:S(2)}) copy-start(bf16[288,560]{1,0:T(8,128)(2,1)} %copy-done.23) | copy-start | bytes 967684
  116.5 5.1 %copy-start.28 = (bf16[2,72,1536]{2,1,0:T(8,128)(2,1)S(1)}, bf16[2,72,1536]{2,1,0:T(8,128)(2,1)}, u32[]{:S(2)}) copy-start(bf16[2,72,1536]{2,1,0:T(8,128)(2,1)} %copy-done.27) | copy-start | bytes 1327108
  120.2 1.3 copy-start.7
  121.5 17.9 %collective-permute-start.22 = (bf16[4,2,96,560]{3,2,1,0:T(8,128)(2,1)}, bf16[4,2,96,560]{3,2,1,0:T(8,128)(2,1)}, u32[]{:S(2)}, u32[]{:S(2)}) collective-permute-start(bf16[4,2,96,560]{3,2,1,0:T(8,128)(2,1)} %get-tuple-element.60), channel_id=1, source_target_pairs={{0,16},{16,0},{32,48},{48,32},{64,80},{80,64},{96,112},{112,96},{1... | collective-permute-start | bytes 2580488 | tf_op jit(solution)/shard_map/ppermute | solution.py:40
  121.5 13.0 %collective-permute-start.15 = (bf16[2,72,1536]{2,1,0:T(8,128)(2,1)S(1)}, bf16[2,72,1536]{2,1,0:T(8,128)(2,1)S(1)}, u32[]{:S(2)}, u32[]{:S(2)}) collective-permute-start(bf16[2,72,1536]{2,1,0:T(8,128)(2,1)S(1)} %copy-done.28), channel_id=1, source_target_pairs={{0,3},{1,0},{2,1},{3,2},{4,7},{5,4},{6,5},{7,6},{8,11},{9,8},{10,9... | collective-permute-start | bytes 1327112 | tf_op jit(solution)/shard_map/ppermute | solution.py:24
  121.8 28.6 %collective-permute-start.16 = (bf16[2,72,1536]{2,1,0:T(8,128)(2,1)}, bf16[2,72,1536]{2,1,0:T(8,128)(2,1)}, u32[]{:S(2)}, u32[]{:S(2)}) collective-permute-start(bf16[2,72,1536]{2,1,0:T(8,128)(2,1)} %get-tuple-element.45), channel_id=1, source_target_pairs={{0,1},{1,2},{2,3},{3,0},{4,5},{5,6},{6,7},{7,4},{8,9},{9,10},{10,1... | collective-permute-start | bytes 1327112 | tf_op jit(solution)/shard_map/ppermute | solution.py:24
  123.6 26.9 %collective-permute-start.17 = (bf16[2,72,1536]{2,1,0:T(8,128)(2,1)}, bf16[2,72,1536]{2,1,0:T(8,128)(2,1)}, u32[]{:S(2)}, u32[]{:S(2)}) collective-permute-start(bf16[2,72,1536]{2,1,0:T(8,128)(2,1)} %get-tuple-element.46), channel_id=1, source_target_pairs={{0,2},{1,3},{2,0},{3,1},{4,6},{5,7},{6,4},{7,5},{8,10},{9,11},{10,... | collective-permute-start | bytes 1327112 | tf_op jit(solution)/shard_map/ppermute | solution.py:24
  124.1 26.3 %collective-permute-start.23 = (bf16[72,1536]{1,0:T(8,128)(2,1)}, bf16[72,1536]{1,0:T(8,128)(2,1)S(1)}, u32[]{:S(2)}, u32[]{:S(2)}) collective-permute-start(bf16[72,1536]{1,0:T(8,128)(2,1)} %get-tuple-element.61), channel_id=1, source_target_pairs={{0,4},{1,5},{2,6},{3,7},{4,8},{5,9},{6,10},{7,11},{8,12},{9,13},{1... | collective-permute-start | bytes 663560 | tf_op jit(solution)/shard_map/ppermute | solution.py:28
  134.5 16.0 %collective-permute-start.24 = (bf16[72,1536]{1,0:T(8,128)(2,1)}, bf16[72,1536]{1,0:T(8,128)(2,1)S(1)}, u32[]{:S(2)}, u32[]{:S(2)}) collective-permute-start(bf16[72,1536]{1,0:T(8,128)(2,1)} %get-tuple-element.58.refs_3_), channel_id=1, source_target_pairs={{0,12},{1,13},{2,14},{3,15},{4,0},{5,1},{6,2},{7,3},{8,4},{9,5},{1... | collective-permute-start | bytes 663560 | tf_op jit(solution)/shard_map/ppermute | solution.py:28
  138.7 0.8 copy-start.21
  139.4 15.9 %collective-permute-start.26 = (bf16[96,1120]{1,0:T(8,128)(2,1)}, bf16[96,1120]{1,0:T(8,128)(2,1)}, u32[]{:S(2)}, u32[]{:S(2)}) collective-permute-start(bf16[96,1120]{1,0:T(8,128)(2,1)} %get-tuple-element.65), channel_id=1, source_target_pairs={{0,32},{16,48},{32,0},{48,16},{64,96},{80,112},{96,64},{112,80},{1... | collective-permute-start | bytes 645128 | tf_op jit(solution)/shard_map/ppermute | solution.py:36
  140.6 1.5 copy-start.8
  145.5 16.9 %all-to-all-start.1 = ((bf16[4,2,96,560]{3,2,1,0:T(8,128)(2,1)}), bf16[4,2,96,560]{3,2,1,0:T(8,128)(2,1)S(1)}, u32[]{:S(2)}, u32[]{:S(2)}) async-start(bf16[4,2,96,560]{3,2,1,0:T(8,128)(2,1)} %over_cores.3.refs_0_), calls=%async_computation.1 | async-start | bytes 1966080 | tf_op jit(solution)/shard_map/all_to_all | solution.py:236
  150.4 4.9 %copy-start.22 = (f32[96,1120]{1,0:T(8,128)S(1)}, f32[96,1120]{1,0:T(8,128)}, u32[]{:S(2)}) copy-start(f32[96,1120]{1,0:T(8,128)} %copy-done.21) | copy-start | bytes 1290244
  151.9 14.6 %collective-permute-start.25 = (bf16[72,1536]{1,0:T(8,128)(2,1)S(1)}, bf16[72,1536]{1,0:T(8,128)(2,1)S(1)}, u32[]{:S(2)}, u32[]{:S(2)}) collective-permute-start(bf16[72,1536]{1,0:T(8,128)(2,1)S(1)} %get-tuple-element.63), channel_id=1, source_target_pairs={{0,8},{1,9},{2,10},{3,11},{4,12},{5,13},{6,14},{7,15},{8,0},{9,1},... | collective-permute-start | bytes 663560 | tf_op jit(solution)/shard_map/ppermute | solution.py:28
  163.1 5.0 %collective-permute-start.27 = (bf16[96,560]{1,0:T(8,128)(2,1)S(1)}, bf16[96,560]{1,0:T(8,128)(2,1)S(1)}, u32[]{:S(2)}, u32[]{:S(2)}) collective-permute-start(bf16[96,560]{1,0:T(8,128)(2,1)S(1)} %get-tuple-element.67), channel_id=1, source_target_pairs={{0,32},{16,48},{32,0},{48,16},{64,96},{80,112},{96,64},{112,80},{1... | collective-permute-start | bytes 322568 | tf_op jit(solution)/shard_map/ppermute | solution.py:36

commit v3 on v2

--- a/solution.py
+++ b/solution.py
@@ -151,7 +151,7 @@
         send[0, z] = held[others, :].astype(BF16)
 
 
-def weight_grad(place, left, right, total, last, after=None):
+def weight_grad(place, left, right, total, last, *after):
     m, model = left.shape
     n = right.shape[1]
     chunk, part = model // 4, model // 16
@@ -165,9 +165,8 @@
     if total is not None:
         in_specs.append(pl.BlockSpec((chunk, n), lambda r, place: (r, 0)))
         args.append(total)
-    if after is not None:
-        in_specs.append(ANY)
-        args.append(after)
+    in_specs += [ANY] * len(after)
+    args += after
     if last:
         out_specs = [pl.BlockSpec((1, 2, part, n), lambda r, place: (r, 0, 0, 0))] * 2
         out_shape = [shape((4, 2, part, n), BF16), shape((4, 2, part, n), F32)]
@@ -241,23 +240,26 @@
     return mine + other_z_lo(others).astype(F32)
 
 
-def add_parts_body(groups, own, left, right, far, *refs):
-    for g, out in enumerate(refs[-groups:]):
+def add_parts_body(first, groups, own, left, right, far, *refs):
+    for g, out in enumerate(refs[-groups:], first):
         total = own[g] + left[g].astype(F32) + right[g].astype(F32) + far[g].astype(F32)
         out[...] = total.astype(out.dtype)
 
 
-def scatter_x(own, to_left, to_right, to_far, types, *after):
-    got = along_x(to_left, -1), along_x(to_right, 1), along_x(to_far, 2)
-    return pl.pallas_call(
-        functools.partial(add_parts_body, len(types)),
+def exchange_x(own, to_left, to_right, to_far):
+    return own, along_x(to_left, -1), along_x(to_right, 1), along_x(to_far, 2)
+
+
+def add_parts(own, left, right, far, first, types, *after):
+    return pl.pallas_call(
+        functools.partial(add_parts_body, first, len(types)),
         out_shape=[jax.ShapeDtypeStruct(own.shape[1:], kind) for kind in types],
         in_specs=[VMEM] * 4 + [ANY] * len(after),
         out_specs=[VMEM] * len(types),
         compiler_params=pltpu.CompilerParams(vmem_limit_bytes=LIMIT),
         cost_estimate=SHORT,
         name="add_parts",
-    )(own, *got, *after)
+    )(own, left, right, far, *after)
 
 
 def on_device(normed, out_grad, gate_weight, up_weight, down_weight):
@@ -285,14 +287,16 @@
     down = weight_grad(place, near[1], near[3], down[0], False)
     away = stage(away, weight, down_weight, False)
     pair = weight_grad(place, away[0], away[2], pair[0], True)
-    late = late_partials([away[2], home[2]], weight, pair[0])
-    pair = over_cores(*pair, late[0])
-    below, above = scatter_x(*near[4:], (BF16, BF16), pair)
-    down = weight_grad(place, away[1], away[3], down[0], True, below)
+    pair = over_cores(*pair)
+    late = late_partials([away[2], home[2]], weight, pair)
+    near = exchange_x(*near[4:])
+    below, above = add_parts(*near, 0, (BF16, BF16), late[0])
+    down = weight_grad(place, away[1], away[3], down[0], True, late[0], *near[1:])
+    pair = over_y(pair)
+    parts = exchange_x(*late)
+    down = over_cores(*down, pair, parts[1])
     from_below, from_above = along_z(above, 1), along_z(below, -1)
-    pair = over_y(pair)
-    down = over_cores(*down, pair)
-    far, mine = scatter_x(*late, (BF16, F32), down, from_below, from_above)
+    far, mine = add_parts(*parts, 0, (BF16, F32), down, from_below, from_above)
     down = over_y(down)
     from_far = along_z(far, 2)
     grad_input = mine + from_below.astype(F32) + from_above.astype(F32) + from_far.astype(F32)

time: 169 us -> 165 us (0.976)
  Pallas kernels: 55.4 us -> 51.9 us
  waiting for transfers between devices: 33.1 us -> 30.2 us
    pallas_call x2, Pallas kernels: 5.32 us -> 1.95 us  [over_cores(): pl.pallas_call(cores_body, grid=(4,), out_shape=jax.ShapeDtypeStruct(keep...]
    ppermute x6, waiting for transfers between devices: 11.7 us -> 9.28 us  [along_z(): lax.ppermute(value, 'tensor', [(i, (i + 4 * step) % 16) for i in range(16)])]
    unnamed x58 -> x60, local copies, waits for them, and re-layouts: 11.9 us -> 12.1 us
  transfers between devices with their start and end apart: 30 -> 30, of which waited for: 10 -> 9; matrix products, arithmetic and copies ran while one was open for 3% -> 4% of each run, Pallas kernels for 29% -> 28%
where the time goes in v3:
time: 165 us; the launch traced here: 164 us
  starting transfers between devices  60.7 us (37%)
  Pallas kernels  51.9 us (31%)
  waiting for transfers between devices  30.2 us (18%)
  local copies, waits for them, and re-layouts  12.9 us (8%)
  other arithmetic  7.05 us (4%)
    ppermute x18, starting transfers between devices, along_x(): lax.ppermute(value, 'tensor', [(i, i // 4 * 4 + (i + step) % 4) for i in...  27 us
    pallas_call x6, Pallas kernels, weight_grad(): pl.pallas_call(functools.partial(weight_body, total is not None, len(args...  24.3 us
    ppermute x6, starting transfers between devices, along_z(): lax.ppermute(value, 'tensor', [(i, (i + 4 * step) % 16) for i in range(16)])  21.5 us
    ppermute x18, waiting for transfers between devices, along_x(): lax.ppermute(value, 'tensor', [(i, i // 4 * 4 + (i + step) % 4) for i in...  14 us
    pallas_call x3, Pallas kernels, stage(): pl.pallas_call(functools.partial(stage_body, groups, send), out_shape=out...  13.8 us
    unnamed x60, local copies, waits for them, and re-layouts  12.1 us
    all_to_all x2, starting transfers between devices, over_y(): lax.all_to_all(sums, 'dp', 0, 0, axis_index_groups=groups, tiled=True)  9.95 us
    ppermute x6, waiting for transfers between devices, along_z(): lax.ppermute(value, 'tensor', [(i, (i + 4 * step) % 16) for i in range(16)])  9.28 us
  transfers between devices with their start and end apart: 30, of which 9 were waited for; matrix products, arithmetic and copies ran while one was open for 4% of the time, Pallas kernels for 28%

profile of v3, /device:TPU:8, one launch (start us, length us, event | category | flops | bytes accessed | tf_op | source)
XLA Modules:
  0.0 163.7 jit_solution(5945431095468467308)
XLA Ops:
  0.6 1.1 pad_maximum_fusion.1.refs_0_
  1.7 1.6 collective-permute-start
  3.3 3.3 %collective-permute-start.7 = (bf16[2,72,1536]{2,1,0:T(8,128)(2,1)S(1)}, bf16[2,72,1536]{2,1,0:T(8,128)(2,1)S(1)}, u32[]{:S(2)}, u32[]{:S(2)}) collective-permute-start(bf16[2,72,1536]{2,1,0:T(8,128)(2,1)S(1)} %pad_maximum_fusion.1.refs_0_), channel_id=1, source_target_pairs={{0,4},{1,5},{2,6},{3,7},{4,8},{5,9},{6,10},{7,11},{8,12},{9,13},{1... | collective-permute-start | bytes 1327112 | tf_op jit(solution)/shard_map/ppermute | solution.py:28
  6.6 3.0 %collective-permute-start.11 = (bf16[2,72,1536]{2,1,0:T(8,128)(2,1)S(1)}, bf16[2,72,1536]{2,1,0:T(8,128)(2,1)S(1)}, u32[]{:S(2)}, u32[]{:S(2)}) collective-permute-start(bf16[2,72,1536]{2,1,0:T(8,128)(2,1)S(1)} %pad_maximum_fusion.1.refs_0_), channel_id=1, source_target_pairs={{0,12},{1,13},{2,14},{3,15},{4,0},{5,1},{6,2},{7,3},{8,4},{9,5},{1... | collective-permute-start | bytes 1327112 | tf_op jit(solution)/shard_map/ppermute | solution.py:28
  9.6 1.7 %collective-permute-start.5 = (bf16[2,72,1536]{2,1,0:T(8,128)(2,1)S(1)}, bf16[2,72,1536]{2,1,0:T(8,128)(2,1)S(1)}, u32[]{:S(2)}, u32[]{:S(2)}) collective-permute-start(bf16[2,72,1536]{2,1,0:T(8,128)(2,1)S(1)} %pad_maximum_fusion.1.refs_0_), channel_id=1, source_target_pairs={{0,3},{1,0},{2,1},{3,2},{4,7},{5,4},{6,5},{7,6},{8,11},{9,8},{10,9... | collective-permute-start | bytes 1327112 | tf_op jit(solution)/shard_map/ppermute | solution.py:24
  11.3 3.6 %collective-permute-done.after.refs_1_ = bf16[2,72,1536]{2,1,0:T(8,128)(2,1)S(1)} collective-permute-done((bf16[2,72,1536]{2,1,0:T(8,128)(2,1)S(1)}, bf16[2,72,1536]{2,1,0:T(8,128)(2,1)S(1)}, u32[]{:S(2)}, u32[]{:S(2)}) %collective-permute-start) | collective-permute-done | bytes 442400 | tf_op jit(solution)/shard_map/ppermute | solution.py:24
  14.9 0.8 copy-done.12
  15.7 1.8 %pack.1 = bf16[2,72,1536]{2,1,0:T(8,128)(2,1)} custom-call(bf16[72,1536]{1,0:T(8,128)(2,1)} %rows.1, bf16[72,1536]{1,0:T(8,128)(2,1)} %grads.1, bf16[2,72,1536]{2,1,0:T(8,128)(2,1)} %copy-done.12), custom_call_target="tpu_custom_call" | custom-call | bytes 1048576 | tf_op jit(solution)/shard_map/pack/pallas_call | solution.py:48
  17.5 1.8 %collective-permute-start.6 = (bf16[2,72,1536]{2,1,0:T(8,128)(2,1)}, bf16[2,72,1536]{2,1,0:T(8,128)(2,1)S(1)}, u32[]{:S(2)}, u32[]{:S(2)}) collective-permute-start(bf16[2,72,1536]{2,1,0:T(8,128)(2,1)} %pack.1), channel_id=1, source_target_pairs={{0,2},{1,3},{2,0},{3,1},{4,6},{5,7},{6,4},{7,5},{8,10},{9,11},{10,... | collective-permute-start | bytes 1327112 | tf_op jit(solution)/shard_map/ppermute | solution.py:24
  19.4 3.5 %collective-permute-done.7.refs_0_ = bf16[2,72,1536]{2,1,0:T(8,128)(2,1)S(1)} collective-permute-done((bf16[2,72,1536]{2,1,0:T(8,128)(2,1)S(1)}, bf16[2,72,1536]{2,1,0:T(8,128)(2,1)S(1)}, u32[]{:S(2)}, u32[]{:S(2)}) %collective-permute-start.7) | collective-permute-done | bytes 442400 | tf_op jit(solution)/shard_map/ppermute | solution.py:28
  22.9 1.5 collective-permute-start.8
  24.4 5.7 %collective-permute-done.11.refs_4_ = bf16[2,72,1536]{2,1,0:T(8,128)(2,1)S(1)} collective-permute-done((bf16[2,72,1536]{2,1,0:T(8,128)(2,1)S(1)}, bf16[2,72,1536]{2,1,0:T(8,128)(2,1)S(1)}, u32[]{:S(2)}, u32[]{:S(2)}) %collective-permute-start.11) | collective-permute-done | bytes 442400 | tf_op jit(solution)/shard_map/ppermute | solution.py:28
  30.1 1.7 %collective-permute-start.13 = (bf16[2,72,1536]{2,1,0:T(8,128)(2,1)S(1)}, bf16[2,72,1536]{2,1,0:T(8,128)(2,1)S(1)}, u32[]{:S(2)}, u32[]{:S(2)}) collective-permute-start(bf16[2,72,1536]{2,1,0:T(8,128)(2,1)S(1)} %collective-permute-done.11.refs_4_), channel_id=1, source_target_pairs={{0,3},{1,0},{2,1},{3,2},{4,7},{5,4},{6,5},{7,6},{8,11},{9,8},{10,9... | collective-permute-start | bytes 1327112 | tf_op jit(solution)/shard_map/ppermute | solution.py:24
  31.9 5.0 %collective-permute-start.1 = (bf16[2,72,1536]{2,1,0:T(8,128)(2,1)}, bf16[2,72,1536]{2,1,0:T(8,128)(2,1)S(1)}, u32[]{:S(2)}, u32[]{:S(2)}) collective-permute-start(bf16[2,72,1536]{2,1,0:T(8,128)(2,1)} %pack.1), channel_id=1, source_target_pairs={{0,8},{1,9},{2,10},{3,11},{4,12},{5,13},{6,14},{7,15},{8,0},{9,1},... | collective-permute-start | bytes 1327112 | tf_op jit(solution)/shard_map/ppermute | solution.py:28
  37.2 3.0 %collective-permute-start.9 = (bf16[2,72,1536]{2,1,0:T(8,128)(2,1)S(1)}, bf16[2,72,1536]{2,1,0:T(8,128)(2,1)S(1)}, u32[]{:S(2)}, u32[]{:S(2)}) collective-permute-start(bf16[2,72,1536]{2,1,0:T(8,128)(2,1)S(1)} %collective-permute-done.7.refs_0_), channel_id=1, source_target_pairs={{0,3},{1,0},{2,1},{3,2},{4,7},{5,4},{6,5},{7,6},{8,11},{9,8},{10,9... | collective-permute-start | bytes 1327112 | tf_op jit(solution)/shard_map/ppermute | solution.py:24
  40.2 1.8 %collective-permute-start.10 = (bf16[2,72,1536]{2,1,0:T(8,128)(2,1)S(1)}, bf16[2,72,1536]{2,1,0:T(8,128)(2,1)S(1)}, u32[]{:S(2)}, u32[]{:S(2)}) collective-permute-start(bf16[2,72,1536]{2,1,0:T(8,128)(2,1)S(1)} %collective-permute-done.8.refs_1_), channel_id=1, source_target_pairs={{0,1},{1,2},{2,3},{3,0},{4,5},{5,6},{6,7},{7,4},{8,9},{9,10},{10,1... | collective-permute-start | bytes 1327112 | tf_op jit(solution)/shard_map/ppermute | solution.py:24
  42.0 1.2 collective-permute-done.13.refs_6_
  43.2 3.0 %collective-permute-start.14 = (bf16[2,72,1536]{2,1,0:T(8,128)(2,1)S(1)}, bf16[2,72,1536]{2,1,0:T(8,128)(2,1)S(1)}, u32[]{:S(2)}, u32[]{:S(2)}) collective-permute-start(bf16[2,72,1536]{2,1,0:T(8,128)(2,1)S(1)} %collective-permute-done.13.refs_6_), channel_id=1, source_target_pairs={{0,3},{1,0},{2,1},{3,2},{4,7},{5,4},{6,5},{7,6},{8,11},{9,8},{10,9... | collective-permute-start | bytes 1327112 | tf_op jit(solution)/shard_map/ppermute | solution.py:24
  46.2 2.3 %pad_maximum_fusion.refs_4_.refs_8_.refs_2_ = bf16[1120,1536]{1,0:T(8,128)(2,1)S(1)} fusion(bf16[560,1536]{1,0:T(8,128)(2,1)} %bitcast.8, bf16[560,1536]{1,0:T(8,128)(2,1)} %bitcast.9), kind=kLoop, calls=%fused_computation | loop fusion | flops 6881280 | bytes 6881280 | tf_op jit(solution)/shard_map/concatenate | solution.py:269
  48.8 2.2 %stage.4 = (bf16[288,1536]{1,0:T(8,128)(2,1)S(1)}, bf16[288,1536]{1,0:T(8,128)(2,1)S(1)}, bf16[288,1120]{1,0:T(8,128)(2,1)S(1)}, bf16[288,560]{1,0:T(8,128)(2,1)S(1)}) custom-call(bf16[2,72,1536]{2,1,0:T(8,128)(2,1)S(1)} %pad_maximum_fusion.1.refs_0_, bf16[2,72,1536]{2,1,0:T(8,128)(2,1)S(1)} %copy-done.13, ...), custom_call_target="tpu_custom_call" | custom-call | tf_op jit(solution)/shard_map/stage/pallas_call | solution.py:103
  51.0 3.5 %weight_grad.6.refs_2_ = f32[1536,1120]{1,0:T(8,128)S(1)} custom-call(s32[2]{0:T(128)S(1)} %pad_add_fusion.place, bf16[288,1536]{1,0:T(8,128)(2,1)S(1)} %get-tuple-element.41.refs_0_, bf16[288,1120]{1,0:T(8,128)(2,1)S(1)} %get-tuple-element.37.refs_1_), custom_call_target="tpu_custom_call" | custom-call | tf_op jit(solution)/shard_map/weight_grad/pallas_call | solution.py:178
  54.6 2.8 %copy-done.2 = f32[1536,1120]{1,0:T(8,128)} copy-done((f32[1536,1120]{1,0:T(8,128)}, f32[1536,1120]{1,0:T(8,128)S(1)}, u32[]{:S(2)}) %copy-start.2) | copy-done | bytes 6881304
  57.4 3.2 %collective-permute-start.3 = (bf16[2,72,1536]{2,1,0:T(8,128)(2,1)S(1)}, bf16[2,72,1536]{2,1,0:T(8,128)(2,1)S(1)}, u32[]{:S(2)}, u32[]{:S(2)}) collective-permute-start(bf16[2,72,1536]{2,1,0:T(8,128)(2,1)S(1)} %collective-permute-done.1.refs_0_), channel_id=1, source_target_pairs={{0,3},{1,0},{2,1},{3,2},{4,7},{5,4},{6,5},{7,6},{8,11},{9,8},{10,9... | collective-permute-start | bytes 1327112 | tf_op jit(solution)/shard_map/ppermute | solution.py:24
  60.6 1.6 collective-permute-done.14.refs_7_
  62.2 9.5 %stage.5 = (bf16[576,1536]{1,0:T(8,128)(2,1)S(1)}, bf16[576,1536]{1,0:T(8,128)(2,1)S(1)}, bf16[576,1120]{1,0:T(8,128)(2,1)S(1)}, bf16[576,560]{1,0:T(8,128)(2,1)...) custom-call(bf16[2,72,1536]{2,1,0:T(8,128)(2,1)S(1)} %collective-per, ...), custom_call_target="tpu_custom_call" | custom-call | flops 4954521600 | bytes 12582912 | tf_op jit(solution)/shard_map/stage/pallas_call | solution.py:103
  71.7 1.3 copy-done.14
  73.0 0.9 copy-done.16
  73.9 0.9 copy-done.22
  74.8 6.9 %weight_grad.7.refs_2_ = f32[1536,1120]{1,0:T(8,128)S(1)} custom-call(s32[2]{0:T(128)S(1)} %pad_add_fusion.place, bf16[576,1536]{1,0:T(8,128)(2,1)S(1)} %get-tuple-element.39.refs_0_, bf16[576,1120]{1,0:T(8,128)(2,1)S(1)} %get-tuple-element.40.refs_1_, f32[1536,1120]{1,0:T(8,128)} %copy-done.2), custom_call_target="tpu_custom_call" | custom-call | tf_op jit(solution)/shard_map/weight_grad/pallas_call | solution.py:178
  81.8 2.2 %stage.3 = (bf16[288,1536]{1,0:T(8,128)(2,1)S(1)}, bf16[288,1536]{1,0:T(8,128)(2,1)S(1)}, bf16[288,1120]{1,0:T(8,128)(2,1)S(1)}, bf16[288,560]{1,0:T(8,128)(2,1)S(1)}) custom-call(bf16[2,72,1536]{2,1,0:T(8,128)(2,1)S(1)} %collective-permute-done.1.refs_0_, bf16[2,72,1536]{2,1,0:T(8,128)(2,1)S(1)} %collective-permute-done.2.refs_1_, ...), custom_call_target="tpu_custom_call" | custom-call | tf_op jit(solution)/shard_map/stage/pallas_call | solution.py:103
  84.0 0.9 copy-done.20
  84.9 3.9 %weight_grad.8 = (bf16[4,2,96,1120]{3,2,1,0:T(8,128)(2,1)S(1)}, f32[4,2,96,1120]{3,2,1,0:T(8,128)S(1)}) custom-call(s32[2]{0:T(128)S(1)} %pad_add_fusion.place, bf16[288,1536]{1,0:T(8,128)(2,1)S(1)} %get-tuple-element.38.refs_0_, bf16[288,1120]{1,0:T(8,128)(2,1)S(1)} %get-tuple-element.36.refs_1_.refs_0_, f32[1536,1120]{1,0:T(8,128)S(1)} %weight_grad.7.refs_2_), custom_call_target="tpu_custom_call" | custom-call | tf_op jit(solution)/shard_map/weight_grad/pallas_call | solution.py:178
  89.0 3.0 %collective-permute-start.19 = (bf16[2,72,1536]{2,1,0:T(8,128)(2,1)}, bf16[2,72,1536]{2,1,0:T(8,128)(2,1)}, u32[]{:S(2)}, u32[]{:S(2)}) collective-permute-start(bf16[2,72,1536]{2,1,0:T(8,128)(2,1)} %get-tuple-element.54), channel_id=1, source_target_pairs={{0,3},{1,0},{2,1},{3,2},{4,7},{5,4},{6,5},{7,6},{8,11},{9,8},{10,9... | collective-permute-start | bytes 1327112 | tf_op jit(solution)/shard_map/ppermute | solution.py:24
  92.0 1.8 %collective-permute-start.21 = (bf16[2,72,1536]{2,1,0:T(8,128)(2,1)}, bf16[2,72,1536]{2,1,0:T(8,128)(2,1)}, u32[]{:S(2)}, u32[]{:S(2)}) collective-permute-start(bf16[2,72,1536]{2,1,0:T(8,128)(2,1)} %get-tuple-element.56), channel_id=1, source_target_pairs={{0,2},{1,3},{2,0},{3,1},{4,6},{5,7},{6,4},{7,5},{8,10},{9,11},{10,... | collective-permute-start | bytes 1327112 | tf_op jit(solution)/shard_map/ppermute | solution.py:24
  94.2 1.2 copy-done.3
  95.4 4.9 %all-to-all-start = ((bf16[4,2,96,1120]{3,2,1,0:T(8,128)(2,1)}), bf16[4,2,96,1120]{3,2,1,0:T(8,128)(2,1)}, u32[]{:S(2)}, u32[]{:S(2)}) async-start(bf16[4,2,96,1120]{3,2,1,0:T(8,128)(2,1)} %copy-done.3), calls=%async_computation | async-start | bytes 3538944 | tf_op jit(solution)/shard_map/all_to_all | solution.py:235
  100.3 1.2 copy-done.19
  101.5 1.0 copy-done.29
  102.5 2.7 %weight_grad.9.refs_2_ = f32[1536,560]{1,0:T(8,128)S(1)} custom-call(s32[2]{0:T(128)S(1)} %pad_add_fusion.place, bf16[288,1536]{1,0:T(8,128)(2,1)S(1)} %copy-done.19, bf16[288,560]{1,0:T(8,128)(2,1)S(1)} %copy-done.29), custom_call_target="tpu_custom_call" | custom-call | tf_op jit(solution)/shard_map/weight_grad/pallas_call | solution.py:178
  105.3 3.4 %weight_grad.10.refs_2_ = f32[1536,560]{1,0:T(8,128)S(1)} custom-call(s32[2]{0:T(128)S(1)} %pad_add_fusion.place, bf16[576,1536]{1,0:T(8,128)(2,1)S(1)} %copy-done.15, bf16[576,560]{1,0:T(8,128)(2,1)S(1)} %copy-done.23, f32[1536,560]{1,0:T(8,128)S(1)} %weight_grad.9.refs_2_), custom_call_target="tpu_custom_call" | custom-call | tf_op jit(solution)/shard_map/weight_grad/pallas_call | solution.py:178
  108.7 3.4 %late_partials.1 = (f32[2,72,1536]{2,1,0:T(8,128)S(1)}, bf16[2,72,1536]{2,1,0:T(8,128)(2,1)S(1)}, bf16[2,72,1536]{2,1,0:T(8,128)(2,1)}, bf16[2,72,1536]{2,1,0:T(8,128)(2,1)}) custom-call(bf16[288,1120]{1,0:T(8,128)(2,1)S(1)} %copy-done.11, bf16[288,1120]{1,0:T(8,128)(2,1)S(1)} %copy-done.9, bf16[1120,1536]{1,0:T(8,128)(2,1)S(1)} %copy-done.1, ...), custom_call_target="tpu_custom_call" | custom-call | tf_op jit(solution)/shard_map/late_partials/pallas_call | solution.py:124
  112.1 3.1 %collective-permute-done.20.refs_5_.right = bf16[2,72,1536]{2,1,0:T(8,128)(2,1)} collective-permute-done((bf16[2,72,1536]{2,1,0:T(8,128)(2,1)}, bf16[2,72,1536]{2,1,0:T(8,128)(2,1)}, u32[]{:S(2)}, u32[]{:S(2)}) %collective-permute-start.20) | collective-permute-done | bytes 442400 | tf_op jit(solution)/shard_map/ppermute | solution.py:24
  115.3 3.8 %weight_grad.11 = (bf16[4,2,96,560]{3,2,1,0:T(8,128)(2,1)}, f32[4,2,96,560]{3,2,1,0:T(8,128)S(1)}) custom-call(s32[2]{0:T(128)S(1)} %pad_add_fusion.place, bf16[288,1536]{1,0:T(8,128)(2,1)S(1)} %copy-done.21, bf16[288,560]{1,0:T(8,128)(2,1)S(1)} %copy-done.27, f32[1536,560]{1,0:T(8,128)S(1)} %weight_grad.10.refs_2_, ...), custom_call_target="tpu_custom_call" | custom-call | tf_op jit(solution)/shard_map/weight_grad/pallas_call | solution.py:178
  119.3 1.7 %collective-permute-start.17 = (bf16[2,72,1536]{2,1,0:T(8,128)(2,1)}, bf16[2,72,1536]{2,1,0:T(8,128)(2,1)}, u32[]{:S(2)}, u32[]{:S(2)}) collective-permute-start(bf16[2,72,1536]{2,1,0:T(8,128)(2,1)} %get-tuple-element.46), channel_id=1, source_target_pairs={{0,1},{1,2},{2,3},{3,0},{4,5},{5,6},{6,7},{7,4},{8,9},{9,10},{10,1... | collective-permute-start | bytes 1327112 | tf_op jit(solution)/shard_map/ppermute | solution.py:24
  121.1 0.6 collective-permute-start.18
  121.6 2.2 %add_parts.2 = (bf16[72,1536]{1,0:T(8,128)(2,1)}, bf16[72,1536]{1,0:T(8,128)(2,1)}) custom-call(f32[2,72,1536]{2,1,0:T(8,128)S(1)} %copy-done.17, bf16[2,72,1536]{2,1,0:T(8,128)(2,1)} %collective-permute-done.19.refs_4_.left, bf16[2,72,1536]{2,1,0:T(8,128)(2,1)} %collective-permute-done.20.refs_5_.right, ...), custom_call_target="tpu_custom_call" | custom-call | tf_op jit(solution)/shard_map/add_parts/pallas_call | solution.py:254
  123.8 3.8 %collective-permute-start.23 = (bf16[72,1536]{1,0:T(8,128)(2,1)}, bf16[72,1536]{1,0:T(8,128)(2,1)}, u32[]{:S(2)}, u32[]{:S(2)}) collective-permute-start(bf16[72,1536]{1,0:T(8,128)(2,1)} %get-tuple-element.60), channel_id=1, source_target_pairs={{0,4},{1,5},{2,6},{3,7},{4,8},{5,9},{6,10},{7,11},{8,12},{9,13},{1... | collective-permute-start | bytes 663560 | tf_op jit(solution)/shard_map/ppermute | solution.py:28
  127.6 4.4 %collective-permute-done.16.refs_1_.left = bf16[2,72,1536]{2,1,0:T(8,128)(2,1)S(1)} collective-permute-done((bf16[2,72,1536]{2,1,0:T(8,128)(2,1)S(1)}, bf16[2,72,1536]{2,1,0:T(8,128)(2,1)S(1)}, u32[]{:S(2)}, u32[]{:S(2)}) %collective-permute-start.16) | collective-permute-done | bytes 442400 | tf_op jit(solution)/shard_map/ppermute | solution.py:24
  132.0 2.6 %collective-permute-start.24 = (bf16[72,1536]{1,0:T(8,128)(2,1)}, bf16[72,1536]{1,0:T(8,128)(2,1)}, u32[]{:S(2)}, u32[]{:S(2)}) collective-permute-start(bf16[72,1536]{1,0:T(8,128)(2,1)} %get-tuple-element.61), channel_id=1, source_target_pairs={{0,12},{1,13},{2,14},{3,15},{4,0},{5,1},{6,2},{7,3},{8,4},{9,5},{1... | collective-permute-start | bytes 663560 | tf_op jit(solution)/shard_map/ppermute | solution.py:28
  134.6 2.3 %add_chunks.2 = (f32[96,1120]{1,0:T(8,128)S(1)}, bf16[96,1120]{1,0:T(8,128)(2,1)}) custom-call(s32[2]{0:T(128)S(1)} %pad_add_fusion.place, bf16[4,2,96,1120]{3,2,1,0:T(8,128)(2,1)} %all-to-all-done.refs_0_.got), custom_call_target="tpu_custom_call" | custom-call | tf_op jit(solution)/shard_map/add_chunks/pallas_call | solution.py:202
  136.9 0.8 copy-done.24
  137.6 1.0 collective-permute-start.26
  138.6 1.6 over_cores.3.refs_0_
  140.2 5.0 %all-to-all-start.1 = ((bf16[4,2,96,560]{3,2,1,0:T(8,128)(2,1)}), bf16[4,2,96,560]{3,2,1,0:T(8,128)(2,1)S(1)}, u32[]{:S(2)}, u32[]{:S(2)}) async-start(bf16[4,2,96,560]{3,2,1,0:T(8,128)(2,1)} %over_cores.3.refs_0_), calls=%async_computation.1 | async-start | bytes 1966080 | tf_op jit(solution)/shard_map/all_to_all | solution.py:235
  145.3 1.4 add_parts.3
  146.7 3.9 %collective-permute-start.25 = (bf16[72,1536]{1,0:T(8,128)(2,1)S(1)}, bf16[72,1536]{1,0:T(8,128)(2,1)S(1)}, u32[]{:S(2)}, u32[]{:S(2)}) collective-permute-start(bf16[72,1536]{1,0:T(8,128)(2,1)S(1)} %get-tuple-element.63), channel_id=1, source_target_pairs={{0,8},{1,9},{2,10},{3,11},{4,12},{5,13},{6,14},{7,15},{8,0},{9,1},... | collective-permute-start | bytes 663560 | tf_op jit(solution)/shard_map/ppermute | solution.py:28
  150.6 1.0 add_multiply_fusion
  151.6 0.8 fusion
  152.4 4.8 %all-to-all-done.1.got = bf16[4,2,96,560]{3,2,1,0:T(8,128)(2,1)S(1)} async-done(((bf16[4,2,96,560]{3,2,1,0:T(8,128)(2,1)}), bf16[4,2,96,560]{3,2,1,0:T(8,128)(2,1)S(1)}, u32[]{:S(2)}, u32[]{:S(2)}) %all-to-all-start.1) | async-done | bytes 860192 | tf_op jit(solution)/shard_map/all_to_all | solution.py:235
  157.3 0.7 add_chunks.3
  157.9 1.1 collective-permute-start.27
  159.1 1.8 %add_convert_fusion = bf16[72,1536]{1,0:T(8,128)(2,1)} fusion(bf16[72,1536]{1,0:T(8,128)(2,1)S(1)} %collective-permute-done.25, bf16[72,1536]{1,0:T(8,128)(2,1)} %collective-permute-done.24.refs_2_, f32[72,1536]{1,0:T(8,128)S(1)} %get-tuple-element.62, bf16[72,1536]{1,0:T(8,128)(2,1)} %collective-permute-done.23.refs_1_), kind=kLoop, calls=%fused_computation.3 | loop fusion | flops 774144 | bytes 1327104 | tf_op jit(solution)/shard_map/convert_element_type | solution.py:307
  160.9 2.1 %collective-permute-done.27 = bf16[96,560]{1,0:T(8,128)(2,1)S(1)} collective-permute-done((bf16[96,560]{1,0:T(8,128)(2,1)S(1)}, bf16[96,560]{1,0:T(8,128)(2,1)S(1)}, u32[]{:S(2)}, u32[]{:S(2)}) %collective-permute-start.27) | collective-permute-done | bytes 107552 | tf_op jit(solution)/shard_map/ppermute | solution.py:36
  163.0 0.7 multiply_bitcast_fusion
  (80 shorter events, 1.5 us)
Async XLA Ops:
  1.7 13.2 %collective-permute-start = (bf16[2,72,1536]{2,1,0:T(8,128)(2,1)S(1)}, bf16[2,72,1536]{2,1,0:T(8,128)(2,1)S(1)}, u32[]{:S(2)}, u32[]{:S(2)}) collective-permute-start(bf16[2,72,1536]{2,1,0:T(8,128)(2,1)S(1)} %pad_maximum_fusion.1.refs_0_), channel_id=1, source_target_pairs={{0,1},{1,2},{2,3},{3,0},{4,5},{5,6},{6,7},{7,4},{8,9},{9,10},{10,1... | collective-permute-start | bytes 1327112 | tf_op jit(solution)/shard_map/ppermute | solution.py:24
  3.3 19.6 %collective-permute-start.7 = (bf16[2,72,1536]{2,1,0:T(8,128)(2,1)S(1)}, bf16[2,72,1536]{2,1,0:T(8,128)(2,1)S(1)}, u32[]{:S(2)}, u32[]{:S(2)}) collective-permute-start(bf16[2,72,1536]{2,1,0:T(8,128)(2,1)S(1)} %pad_maximum_fusion.1.refs_0_), channel_id=1, source_target_pairs={{0,4},{1,5},{2,6},{3,7},{4,8},{5,9},{6,10},{7,11},{8,12},{9,13},{1... | collective-permute-start | bytes 1327112 | tf_op jit(solution)/shard_map/ppermute | solution.py:28
  6.6 23.6 %collective-permute-start.11 = (bf16[2,72,1536]{2,1,0:T(8,128)(2,1)S(1)}, bf16[2,72,1536]{2,1,0:T(8,128)(2,1)S(1)}, u32[]{:S(2)}, u32[]{:S(2)}) collective-permute-start(bf16[2,72,1536]{2,1,0:T(8,128)(2,1)S(1)} %pad_maximum_fusion.1.refs_0_), channel_id=1, source_target_pairs={{0,12},{1,13},{2,14},{3,15},{4,0},{5,1},{6,2},{7,3},{8,4},{9,5},{1... | collective-permute-start | bytes 1327112 | tf_op jit(solution)/shard_map/ppermute | solution.py:28
  9.6 27.3 %collective-permute-start.5 = (bf16[2,72,1536]{2,1,0:T(8,128)(2,1)S(1)}, bf16[2,72,1536]{2,1,0:T(8,128)(2,1)S(1)}, u32[]{:S(2)}, u32[]{:S(2)}) collective-permute-start(bf16[2,72,1536]{2,1,0:T(8,128)(2,1)S(1)} %pad_maximum_fusion.1.refs_0_), channel_id=1, source_target_pairs={{0,3},{1,0},{2,1},{3,2},{4,7},{5,4},{6,5},{7,6},{8,11},{9,8},{10,9... | collective-permute-start | bytes 1327112 | tf_op jit(solution)/shard_map/ppermute | solution.py:24
  14.9 0.8 copy-start.12
  17.5 19.7 %collective-permute-start.6 = (bf16[2,72,1536]{2,1,0:T(8,128)(2,1)}, bf16[2,72,1536]{2,1,0:T(8,128)(2,1)S(1)}, u32[]{:S(2)}, u32[]{:S(2)}) collective-permute-start(bf16[2,72,1536]{2,1,0:T(8,128)(2,1)} %pack.1), channel_id=1, source_target_pairs={{0,2},{1,3},{2,0},{3,1},{4,6},{5,7},{6,4},{7,5},{8,10},{9,11},{10,... | collective-permute-start | bytes 1327112 | tf_op jit(solution)/shard_map/ppermute | solution.py:24
  22.9 17.3 %collective-permute-start.8 = (bf16[2,72,1536]{2,1,0:T(8,128)(2,1)S(1)}, bf16[2,72,1536]{2,1,0:T(8,128)(2,1)S(1)}, u32[]{:S(2)}, u32[]{:S(2)}) collective-permute-start(bf16[2,72,1536]{2,1,0:T(8,128)(2,1)S(1)} %collective-permute-done.7.refs_0_), channel_id=1, source_target_pairs={{0,1},{1,2},{2,3},{3,0},{4,5},{5,6},{6,7},{7,4},{8,9},{9,10},{10,1... | collective-permute-start | bytes 1327112 | tf_op jit(solution)/shard_map/ppermute | solution.py:24
  30.1 13.1 %collective-permute-start.13 = (bf16[2,72,1536]{2,1,0:T(8,128)(2,1)S(1)}, bf16[2,72,1536]{2,1,0:T(8,128)(2,1)S(1)}, u32[]{:S(2)}, u32[]{:S(2)}) collective-permute-start(bf16[2,72,1536]{2,1,0:T(8,128)(2,1)S(1)} %collective-permute-done.11.refs_4_), channel_id=1, source_target_pairs={{0,3},{1,0},{2,1},{3,2},{4,7},{5,4},{6,5},{7,6},{8,11},{9,8},{10,9... | collective-permute-start | bytes 1327112 | tf_op jit(solution)/shard_map/ppermute | solution.py:24
  31.9 25.4 %collective-permute-start.1 = (bf16[2,72,1536]{2,1,0:T(8,128)(2,1)}, bf16[2,72,1536]{2,1,0:T(8,128)(2,1)S(1)}, u32[]{:S(2)}, u32[]{:S(2)}) collective-permute-start(bf16[2,72,1536]{2,1,0:T(8,128)(2,1)} %pack.1), channel_id=1, source_target_pairs={{0,8},{1,9},{2,10},{3,11},{4,12},{5,13},{6,14},{7,15},{8,0},{9,1},... | collective-permute-start | bytes 1327112 | tf_op jit(solution)/shard_map/ppermute | solution.py:28
  36.9 20.4 %collective-permute-start.12 = (bf16[2,72,1536]{2,1,0:T(8,128)(2,1)S(1)}, bf16[2,72,1536]{2,1,0:T(8,128)(2,1)S(1)}, u32[]{:S(2)}, u32[]{:S(2)}) collective-permute-start(bf16[2,72,1536]{2,1,0:T(8,128)(2,1)S(1)} %collective-permute-done.11.refs_4_), channel_id=1, source_target_pairs={{0,1},{1,2},{2,3},{3,0},{4,5},{5,6},{6,7},{7,4},{8,9},{9,10},{10,1... | collective-permute-start | bytes 1327112 | tf_op jit(solution)/shard_map/ppermute | solution.py:24
  37.2 23.4 %collective-permute-start.9 = (bf16[2,72,1536]{2,1,0:T(8,128)(2,1)S(1)}, bf16[2,72,1536]{2,1,0:T(8,128)(2,1)S(1)}, u32[]{:S(2)}, u32[]{:S(2)}) collective-permute-start(bf16[2,72,1536]{2,1,0:T(8,128)(2,1)S(1)} %collective-permute-done.7.refs_0_), channel_id=1, source_target_pairs={{0,3},{1,0},{2,1},{3,2},{4,7},{5,4},{6,5},{7,6},{8,11},{9,8},{10,9... | collective-permute-start | bytes 1327112 | tf_op jit(solution)/shard_map/ppermute | solution.py:24
  40.2 20.4 %collective-permute-start.10 = (bf16[2,72,1536]{2,1,0:T(8,128)(2,1)S(1)}, bf16[2,72,1536]{2,1,0:T(8,128)(2,1)S(1)}, u32[]{:S(2)}, u32[]{:S(2)}) collective-permute-start(bf16[2,72,1536]{2,1,0:T(8,128)(2,1)S(1)} %collective-permute-done.8.refs_1_), channel_id=1, source_target_pairs={{0,1},{1,2},{2,3},{3,0},{4,5},{5,6},{6,7},{7,4},{8,9},{9,10},{10,1... | collective-permute-start | bytes 1327112 | tf_op jit(solution)/shard_map/ppermute | solution.py:24
  43.2 19.0 %collective-permute-start.14 = (bf16[2,72,1536]{2,1,0:T(8,128)(2,1)S(1)}, bf16[2,72,1536]{2,1,0:T(8,128)(2,1)S(1)}, u32[]{:S(2)}, u32[]{:S(2)}) collective-permute-start(bf16[2,72,1536]{2,1,0:T(8,128)(2,1)S(1)} %collective-permute-done.13.refs_6_), channel_id=1, source_target_pairs={{0,3},{1,0},{2,1},{3,2},{4,7},{5,4},{6,5},{7,6},{8,11},{9,8},{10,9... | collective-permute-start | bytes 1327112 | tf_op jit(solution)/shard_map/ppermute | solution.py:24
  46.2 2.5 %copy-start.7 = (bf16[560,1536]{1,0:T(8,128)(2,1)S(1)}, bf16[560,1536]{1,0:T(8,128)(2,1)}, u32[]{:S(2)}) copy-start(bf16[560,1536]{1,0:T(8,128)(2,1)} %refs_9_.1) | copy-start | bytes 5160964
  46.2 2.6 %copy-start.13 = (bf16[2,72,1536]{2,1,0:T(8,128)(2,1)S(1)}, bf16[2,72,1536]{2,1,0:T(8,128)(2,1)}, u32[]{:S(2)}) copy-start(bf16[2,72,1536]{2,1,0:T(8,128)(2,1)} %copy-done.12) | copy-start | bytes 1327108
  48.7 2.2 %copy-start = (bf16[1120,1536]{1,0:T(8,128)(2,1)}, bf16[1120,1536]{1,0:T(8,128)(2,1)S(1)}, u32[]{:S(2)}) copy-start(bf16[1120,1536]{1,0:T(8,128)(2,1)S(1)} %pad_maximum_fusion.refs_4_.refs_8_.refs_2_) | copy-start | bytes 10321924
  50.9 3.6 %copy-start.8 = (bf16[288,1120]{1,0:T(8,128)(2,1)}, bf16[288,1120]{1,0:T(8,128)(2,1)S(1)}, u32[]{:S(2)}) copy-start(bf16[288,1120]{1,0:T(8,128)(2,1)S(1)} %get-tuple-element.37.refs_1_) | copy-start | bytes 1935364
  51.0 3.6 %copy-start.18 = (bf16[288,1536]{1,0:T(8,128)(2,1)}, bf16[288,1536]{1,0:T(8,128)(2,1)S(1)}, u32[]{:S(2)}) copy-start(bf16[288,1536]{1,0:T(8,128)(2,1)S(1)} %get-tuple-element.52.refs_0_) | copy-start | bytes 2654212
  51.0 3.6 %copy-start.28 = (bf16[288,560]{1,0:T(8,128)(2,1)}, bf16[288,560]{1,0:T(8,128)(2,1)S(1)}, u32[]{:S(2)}) copy-start(bf16[288,560]{1,0:T(8,128)(2,1)S(1)} %get-tuple-element.53.refs_1_) | copy-start | bytes 967684
  54.6 2.8 %copy-start.2 = (f32[1536,1120]{1,0:T(8,128)}, f32[1536,1120]{1,0:T(8,128)S(1)}, u32[]{:S(2)}) copy-start(f32[1536,1120]{1,0:T(8,128)S(1)} %weight_grad.6.refs_2_) | copy-start | bytes 20643844
  57.4 24.4 %collective-permute-start.2 = (bf16[2,72,1536]{2,1,0:T(8,128)(2,1)S(1)}, bf16[2,72,1536]{2,1,0:T(8,128)(2,1)S(1)}, u32[]{:S(2)}, u32[]{:S(2)}) collective-permute-start(bf16[2,72,1536]{2,1,0:T(8,128)(2,1)S(1)} %collective-permute-done.1.refs_0_), channel_id=1, source_target_pairs={{0,1},{1,2},{2,3},{3,0},{4,5},{5,6},{6,7},{7,4},{8,9},{9,10},{10,1... | collective-permute-start | bytes 1327112 | tf_op jit(solution)/shard_map/ppermute | solution.py:24
  57.4 24.4 %collective-permute-start.3 = (bf16[2,72,1536]{2,1,0:T(8,128)(2,1)S(1)}, bf16[2,72,1536]{2,1,0:T(8,128)(2,1)S(1)}, u32[]{:S(2)}, u32[]{:S(2)}) collective-permute-start(bf16[2,72,1536]{2,1,0:T(8,128)(2,1)S(1)} %collective-permute-done.1.refs_0_), channel_id=1, source_target_pairs={{0,3},{1,0},{2,1},{3,2},{4,7},{5,4},{6,5},{7,6},{8,11},{9,8},{10,9... | collective-permute-start | bytes 1327112 | tf_op jit(solution)/shard_map/ppermute | solution.py:24
  60.6 21.2 %collective-permute-start.4 = (bf16[2,72,1536]{2,1,0:T(8,128)(2,1)S(1)}, bf16[2,72,1536]{2,1,0:T(8,128)(2,1)S(1)}, u32[]{:S(2)}, u32[]{:S(2)}) collective-permute-start(bf16[2,72,1536]{2,1,0:T(8,128)(2,1)S(1)} %collective-permute-done.1.refs_0_), channel_id=1, source_target_pairs={{0,2},{1,3},{2,0},{3,1},{4,6},{5,7},{6,4},{7,5},{8,10},{9,11},{10,... | collective-permute-start | bytes 1327112 | tf_op jit(solution)/shard_map/ppermute | solution.py:24
  71.7 1.3 copy-start.14
  73.0 0.9 copy-start.16
  73.9 0.9 copy-start.22
  74.8 7.0 %copy-start.1 = (bf16[1120,1536]{1,0:T(8,128)(2,1)S(1)}, bf16[1120,1536]{1,0:T(8,128)(2,1)}, u32[]{:S(2)}) copy-start(bf16[1120,1536]{1,0:T(8,128)(2,1)} %copy-done) | copy-start | bytes 10321924
  84.0 0.9 copy-start.20
  84.9 4.0 %copy-start.10 = (bf16[288,1120]{1,0:T(8,128)(2,1)}, bf16[288,1120]{1,0:T(8,128)(2,1)S(1)}, u32[]{:S(2)}) copy-start(bf16[288,1120]{1,0:T(8,128)(2,1)S(1)} %get-tuple-element.36.refs_1_.refs_0_) | copy-start | bytes 1935364
  84.9 4.0 %copy-start.26 = (bf16[288,560]{1,0:T(8,128)(2,1)}, bf16[288,560]{1,0:T(8,128)(2,1)S(1)}, u32[]{:S(2)}) copy-start(bf16[288,560]{1,0:T(8,128)(2,1)S(1)} %get-tuple-element.49.refs_1_) | copy-start | bytes 967684
  88.9 4.9 %collective-permute-start.15 = (bf16[4,2,96,1120]{3,2,1,0:T(8,128)(2,1)S(1)}, bf16[4,2,96,1120]{3,2,1,0:T(8,128)(2,1)S(1)}, u32[]{:S(2)}, u32[]{:S(2)}) collective-permute-start(bf16[4,2,96,1120]{3,2,1,0:T(8,128)(2,1)S(1)} %get-tuple-element.43), channel_id=1, source_target_pairs={{0,16},{16,0},{32,48},{48,32},{64,80},{80,64},{96,112},{112,96},{1... | collective-permute-start | bytes 5160968 | tf_op jit(solution)/shard_map/ppermute | solution.py:40
  89.0 23.1 %collective-permute-start.19 = (bf16[2,72,1536]{2,1,0:T(8,128)(2,1)}, bf16[2,72,1536]{2,1,0:T(8,128)(2,1)}, u32[]{:S(2)}, u32[]{:S(2)}) collective-permute-start(bf16[2,72,1536]{2,1,0:T(8,128)(2,1)} %get-tuple-element.54), channel_id=1, source_target_pairs={{0,3},{1,0},{2,1},{3,2},{4,7},{5,4},{6,5},{7,6},{8,11},{9,8},{10,9... | collective-permute-start | bytes 1327112 | tf_op jit(solution)/shard_map/ppermute | solution.py:24
  92.0 23.2 %collective-permute-start.20 = (bf16[2,72,1536]{2,1,0:T(8,128)(2,1)}, bf16[2,72,1536]{2,1,0:T(8,128)(2,1)}, u32[]{:S(2)}, u32[]{:S(2)}) collective-permute-start(bf16[2,72,1536]{2,1,0:T(8,128)(2,1)} %get-tuple-element.55), channel_id=1, source_target_pairs={{0,1},{1,2},{2,3},{3,0},{4,5},{5,6},{6,7},{7,4},{8,9},{9,10},{10,1... | collective-permute-start | bytes 1327112 | tf_op jit(solution)/shard_map/ppermute | solution.py:24
  92.0 23.2 %collective-permute-start.21 = (bf16[2,72,1536]{2,1,0:T(8,128)(2,1)}, bf16[2,72,1536]{2,1,0:T(8,128)(2,1)}, u32[]{:S(2)}, u32[]{:S(2)}) collective-permute-start(bf16[2,72,1536]{2,1,0:T(8,128)(2,1)} %get-tuple-element.56), channel_id=1, source_target_pairs={{0,2},{1,3},{2,0},{3,1},{4,6},{5,7},{6,4},{7,5},{8,10},{9,11},{10,... | collective-permute-start | bytes 1327112 | tf_op jit(solution)/shard_map/ppermute | solution.py:24
  94.2 1.2 copy-start.3
  95.4 39.2 %all-to-all-start = ((bf16[4,2,96,1120]{3,2,1,0:T(8,128)(2,1)}), bf16[4,2,96,1120]{3,2,1,0:T(8,128)(2,1)}, u32[]{:S(2)}, u32[]{:S(2)}) async-start(bf16[4,2,96,1120]{3,2,1,0:T(8,128)(2,1)} %copy-done.3), calls=%async_computation | async-start | bytes 3538944 | tf_op jit(solution)/shard_map/all_to_all | solution.py:235
  100.3 1.2 copy-start.19
  101.5 1.0 copy-start.29
  102.5 2.7 %copy-start.15 = (bf16[576,1536]{1,0:T(8,128)(2,1)S(1)}, bf16[576,1536]{1,0:T(8,128)(2,1)}, u32[]{:S(2)}) copy-start(bf16[576,1536]{1,0:T(8,128)(2,1)} %copy-done.14) | copy-start | bytes 5308420
  102.5 2.7 %copy-start.23 = (bf16[576,560]{1,0:T(8,128)(2,1)S(1)}, bf16[576,560]{1,0:T(8,128)(2,1)}, u32[]{:S(2)}) copy-start(bf16[576,560]{1,0:T(8,128)(2,1)} %copy-done.22) | copy-start | bytes 1935364
  105.2 3.4 %copy-start.4 = (bf16[4,2,96,1120]{3,2,1,0:T(8,128)(2,1)S(1)}, bf16[4,2,96,1120]{3,2,1,0:T(8,128)(2,1)}, u32[]{:S(2)}) copy-start(bf16[4,2,96,1120]{3,2,1,0:T(8,128)(2,1)} %copy-done.3) | copy-start | bytes 5160964
  105.2 3.4 %copy-start.9 = (bf16[288,1120]{1,0:T(8,128)(2,1)S(1)}, bf16[288,1120]{1,0:T(8,128)(2,1)}, u32[]{:S(2)}) copy-start(bf16[288,1120]{1,0:T(8,128)(2,1)} %copy-done.8) | copy-start | bytes 1935364
  105.2 3.4 %copy-start.11 = (bf16[288,1120]{1,0:T(8,128)(2,1)S(1)}, bf16[288,1120]{1,0:T(8,128)(2,1)}, u32[]{:S(2)}) copy-start(bf16[288,1120]{1,0:T(8,128)(2,1)} %copy-done.10) | copy-start | bytes 1935364
  108.7 6.6 %copy-start.21 = (bf16[288,1536]{1,0:T(8,128)(2,1)S(1)}, bf16[288,1536]{1,0:T(8,128)(2,1)}, u32[]{:S(2)}) copy-start(bf16[288,1536]{1,0:T(8,128)(2,1)} %copy-done.20) | copy-start | bytes 2654212
  108.7 6.6 %copy-start.27 = (bf16[288,560]{1,0:T(8,128)(2,1)S(1)}, bf16[288,560]{1,0:T(8,128)(2,1)}, u32[]{:S(2)}) copy-start(bf16[288,560]{1,0:T(8,128)(2,1)} %copy-done.26) | copy-start | bytes 967684
  112.1 9.5 %copy-start.5 = (f32[2,72,1536]{2,1,0:T(8,128)}, f32[2,72,1536]{2,1,0:T(8,128)S(1)}, u32[]{:S(2)}) copy-start(f32[2,72,1536]{2,1,0:T(8,128)S(1)} %get-tuple-element.44.refs_3_.refs_0_.own) | copy-start | bytes 2654212
  115.3 6.4 %copy-start.17 = (f32[2,72,1536]{2,1,0:T(8,128)S(1)}, f32[2,72,1536]{2,1,0:T(8,128)}, u32[]{:S(2)}) copy-start(f32[2,72,1536]{2,1,0:T(8,128)} %copy-done.16) | copy-start | bytes 2654212
  119.0 18.6 %collective-permute-start.22 = (bf16[4,2,96,560]{3,2,1,0:T(8,128)(2,1)}, bf16[4,2,96,560]{3,2,1,0:T(8,128)(2,1)S(1)}, u32[]{:S(2)}, u32[]{:S(2)}) collective-permute-start(bf16[4,2,96,560]{3,2,1,0:T(8,128)(2,1)} %get-tuple-element.58), channel_id=1, source_target_pairs={{0,16},{16,0},{32,48},{48,32},{64,80},{80,64},{96,112},{112,96},{1... | collective-permute-start | bytes 2580488 | tf_op jit(solution)/shard_map/ppermute | solution.py:40
  119.0 13.0 %collective-permute-start.16 = (bf16[2,72,1536]{2,1,0:T(8,128)(2,1)S(1)}, bf16[2,72,1536]{2,1,0:T(8,128)(2,1)S(1)}, u32[]{:S(2)}, u32[]{:S(2)}) collective-permute-start(bf16[2,72,1536]{2,1,0:T(8,128)(2,1)S(1)} %get-tuple-element.45), channel_id=1, source_target_pairs={{0,3},{1,0},{2,1},{3,2},{4,7},{5,4},{6,5},{7,6},{8,11},{9,8},{10,9... | collective-permute-start | bytes 1327112 | tf_op jit(solution)/shard_map/ppermute | solution.py:24
  119.3 26.0 %collective-permute-start.17 = (bf16[2,72,1536]{2,1,0:T(8,128)(2,1)}, bf16[2,72,1536]{2,1,0:T(8,128)(2,1)}, u32[]{:S(2)}, u32[]{:S(2)}) collective-permute-start(bf16[2,72,1536]{2,1,0:T(8,128)(2,1)} %get-tuple-element.46), channel_id=1, source_target_pairs={{0,1},{1,2},{2,3},{3,0},{4,5},{5,6},{6,7},{7,4},{8,9},{9,10},{10,1... | collective-permute-start | bytes 1327112 | tf_op jit(solution)/shard_map/ppermute | solution.py:24
  121.1 24.2 %collective-permute-start.18 = (bf16[2,72,1536]{2,1,0:T(8,128)(2,1)}, bf16[2,72,1536]{2,1,0:T(8,128)(2,1)}, u32[]{:S(2)}, u32[]{:S(2)}) collective-permute-start(bf16[2,72,1536]{2,1,0:T(8,128)(2,1)} %get-tuple-element.47), channel_id=1, source_target_pairs={{0,2},{1,3},{2,0},{3,1},{4,6},{5,7},{6,4},{7,5},{8,10},{9,11},{10,... | collective-permute-start | bytes 1327112 | tf_op jit(solution)/shard_map/ppermute | solution.py:24
  123.8 21.5 %collective-permute-start.23 = (bf16[72,1536]{1,0:T(8,128)(2,1)}, bf16[72,1536]{1,0:T(8,128)(2,1)}, u32[]{:S(2)}, u32[]{:S(2)}) collective-permute-start(bf16[72,1536]{1,0:T(8,128)(2,1)} %get-tuple-element.60), channel_id=1, source_target_pairs={{0,4},{1,5},{2,6},{3,7},{4,8},{5,9},{6,10},{7,11},{8,12},{9,13},{1... | collective-permute-start | bytes 663560 | tf_op jit(solution)/shard_map/ppermute | solution.py:28
  132.0 13.3 %collective-permute-start.24 = (bf16[72,1536]{1,0:T(8,128)(2,1)}, bf16[72,1536]{1,0:T(8,128)(2,1)}, u32[]{:S(2)}, u32[]{:S(2)}) collective-permute-start(bf16[72,1536]{1,0:T(8,128)(2,1)} %get-tuple-element.61), channel_id=1, source_target_pairs={{0,12},{1,13},{2,14},{3,15},{4,0},{5,1},{6,2},{7,3},{8,4},{9,5},{1... | collective-permute-start | bytes 663560 | tf_op jit(solution)/shard_map/ppermute | solution.py:28
  136.9 0.8 copy-start.24
  137.6 13.0 %collective-permute-start.26 = (bf16[96,1120]{1,0:T(8,128)(2,1)}, bf16[96,1120]{1,0:T(8,128)(2,1)}, u32[]{:S(2)}, u32[]{:S(2)}) collective-permute-start(bf16[96,1120]{1,0:T(8,128)(2,1)} %get-tuple-element.65), channel_id=1, source_target_pairs={{0,32},{16,48},{32,0},{48,16},{64,96},{80,112},{96,64},{112,80},{1... | collective-permute-start | bytes 645128 | tf_op jit(solution)/shard_map/ppermute | solution.py:36
  140.2 5.1 %copy-start.6 = (f32[2,72,1536]{2,1,0:T(8,128)S(1)}, f32[2,72,1536]{2,1,0:T(8,128)}, u32[]{:S(2)}) copy-start(f32[2,72,1536]{2,1,0:T(8,128)} %copy-done.5) | copy-start | bytes 2654212
  140.2 17.0 %all-to-all-start.1 = ((bf16[4,2,96,560]{3,2,1,0:T(8,128)(2,1)}), bf16[4,2,96,560]{3,2,1,0:T(8,128)(2,1)S(1)}, u32[]{:S(2)}, u32[]{:S(2)}) async-start(bf16[4,2,96,560]{3,2,1,0:T(8,128)(2,1)} %over_cores.3.refs_0_), calls=%async_computation.1 | async-start | bytes 1966080 | tf_op jit(solution)/shard_map/all_to_all | solution.py:235
  145.3 5.3 %copy-start.25 = (f32[96,1120]{1,0:T(8,128)S(1)}, f32[96,1120]{1,0:T(8,128)}, u32[]{:S(2)}) copy-start(f32[96,1120]{1,0:T(8,128)} %copy-done.24) | copy-start | bytes 1290244
  146.7 12.3 %collective-permute-start.25 = (bf16[72,1536]{1,0:T(8,128)(2,1)S(1)}, bf16[72,1536]{1,0:T(8,128)(2,1)S(1)}, u32[]{:S(2)}, u32[]{:S(2)}) collective-permute-start(bf16[72,1536]{1,0:T(8,128)(2,1)S(1)} %get-tuple-element.63), channel_id=1, source_target_pairs={{0,8},{1,9},{2,10},{3,11},{4,12},{5,13},{6,14},{7,15},{8,0},{9,1},... | collective-permute-start | bytes 663560 | tf_op jit(solution)/shard_map/ppermute | solution.py:28
  157.9 5.1 %collective-permute-start.27 = (bf16[96,560]{1,0:T(8,128)(2,1)S(1)}, bf16[96,560]{1,0:T(8,128)(2,1)S(1)}, u32[]{:S(2)}, u32[]{:S(2)}) collective-permute-start(bf16[96,560]{1,0:T(8,128)(2,1)S(1)} %get-tuple-element.67), channel_id=1, source_target_pairs={{0,32},{16,48},{32,0},{48,16},{64,96},{80,112},{96,64},{112,80},{1... | collective-permute-start | bytes 322568 | tf_op jit(solution)/shard_map/ppermute | solution.py:36

commit v4 on v3

--- a/solution.py
+++ b/solution.py
@@ -290,13 +290,13 @@
     pair = over_cores(*pair)
     late = late_partials([away[2], home[2]], weight, pair)
     near = exchange_x(*near[4:])
-    below, above = add_parts(*near, 0, (BF16, BF16), late[0])
     down = weight_grad(place, away[1], away[3], down[0], True, late[0], *near[1:])
     pair = over_y(pair)
     parts = exchange_x(*late)
     down = over_cores(*down, pair, parts[1])
+    below, above = add_parts(*near, 0, (BF16, BF16), down)
     from_below, from_above = along_z(above, 1), along_z(below, -1)
-    far, mine = add_parts(*parts, 0, (BF16, F32), down, from_below, from_above)
+    far, mine = add_parts(*parts, 0, (BF16, F32), below)
     down = over_y(down)
     from_far = along_z(far, 2)
     grad_input = mine + from_below.astype(F32) + from_above.astype(F32) + from_far.astype(F32)

time: 165 us -> 182 us (1.10)
  waiting for transfers between devices: 30.2 us -> 52.8 us
  starting transfers between devices: 60.7 us -> 56.5 us
  local copies, waits for them, and re-layouts: 12.9 us -> 16.5 us
  Pallas kernels: 51.9 us -> 48.9 us
    ppermute x6, waiting for transfers between devices: 9.28 us -> 26.3 us  [along_z(): lax.ppermute(value, 'tensor', [(i, (i + 4 * step) % 16) for i in range(16)])]
    ppermute x18, waiting for transfers between devices: 14 us -> 22.7 us  [along_x(): lax.ppermute(value, 'tensor', [(i, i // 4 * 4 + (i + step) % 4) for i in...]
    all_to_all x2, waiting for transfers between devices: 4.83 us -> 0.18 us  [over_y(): lax.all_to_all(sums, 'dp', 0, 0, axis_index_groups=groups, tiled=True)]
    ppermute x2, waiting for transfers between devices: 0.01 us -> 3.68 us  [other_core(): return lax.ppermute(value, 'dp', [(i, i ^ 1) for i in range(16)])]
    unnamed x60 -> x78, local copies, waits for them, and re-layouts: 12.1 us -> 15.7 us
    ppermute x6, starting transfers between devices: 21.5 us -> 18.8 us  [along_z(): lax.ppermute(value, 'tensor', [(i, (i + 4 * step) % 16) for i in range(16)])]
    ppermute x2, waiting for transfers between devices: 2.09 us -> 0.01 us  [other_z_lo(): return lax.ppermute(value, 'dp', [(i, i ^ 2) for i in range(16)])]
    pallas_call x2, Pallas kernels: 3.57 us -> 1.58 us  [add_parts(): pl.pallas_call(functools.partial(add_parts_body, first, len(types)), out_...]
  transfers between devices with their start and end apart: 30 -> 30, of which waited for: 9 -> 12; matrix products, arithmetic and copies ran while one was open for 4% -> 3% of each run, Pallas kernels for 28% -> 23%
where the time goes in v4:
time: 182 us
  starting transfers between devices  56.5 us (31%)
  waiting for transfers between devices  52.8 us (29%)
  Pallas kernels  48.9 us (27%)
  local copies, waits for them, and re-layouts  16.5 us (9%)
  other arithmetic  6.02 us (3%)
    ppermute x18, starting transfers between devices, along_x(): lax.ppermute(value, 'tensor', [(i, i // 4 * 4 + (i + step) % 4) for i in...  27 us
    ppermute x6, waiting for transfers between devices, along_z(): lax.ppermute(value, 'tensor', [(i, (i + 4 * step) % 16) for i in range(16)])  26.3 us
    pallas_call x6, Pallas kernels, weight_grad(): pl.pallas_call(functools.partial(weight_body, total is not None, len(args...  24.3 us
    ppermute x18, waiting for transfers between devices, along_x(): lax.ppermute(value, 'tensor', [(i, i // 4 * 4 + (i + step) % 4) for i in...  22.7 us
    ppermute x6, starting transfers between devices, along_z(): lax.ppermute(value, 'tensor', [(i, (i + 4 * step) % 16) for i in range(16)])  18.8 us
    unnamed x78, local copies, waits for them, and re-layouts  15.7 us
    pallas_call x3, Pallas kernels, stage(): pl.pallas_call(functools.partial(stage_body, groups, send), out_shape=out...  12.8 us
    all_to_all x2, starting transfers between devices, over_y(): lax.all_to_all(sums, 'dp', 0, 0, axis_index_groups=groups, tiled=True)  9.88 us
  transfers between devices with their start and end apart: 30, of which 12 were waited for; matrix products, arithmetic and copies ran while one was open for 3% of the time, Pallas kernels for 23%

profile of v4, /device:TPU:8, one launch (start us, length us, event | category | flops | bytes accessed | tf_op | source)
XLA Modules:
  0.0 181.9 jit_solution(9455914083263948344)
XLA Ops:
  0.6 1.1 pad_maximum_fusion.1.refs_0_
  1.7 1.6 collective-permute-start
  3.3 3.3 %collective-permute-start.7 = (bf16[2,72,1536]{2,1,0:T(8,128)(2,1)S(1)}, bf16[2,72,1536]{2,1,0:T(8,128)(2,1)S(1)}, u32[]{:S(2)}, u32[]{:S(2)}) collective-permute-start(bf16[2,72,1536]{2,1,0:T(8,128)(2,1)S(1)} %pad_maximum_fusion.1.refs_0_), channel_id=1, source_target_pairs={{0,4},{1,5},{2,6},{3,7},{4,8},{5,9},{6,10},{7,11},{8,12},{9,13},{1... | collective-permute-start | bytes 1327112 | tf_op jit(solution)/shard_map/ppermute | solution.py:28
  6.6 3.0 %collective-permute-start.11 = (bf16[2,72,1536]{2,1,0:T(8,128)(2,1)S(1)}, bf16[2,72,1536]{2,1,0:T(8,128)(2,1)S(1)}, u32[]{:S(2)}, u32[]{:S(2)}) collective-permute-start(bf16[2,72,1536]{2,1,0:T(8,128)(2,1)S(1)} %pad_maximum_fusion.1.refs_0_), channel_id=1, source_target_pairs={{0,12},{1,13},{2,14},{3,15},{4,0},{5,1},{6,2},{7,3},{8,4},{9,5},{1... | collective-permute-start | bytes 1327112 | tf_op jit(solution)/shard_map/ppermute | solution.py:28
  9.6 1.7 collective-permute-start.5
  11.3 3.6 %collective-permute-done.after.refs_1_ = bf16[2,72,1536]{2,1,0:T(8,128)(2,1)S(1)} collective-permute-done((bf16[2,72,1536]{2,1,0:T(8,128)(2,1)S(1)}, bf16[2,72,1536]{2,1,0:T(8,128)(2,1)S(1)}, u32[]{:S(2)}, u32[]{:S(2)}) %collective-permute-start) | collective-permute-done | bytes 442400 | tf_op jit(solution)/shard_map/ppermute | solution.py:24
  14.9 0.8 copy-done.18
  15.7 1.8 %pack.1 = bf16[2,72,1536]{2,1,0:T(8,128)(2,1)} custom-call(bf16[72,1536]{1,0:T(8,128)(2,1)} %rows.1, bf16[72,1536]{1,0:T(8,128)(2,1)} %grads.1, bf16[2,72,1536]{2,1,0:T(8,128)(2,1)} %copy-done.18), custom_call_target="tpu_custom_call" | custom-call | bytes 1048576 | tf_op jit(solution)/shard_map/pack/pallas_call | solution.py:48
  17.5 1.8 collective-permute-start.6
  19.4 3.6 %collective-permute-done.7.refs_0_ = bf16[2,72,1536]{2,1,0:T(8,128)(2,1)S(1)} collective-permute-done((bf16[2,72,1536]{2,1,0:T(8,128)(2,1)S(1)}, bf16[2,72,1536]{2,1,0:T(8,128)(2,1)S(1)}, u32[]{:S(2)}, u32[]{:S(2)}) %collective-permute-start.7) | collective-permute-done | bytes 442400 | tf_op jit(solution)/shard_map/ppermute | solution.py:28
  22.9 1.5 collective-permute-start.8
  24.4 5.7 %collective-permute-done.11.refs_4_ = bf16[2,72,1536]{2,1,0:T(8,128)(2,1)S(1)} collective-permute-done((bf16[2,72,1536]{2,1,0:T(8,128)(2,1)S(1)}, bf16[2,72,1536]{2,1,0:T(8,128)(2,1)S(1)}, u32[]{:S(2)}, u32[]{:S(2)}) %collective-permute-start.11) | collective-permute-done | bytes 442400 | tf_op jit(solution)/shard_map/ppermute | solution.py:28
  30.1 1.7 collective-permute-start.13
  31.9 5.0 %collective-permute-start.1 = (bf16[2,72,1536]{2,1,0:T(8,128)(2,1)}, bf16[2,72,1536]{2,1,0:T(8,128)(2,1)S(1)}, u32[]{:S(2)}, u32[]{:S(2)}) collective-permute-start(bf16[2,72,1536]{2,1,0:T(8,128)(2,1)} %pack.1), channel_id=1, source_target_pairs={{0,8},{1,9},{2,10},{3,11},{4,12},{5,13},{6,14},{7,15},{8,0},{9,1},... | collective-permute-start | bytes 1327112 | tf_op jit(solution)/shard_map/ppermute | solution.py:28
  37.2 3.0 %collective-permute-start.9 = (bf16[2,72,1536]{2,1,0:T(8,128)(2,1)S(1)}, bf16[2,72,1536]{2,1,0:T(8,128)(2,1)S(1)}, u32[]{:S(2)}, u32[]{:S(2)}) collective-permute-start(bf16[2,72,1536]{2,1,0:T(8,128)(2,1)S(1)} %collective-permute-done.7.refs_0_), channel_id=1, source_target_pairs={{0,3},{1,0},{2,1},{3,2},{4,7},{5,4},{6,5},{7,6},{8,11},{9,8},{10,9... | collective-permute-start | bytes 1327112 | tf_op jit(solution)/shard_map/ppermute | solution.py:24
  40.2 1.8 collective-permute-start.10
  42.0 1.2 collective-permute-done.13.refs_6_
  43.2 3.0 %collective-permute-start.14 = (bf16[2,72,1536]{2,1,0:T(8,128)(2,1)S(1)}, bf16[2,72,1536]{2,1,0:T(8,128)(2,1)S(1)}, u32[]{:S(2)}, u32[]{:S(2)}) collective-permute-start(bf16[2,72,1536]{2,1,0:T(8,128)(2,1)S(1)} %collective-permute-done.13.refs_6_), channel_id=1, source_target_pairs={{0,3},{1,0},{2,1},{3,2},{4,7},{5,4},{6,5},{7,6},{8,11},{9,8},{10,9... | collective-permute-start | bytes 1327112 | tf_op jit(solution)/shard_map/ppermute | solution.py:24
  46.2 2.3 %pad_maximum_fusion.refs_4_.refs_8_.refs_2_ = bf16[1120,1536]{1,0:T(8,128)(2,1)S(1)} fusion(bf16[560,1536]{1,0:T(8,128)(2,1)} %bitcast.8, bf16[560,1536]{1,0:T(8,128)(2,1)} %bitcast.9), kind=kLoop, calls=%fused_computation | loop fusion | flops 6881280 | bytes 6881280 | tf_op jit(solution)/shard_map/concatenate | solution.py:269
  48.8 2.2 %stage.4 = (bf16[288,1536]{1,0:T(8,128)(2,1)S(1)}, bf16[288,1536]{1,0:T(8,128)(2,1)S(1)}, bf16[288,1120]{1,0:T(8,128)(2,1)S(1)}, bf16[288,560]{1,0:T(8,128)(2,1)S(1)}) custom-call(bf16[2,72,1536]{2,1,0:T(8,128)(2,1)S(1)} %pad_maximum_fusion.1.refs_0_, bf16[2,72,1536]{2,1,0:T(8,128)(2,1)S(1)} %copy-done.19, ...), custom_call_target="tpu_custom_call" | custom-call | tf_op jit(solution)/shard_map/stage/pallas_call | solution.py:103
  51.0 3.5 %weight_grad.6.refs_2_ = f32[1536,1120]{1,0:T(8,128)S(1)} custom-call(s32[2]{0:T(128)S(1)} %pad_add_fusion.place, bf16[288,1536]{1,0:T(8,128)(2,1)S(1)} %get-tuple-element.41.refs_0_, bf16[288,1120]{1,0:T(8,128)(2,1)S(1)} %get-tuple-element.37.refs_1_), custom_call_target="tpu_custom_call" | custom-call | tf_op jit(solution)/shard_map/weight_grad/pallas_call | solution.py:178
  54.6 2.8 %copy-done.2 = f32[1536,1120]{1,0:T(8,128)} copy-done((f32[1536,1120]{1,0:T(8,128)}, f32[1536,1120]{1,0:T(8,128)S(1)}, u32[]{:S(2)}) %copy-start.2) | copy-done | bytes 6881304
  57.4 3.2 %collective-permute-start.3 = (bf16[2,72,1536]{2,1,0:T(8,128)(2,1)S(1)}, bf16[2,72,1536]{2,1,0:T(8,128)(2,1)S(1)}, u32[]{:S(2)}, u32[]{:S(2)}) collective-permute-start(bf16[2,72,1536]{2,1,0:T(8,128)(2,1)S(1)} %collective-permute-done.1.refs_0_), channel_id=1, source_target_pairs={{0,3},{1,0},{2,1},{3,2},{4,7},{5,4},{6,5},{7,6},{8,11},{9,8},{10,9... | collective-permute-start | bytes 1327112 | tf_op jit(solution)/shard_map/ppermute | solution.py:24
  60.6 1.6 collective-permute-done.14.refs_7_
  62.2 8.4 %stage.5 = (bf16[576,1536]{1,0:T(8,128)(2,1)S(1)}, bf16[576,1536]{1,0:T(8,128)(2,1)S(1)}, bf16[576,1120]{1,0:T(8,128)(2,1)S(1)}, bf16[576,560]{1,0:T(8,128)(2,1)...) custom-call(bf16[2,72,1536]{2,1,0:T(8,128)(2,1)S(1)} %collective-per, ...), custom_call_target="tpu_custom_call" | custom-call | flops 4954521600 | bytes 12582912 | tf_op jit(solution)/shard_map/stage/pallas_call | solution.py:103
  70.6 1.3 copy-done.20
  71.9 0.9 copy-done.22
  72.9 0.9 copy-done.28
  73.8 0.8 copy-done.36
  74.5 0.8 copy-done.37
  75.3 0.8 copy-done.38
  76.1 7.0 %weight_grad.7.refs_2_ = f32[1536,1120]{1,0:T(8,128)S(1)} custom-call(s32[2]{0:T(128)S(1)} %pad_add_fusion.place, bf16[576,1536]{1,0:T(8,128)(2,1)S(1)} %get-tuple-element.39.refs_0_, bf16[576,1120]{1,0:T(8,128)(2,1)S(1)} %get-tuple-element.40.refs_1_, f32[1536,1120]{1,0:T(8,128)} %copy-done.2), custom_call_target="tpu_custom_call" | custom-call | tf_op jit(solution)/shard_map/weight_grad/pallas_call | solution.py:178
  83.1 2.2 %stage.3 = (bf16[288,1536]{1,0:T(8,128)(2,1)S(1)}, bf16[288,1536]{1,0:T(8,128)(2,1)S(1)}, bf16[288,1120]{1,0:T(8,128)(2,1)S(1)}, bf16[288,560]{1,0:T(8,128)(2,1)S(1)}) custom-call(bf16[2,72,1536]{2,1,0:T(8,128)(2,1)S(1)} %collective-permute-done.1.refs_0_, bf16[2,72,1536]{2,1,0:T(8,128)(2,1)S(1)} %collective-permute-done.2.refs_1_, ...), custom_call_target="tpu_custom_call" | custom-call | tf_op jit(solution)/shard_map/stage/pallas_call | solution.py:103
  85.3 1.0 copy-done.26
  86.2 3.9 %weight_grad.8 = (bf16[4,2,96,1120]{3,2,1,0:T(8,128)(2,1)S(1)}, f32[4,2,96,1120]{3,2,1,0:T(8,128)S(1)}) custom-call(s32[2]{0:T(128)S(1)} %pad_add_fusion.place, bf16[288,1536]{1,0:T(8,128)(2,1)S(1)} %get-tuple-element.38.refs_0_, bf16[288,1120]{1,0:T(8,128)(2,1)S(1)} %get-tuple-element.36.refs_1_.refs_0_, f32[1536,1120]{1,0:T(8,128)S(1)} %weight_grad.7.refs_2_), custom_call_target="tpu_custom_call" | custom-call | tf_op jit(solution)/shard_map/weight_grad/pallas_call | solution.py:178
  90.3 3.7 %collective-permute-done.15.got = bf16[4,2,96,1120]{3,2,1,0:T(8,128)(2,1)S(1)} collective-permute-done((bf16[4,2,96,1120]{3,2,1,0:T(8,128)(2,1)S(1)}, bf16[4,2,96,1120]{3,2,1,0:T(8,128)(2,1)S(1)}, u32[]{:S(2)}, u32[]{:S(2)}) %collective-permute-start.15) | collective-permute-done | bytes 1720352 | tf_op jit(solution)/shard_map/ppermute | solution.py:40
  94.4 1.2 copy-done.3
  95.6 4.9 %all-to-all-start = ((bf16[4,2,96,1120]{3,2,1,0:T(8,128)(2,1)}), bf16[4,2,96,1120]{3,2,1,0:T(8,128)(2,1)}, u32[]{:S(2)}, u32[]{:S(2)}) async-start(bf16[4,2,96,1120]{3,2,1,0:T(8,128)(2,1)} %copy-done.3), calls=%async_computation | async-start | bytes 3538944 | tf_op jit(solution)/shard_map/all_to_all | solution.py:235
  100.5 2.9 %collective-permute-start.19 = (bf16[2,72,1536]{2,1,0:T(8,128)(2,1)}, bf16[2,72,1536]{2,1,0:T(8,128)(2,1)S(1)}, u32[]{:S(2)}, u32[]{:S(2)}) collective-permute-start(bf16[2,72,1536]{2,1,0:T(8,128)(2,1)} %copy-done.38), channel_id=1, source_target_pairs={{0,3},{1,0},{2,1},{3,2},{4,7},{5,4},{6,5},{7,6},{8,11},{9,8},{10,9... | collective-permute-start | bytes 1327112 | tf_op jit(solution)/shard_map/ppermute | solution.py:24
  103.4 1.8 collective-permute-start.21
  105.2 1.2 copy-done.25
  106.4 1.0 copy-done.35
  107.4 2.7 %weight_grad.9.refs_2_ = f32[1536,560]{1,0:T(8,128)S(1)} custom-call(s32[2]{0:T(128)S(1)} %pad_add_fusion.place, bf16[288,1536]{1,0:T(8,128)(2,1)S(1)} %copy-done.25, bf16[288,560]{1,0:T(8,128)(2,1)S(1)} %copy-done.35), custom_call_target="tpu_custom_call" | custom-call | tf_op jit(solution)/shard_map/weight_grad/pallas_call | solution.py:178
  110.2 3.4 %weight_grad.10.refs_2_ = f32[1536,560]{1,0:T(8,128)S(1)} custom-call(s32[2]{0:T(128)S(1)} %pad_add_fusion.place, bf16[576,1536]{1,0:T(8,128)(2,1)S(1)} %copy-done.21, bf16[576,560]{1,0:T(8,128)(2,1)S(1)} %copy-done.29, f32[1536,560]{1,0:T(8,128)S(1)} %weight_grad.9.refs_2_), custom_call_target="tpu_custom_call" | custom-call | tf_op jit(solution)/shard_map/weight_grad/pallas_call | solution.py:178
  113.6 3.5 %late_partials.1 = (f32[2,72,1536]{2,1,0:T(8,128)S(1)}, bf16[2,72,1536]{2,1,0:T(8,128)(2,1)}, bf16[2,72,1536]{2,1,0:T(8,128)(2,1)}, bf16[2,72,1536]{2,1,0:T(8,128)(2,1)}) custom-call(bf16[288,1120]{1,0:T(8,128)(2,1)S(1)} %copy-done.11, bf16[288,1120]{1,0:T(8,128)(2,1)S(1)} %copy-done.9, bf16[1120,1536]{1,0:T(8,128)(2,1)S(1)} %copy-done.1, ...), custom_call_target="tpu_custom_call" | custom-call | tf_op jit(solution)/shard_map/late_partials/pallas_call | solution.py:124
  117.1 5.4 %collective-permute-done.19.refs_4_.left = bf16[2,72,1536]{2,1,0:T(8,128)(2,1)S(1)} collective-permute-done((bf16[2,72,1536]{2,1,0:T(8,128)(2,1)}, bf16[2,72,1536]{2,1,0:T(8,128)(2,1)S(1)}, u32[]{:S(2)}, u32[]{:S(2)}) %collective-permute-start.19) | collective-permute-done | bytes 442400 | tf_op jit(solution)/shard_map/ppermute | solution.py:24
  122.6 3.3 %collective-permute-done.20.refs_5_.right = bf16[2,72,1536]{2,1,0:T(8,128)(2,1)S(1)} collective-permute-done((bf16[2,72,1536]{2,1,0:T(8,128)(2,1)}, bf16[2,72,1536]{2,1,0:T(8,128)(2,1)S(1)}, u32[]{:S(2)}, u32[]{:S(2)}) %collective-permute-start.20) | collective-permute-done | bytes 442400 | tf_op jit(solution)/shard_map/ppermute | solution.py:24
  125.9 3.7 %weight_grad.11 = (bf16[4,2,96,560]{3,2,1,0:T(8,128)(2,1)}, f32[4,2,96,560]{3,2,1,0:T(8,128)S(1)}) custom-call(s32[2]{0:T(128)S(1)} %pad_add_fusion.place, bf16[288,1536]{1,0:T(8,128)(2,1)S(1)} %copy-done.27, bf16[288,560]{1,0:T(8,128)(2,1)S(1)} %copy-done.33, f32[1536,560]{1,0:T(8,128)S(1)} %weight_grad.10.refs_2_, ...), custom_call_target="tpu_custom_call" | custom-call | tf_op jit(solution)/shard_map/weight_grad/pallas_call | solution.py:178
  130.1 1.7 collective-permute-start.17
  132.4 2.3 %add_chunks.2 = (f32[96,1120]{1,0:T(8,128)S(1)}, bf16[96,1120]{1,0:T(8,128)(2,1)}) custom-call(s32[2]{0:T(128)S(1)} %pad_add_fusion.place, bf16[4,2,96,1120]{3,2,1,0:T(8,128)(2,1)} %all-to-all-done.refs_0_.got), custom_call_target="tpu_custom_call" | custom-call | tf_op jit(solution)/shard_map/add_chunks/pallas_call | solution.py:202
  134.7 0.8 copy-done.30
  135.5 7.5 %collective-permute-done.16.refs_1_.left = bf16[2,72,1536]{2,1,0:T(8,128)(2,1)S(1)} collective-permute-done((bf16[2,72,1536]{2,1,0:T(8,128)(2,1)}, bf16[2,72,1536]{2,1,0:T(8,128)(2,1)S(1)}, u32[]{:S(2)}, u32[]{:S(2)}) %collective-permute-start.16) | collective-permute-done | bytes 442400 | tf_op jit(solution)/shard_map/ppermute | solution.py:24
  143.0 1.6 over_cores.3.refs_0_
  144.6 5.0 %all-to-all-start.1 = ((bf16[4,2,96,560]{3,2,1,0:T(8,128)(2,1)}), bf16[4,2,96,560]{3,2,1,0:T(8,128)(2,1)S(1)}, u32[]{:S(2)}, u32[]{:S(2)}) async-start(bf16[4,2,96,560]{3,2,1,0:T(8,128)(2,1)} %over_cores.3.refs_0_), calls=%async_computation.1 | async-start | bytes 1966080 | tf_op jit(solution)/shard_map/all_to_all | solution.py:235
  149.6 1.2 copy-done.23
  151.1 2.6 %collective-permute-start.24 = (bf16[72,1536]{1,0:T(8,128)(2,1)S(1)}, bf16[72,1536]{1,0:T(8,128)(2,1)S(1)}, u32[]{:S(2)}, u32[]{:S(2)}) collective-permute-start(bf16[72,1536]{1,0:T(8,128)(2,1)S(1)} %get-tuple-element.60.refs_0_), channel_id=1, source_target_pairs={{0,12},{1,13},{2,14},{3,15},{4,0},{5,1},{6,2},{7,3},{8,4},{9,5},{1... | collective-permute-start | bytes 663560 | tf_op jit(solution)/shard_map/ppermute | solution.py:28
  153.8 1.4 add_parts.3
  155.1 4.9 %collective-permute-start.25 = (bf16[72,1536]{1,0:T(8,128)(2,1)S(1)}, bf16[72,1536]{1,0:T(8,128)(2,1)S(1)}, u32[]{:S(2)}, u32[]{:S(2)}) collective-permute-start(bf16[72,1536]{1,0:T(8,128)(2,1)S(1)} %get-tuple-element.63), channel_id=1, source_target_pairs={{0,8},{1,9},{2,10},{3,11},{4,12},{5,13},{6,14},{7,15},{8,0},{9,1},... | collective-permute-start | bytes 663560 | tf_op jit(solution)/shard_map/ppermute | solution.py:28
  160.0 1.0 add_multiply_fusion
  161.0 0.8 fusion
  163.3 7.7 %collective-permute-done.25 = bf16[72,1536]{1,0:T(8,128)(2,1)S(1)} collective-permute-done((bf16[72,1536]{1,0:T(8,128)(2,1)S(1)}, bf16[72,1536]{1,0:T(8,128)(2,1)S(1)}, u32[]{:S(2)}, u32[]{:S(2)}) %collective-permute-start.25) | collective-permute-done | bytes 221216 | tf_op jit(solution)/shard_map/ppermute | solution.py:28
  171.0 9.3 %collective-permute-done.23 = bf16[72,1536]{1,0:T(8,128)(2,1)S(1)} collective-permute-done((bf16[72,1536]{1,0:T(8,128)(2,1)S(1)}, bf16[72,1536]{1,0:T(8,128)(2,1)S(1)}, u32[]{:S(2)}, u32[]{:S(2)}) %collective-permute-start.23) | collective-permute-done | bytes 221216 | tf_op jit(solution)/shard_map/ppermute | solution.py:28
  180.3 0.8 add_convert_fusion
  181.1 0.7 multiply_bitcast_fusion
  (98 shorter events, 4.0 us)
Async XLA Ops:
  1.7 13.2 %collective-permute-start = (bf16[2,72,1536]{2,1,0:T(8,128)(2,1)S(1)}, bf16[2,72,1536]{2,1,0:T(8,128)(2,1)S(1)}, u32[]{:S(2)}, u32[]{:S(2)}) collective-permute-start(bf16[2,72,1536]{2,1,0:T(8,128)(2,1)S(1)} %pad_maximum_fusion.1.refs_0_), channel_id=1, source_target_pairs={{0,1},{1,2},{2,3},{3,0},{4,5},{5,6},{6,7},{7,4},{8,9},{9,10},{10,1... | collective-permute-start | bytes 1327112 | tf_op jit(solution)/shard_map/ppermute | solution.py:24
  3.3 19.6 %collective-permute-start.7 = (bf16[2,72,1536]{2,1,0:T(8,128)(2,1)S(1)}, bf16[2,72,1536]{2,1,0:T(8,128)(2,1)S(1)}, u32[]{:S(2)}, u32[]{:S(2)}) collective-permute-start(bf16[2,72,1536]{2,1,0:T(8,128)(2,1)S(1)} %pad_maximum_fusion.1.refs_0_), channel_id=1, source_target_pairs={{0,4},{1,5},{2,6},{3,7},{4,8},{5,9},{6,10},{7,11},{8,12},{9,13},{1... | collective-permute-start | bytes 1327112 | tf_op jit(solution)/shard_map/ppermute | solution.py:28
  6.6 23.6 %collective-permute-start.11 = (bf16[2,72,1536]{2,1,0:T(8,128)(2,1)S(1)}, bf16[2,72,1536]{2,1,0:T(8,128)(2,1)S(1)}, u32[]{:S(2)}, u32[]{:S(2)}) collective-permute-start(bf16[2,72,1536]{2,1,0:T(8,128)(2,1)S(1)} %pad_maximum_fusion.1.refs_0_), channel_id=1, source_target_pairs={{0,12},{1,13},{2,14},{3,15},{4,0},{5,1},{6,2},{7,3},{8,4},{9,5},{1... | collective-permute-start | bytes 1327112 | tf_op jit(solution)/shard_map/ppermute | solution.py:28
  9.6 27.3 %collective-permute-start.5 = (bf16[2,72,1536]{2,1,0:T(8,128)(2,1)S(1)}, bf16[2,72,1536]{2,1,0:T(8,128)(2,1)S(1)}, u32[]{:S(2)}, u32[]{:S(2)}) collective-permute-start(bf16[2,72,1536]{2,1,0:T(8,128)(2,1)S(1)} %pad_maximum_fusion.1.refs_0_), channel_id=1, source_target_pairs={{0,3},{1,0},{2,1},{3,2},{4,7},{5,4},{6,5},{7,6},{8,11},{9,8},{10,9... | collective-permute-start | bytes 1327112 | tf_op jit(solution)/shard_map/ppermute | solution.py:24
  17.5 19.7 %collective-permute-start.6 = (bf16[2,72,1536]{2,1,0:T(8,128)(2,1)}, bf16[2,72,1536]{2,1,0:T(8,128)(2,1)S(1)}, u32[]{:S(2)}, u32[]{:S(2)}) collective-permute-start(bf16[2,72,1536]{2,1,0:T(8,128)(2,1)} %pack.1), channel_id=1, source_target_pairs={{0,2},{1,3},{2,0},{3,1},{4,6},{5,7},{6,4},{7,5},{8,10},{9,11},{10,... | collective-permute-start | bytes 1327112 | tf_op jit(solution)/shard_map/ppermute | solution.py:24
  22.9 17.3 %collective-permute-start.8 = (bf16[2,72,1536]{2,1,0:T(8,128)(2,1)S(1)}, bf16[2,72,1536]{2,1,0:T(8,128)(2,1)S(1)}, u32[]{:S(2)}, u32[]{:S(2)}) collective-permute-start(bf16[2,72,1536]{2,1,0:T(8,128)(2,1)S(1)} %collective-permute-done.7.refs_0_), channel_id=1, source_target_pairs={{0,1},{1,2},{2,3},{3,0},{4,5},{5,6},{6,7},{7,4},{8,9},{9,10},{10,1... | collective-permute-start | bytes 1327112 | tf_op jit(solution)/shard_map/ppermute | solution.py:24
  30.1 13.1 %collective-permute-start.13 = (bf16[2,72,1536]{2,1,0:T(8,128)(2,1)S(1)}, bf16[2,72,1536]{2,1,0:T(8,128)(2,1)S(1)}, u32[]{:S(2)}, u32[]{:S(2)}) collective-permute-start(bf16[2,72,1536]{2,1,0:T(8,128)(2,1)S(1)} %collective-permute-done.11.refs_4_), channel_id=1, source_target_pairs={{0,3},{1,0},{2,1},{3,2},{4,7},{5,4},{6,5},{7,6},{8,11},{9,8},{10,9... | collective-permute-start | bytes 1327112 | tf_op jit(solution)/shard_map/ppermute | solution.py:24
  31.9 25.4 %collective-permute-start.1 = (bf16[2,72,1536]{2,1,0:T(8,128)(2,1)}, bf16[2,72,1536]{2,1,0:T(8,128)(2,1)S(1)}, u32[]{:S(2)}, u32[]{:S(2)}) collective-permute-start(bf16[2,72,1536]{2,1,0:T(8,128)(2,1)} %pack.1), channel_id=1, source_target_pairs={{0,8},{1,9},{2,10},{3,11},{4,12},{5,13},{6,14},{7,15},{8,0},{9,1},... | collective-permute-start | bytes 1327112 | tf_op jit(solution)/shard_map/ppermute | solution.py:28
  36.9 20.5 %collective-permute-start.12 = (bf16[2,72,1536]{2,1,0:T(8,128)(2,1)S(1)}, bf16[2,72,1536]{2,1,0:T(8,128)(2,1)S(1)}, u32[]{:S(2)}, u32[]{:S(2)}) collective-permute-start(bf16[2,72,1536]{2,1,0:T(8,128)(2,1)S(1)} %collective-permute-done.11.refs_4_), channel_id=1, source_target_pairs={{0,1},{1,2},{2,3},{3,0},{4,5},{5,6},{6,7},{7,4},{8,9},{9,10},{10,1... | collective-permute-start | bytes 1327112 | tf_op jit(solution)/shard_map/ppermute | solution.py:24
  37.2 23.4 %collective-permute-start.9 = (bf16[2,72,1536]{2,1,0:T(8,128)(2,1)S(1)}, bf16[2,72,1536]{2,1,0:T(8,128)(2,1)S(1)}, u32[]{:S(2)}, u32[]{:S(2)}) collective-permute-start(bf16[2,72,1536]{2,1,0:T(8,128)(2,1)S(1)} %collective-permute-done.7.refs_0_), channel_id=1, source_target_pairs={{0,3},{1,0},{2,1},{3,2},{4,7},{5,4},{6,5},{7,6},{8,11},{9,8},{10,9... | collective-permute-start | bytes 1327112 | tf_op jit(solution)/shard_map/ppermute | solution.py:24
  40.2 20.5 %collective-permute-start.10 = (bf16[2,72,1536]{2,1,0:T(8,128)(2,1)S(1)}, bf16[2,72,1536]{2,1,0:T(8,128)(2,1)S(1)}, u32[]{:S(2)}, u32[]{:S(2)}) collective-permute-start(bf16[2,72,1536]{2,1,0:T(8,128)(2,1)S(1)} %collective-permute-done.8.refs_1_), channel_id=1, source_target_pairs={{0,1},{1,2},{2,3},{3,0},{4,5},{5,6},{6,7},{7,4},{8,9},{9,10},{10,1... | collective-permute-start | bytes 1327112 | tf_op jit(solution)/shard_map/ppermute | solution.py:24
  43.2 19.0 %collective-permute-start.14 = (bf16[2,72,1536]{2,1,0:T(8,128)(2,1)S(1)}, bf16[2,72,1536]{2,1,0:T(8,128)(2,1)S(1)}, u32[]{:S(2)}, u32[]{:S(2)}) collective-permute-start(bf16[2,72,1536]{2,1,0:T(8,128)(2,1)S(1)} %collective-permute-done.13.refs_6_), channel_id=1, source_target_pairs={{0,3},{1,0},{2,1},{3,2},{4,7},{5,4},{6,5},{7,6},{8,11},{9,8},{10,9... | collective-permute-start | bytes 1327112 | tf_op jit(solution)/shard_map/ppermute | solution.py:24
  46.2 2.5 %copy-start.5 = (bf16[560,1536]{1,0:T(8,128)(2,1)S(1)}, bf16[560,1536]{1,0:T(8,128)(2,1)}, u32[]{:S(2)}) copy-start(bf16[560,1536]{1,0:T(8,128)(2,1)} %refs_9_.1) | copy-start | bytes 5160964
  46.2 2.6 %copy-start.19 = (bf16[2,72,1536]{2,1,0:T(8,128)(2,1)S(1)}, bf16[2,72,1536]{2,1,0:T(8,128)(2,1)}, u32[]{:S(2)}) copy-start(bf16[2,72,1536]{2,1,0:T(8,128)(2,1)} %copy-done.18) | copy-start | bytes 1327108
  48.7 2.2 %copy-start = (bf16[1120,1536]{1,0:T(8,128)(2,1)}, bf16[1120,1536]{1,0:T(8,128)(2,1)S(1)}, u32[]{:S(2)}) copy-start(bf16[1120,1536]{1,0:T(8,128)(2,1)S(1)} %pad_maximum_fusion.refs_4_.refs_8_.refs_2_) | copy-start | bytes 10321924
  50.9 3.6 %copy-start.8 = (bf16[288,1120]{1,0:T(8,128)(2,1)}, bf16[288,1120]{1,0:T(8,128)(2,1)S(1)}, u32[]{:S(2)}) copy-start(bf16[288,1120]{1,0:T(8,128)(2,1)S(1)} %get-tuple-element.37.refs_1_) | copy-start | bytes 1935364
  51.0 3.6 %copy-start.24 = (bf16[288,1536]{1,0:T(8,128)(2,1)}, bf16[288,1536]{1,0:T(8,128)(2,1)S(1)}, u32[]{:S(2)}) copy-start(bf16[288,1536]{1,0:T(8,128)(2,1)S(1)} %get-tuple-element.56.refs_0_) | copy-start | bytes 2654212
  51.0 3.6 %copy-start.34 = (bf16[288,560]{1,0:T(8,128)(2,1)}, bf16[288,560]{1,0:T(8,128)(2,1)S(1)}, u32[]{:S(2)}) copy-start(bf16[288,560]{1,0:T(8,128)(2,1)S(1)} %get-tuple-element.57.refs_1_) | copy-start | bytes 967684
  54.6 2.8 %copy-start.2 = (f32[1536,1120]{1,0:T(8,128)}, f32[1536,1120]{1,0:T(8,128)S(1)}, u32[]{:S(2)}) copy-start(f32[1536,1120]{1,0:T(8,128)S(1)} %weight_grad.6.refs_2_) | copy-start | bytes 20643844
  57.4 25.7 %collective-permute-start.2 = (bf16[2,72,1536]{2,1,0:T(8,128)(2,1)S(1)}, bf16[2,72,1536]{2,1,0:T(8,128)(2,1)S(1)}, u32[]{:S(2)}, u32[]{:S(2)}) collective-permute-start(bf16[2,72,1536]{2,1,0:T(8,128)(2,1)S(1)} %collective-permute-done.1.refs_0_), channel_id=1, source_target_pairs={{0,1},{1,2},{2,3},{3,0},{4,5},{5,6},{6,7},{7,4},{8,9},{9,10},{10,1... | collective-permute-start | bytes 1327112 | tf_op jit(solution)/shard_map/ppermute | solution.py:24
  57.4 25.7 %collective-permute-start.3 = (bf16[2,72,1536]{2,1,0:T(8,128)(2,1)S(1)}, bf16[2,72,1536]{2,1,0:T(8,128)(2,1)S(1)}, u32[]{:S(2)}, u32[]{:S(2)}) collective-permute-start(bf16[2,72,1536]{2,1,0:T(8,128)(2,1)S(1)} %collective-permute-done.1.refs_0_), channel_id=1, source_target_pairs={{0,3},{1,0},{2,1},{3,2},{4,7},{5,4},{6,5},{7,6},{8,11},{9,8},{10,9... | collective-permute-start | bytes 1327112 | tf_op jit(solution)/shard_map/ppermute | solution.py:24
  60.6 22.4 %collective-permute-start.4 = (bf16[2,72,1536]{2,1,0:T(8,128)(2,1)S(1)}, bf16[2,72,1536]{2,1,0:T(8,128)(2,1)S(1)}, u32[]{:S(2)}, u32[]{:S(2)}) collective-permute-start(bf16[2,72,1536]{2,1,0:T(8,128)(2,1)S(1)} %collective-permute-done.1.refs_0_), channel_id=1, source_target_pairs={{0,2},{1,3},{2,0},{3,1},{4,6},{5,7},{6,4},{7,5},{8,10},{9,11},{10,... | collective-permute-start | bytes 1327112 | tf_op jit(solution)/shard_map/ppermute | solution.py:24
  70.6 1.3 copy-start.20
  71.9 0.9 copy-start.22
  72.9 0.9 copy-start.28
  76.1 7.0 %copy-start.1 = (bf16[1120,1536]{1,0:T(8,128)(2,1)S(1)}, bf16[1120,1536]{1,0:T(8,128)(2,1)}, u32[]{:S(2)}) copy-start(bf16[1120,1536]{1,0:T(8,128)(2,1)} %copy-done) | copy-start | bytes 10321924
  85.3 1.0 copy-start.26
  86.2 4.0 %copy-start.10 = (bf16[288,1120]{1,0:T(8,128)(2,1)}, bf16[288,1120]{1,0:T(8,128)(2,1)S(1)}, u32[]{:S(2)}) copy-start(bf16[288,1120]{1,0:T(8,128)(2,1)S(1)} %get-tuple-element.36.refs_1_.refs_0_) | copy-start | bytes 1935364
  86.2 4.0 %copy-start.32 = (bf16[288,560]{1,0:T(8,128)(2,1)}, bf16[288,560]{1,0:T(8,128)(2,1)S(1)}, u32[]{:S(2)}) copy-start(bf16[288,560]{1,0:T(8,128)(2,1)S(1)} %get-tuple-element.53.refs_1_) | copy-start | bytes 967684
  90.2 3.8 %collective-permute-start.15 = (bf16[4,2,96,1120]{3,2,1,0:T(8,128)(2,1)S(1)}, bf16[4,2,96,1120]{3,2,1,0:T(8,128)(2,1)S(1)}, u32[]{:S(2)}, u32[]{:S(2)}) collective-permute-start(bf16[4,2,96,1120]{3,2,1,0:T(8,128)(2,1)S(1)} %get-tuple-element.43), channel_id=1, source_target_pairs={{0,16},{16,0},{32,48},{48,32},{64,80},{80,64},{96,112},{112,96},{1... | collective-permute-start | bytes 5160968 | tf_op jit(solution)/shard_map/ppermute | solution.py:40
  94.3 1.2 copy-start.3
  95.6 36.8 %all-to-all-start = ((bf16[4,2,96,1120]{3,2,1,0:T(8,128)(2,1)}), bf16[4,2,96,1120]{3,2,1,0:T(8,128)(2,1)}, u32[]{:S(2)}, u32[]{:S(2)}) async-start(bf16[4,2,96,1120]{3,2,1,0:T(8,128)(2,1)} %copy-done.3), calls=%async_computation | async-start | bytes 3538944 | tf_op jit(solution)/shard_map/all_to_all | solution.py:235
  100.5 22.1 %collective-permute-start.19 = (bf16[2,72,1536]{2,1,0:T(8,128)(2,1)}, bf16[2,72,1536]{2,1,0:T(8,128)(2,1)S(1)}, u32[]{:S(2)}, u32[]{:S(2)}) collective-permute-start(bf16[2,72,1536]{2,1,0:T(8,128)(2,1)} %copy-done.38), channel_id=1, source_target_pairs={{0,3},{1,0},{2,1},{3,2},{4,7},{5,4},{6,5},{7,6},{8,11},{9,8},{10,9... | collective-permute-start | bytes 1327112 | tf_op jit(solution)/shard_map/ppermute | solution.py:24
  103.4 22.4 %collective-permute-start.20 = (bf16[2,72,1536]{2,1,0:T(8,128)(2,1)}, bf16[2,72,1536]{2,1,0:T(8,128)(2,1)S(1)}, u32[]{:S(2)}, u32[]{:S(2)}) collective-permute-start(bf16[2,72,1536]{2,1,0:T(8,128)(2,1)} %copy-done.37), channel_id=1, source_target_pairs={{0,1},{1,2},{2,3},{3,0},{4,5},{5,6},{6,7},{7,4},{8,9},{9,10},{10,1... | collective-permute-start | bytes 1327112 | tf_op jit(solution)/shard_map/ppermute | solution.py:24
  103.4 22.4 %collective-permute-start.21 = (bf16[2,72,1536]{2,1,0:T(8,128)(2,1)}, bf16[2,72,1536]{2,1,0:T(8,128)(2,1)S(1)}, u32[]{:S(2)}, u32[]{:S(2)}) collective-permute-start(bf16[2,72,1536]{2,1,0:T(8,128)(2,1)} %copy-done.36), channel_id=1, source_target_pairs={{0,2},{1,3},{2,0},{3,1},{4,6},{5,7},{6,4},{7,5},{8,10},{9,11},{10,... | collective-permute-start | bytes 1327112 | tf_op jit(solution)/shard_map/ppermute | solution.py:24
  105.2 1.2 copy-start.25
  106.4 1.0 copy-start.35
  107.4 2.7 %copy-start.21 = (bf16[576,1536]{1,0:T(8,128)(2,1)S(1)}, bf16[576,1536]{1,0:T(8,128)(2,1)}, u32[]{:S(2)}) copy-start(bf16[576,1536]{1,0:T(8,128)(2,1)} %copy-done.20) | copy-start | bytes 5308420
  107.4 2.7 %copy-start.29 = (bf16[576,560]{1,0:T(8,128)(2,1)S(1)}, bf16[576,560]{1,0:T(8,128)(2,1)}, u32[]{:S(2)}) copy-start(bf16[576,560]{1,0:T(8,128)(2,1)} %copy-done.28) | copy-start | bytes 1935364
  110.1 3.4 %copy-start.4 = (bf16[4,2,96,1120]{3,2,1,0:T(8,128)(2,1)S(1)}, bf16[4,2,96,1120]{3,2,1,0:T(8,128)(2,1)}, u32[]{:S(2)}) copy-start(bf16[4,2,96,1120]{3,2,1,0:T(8,128)(2,1)} %copy-done.3) | copy-start | bytes 5160964
  110.1 3.4 %copy-start.9 = (bf16[288,1120]{1,0:T(8,128)(2,1)S(1)}, bf16[288,1120]{1,0:T(8,128)(2,1)}, u32[]{:S(2)}) copy-start(bf16[288,1120]{1,0:T(8,128)(2,1)} %copy-done.8) | copy-start | bytes 1935364
  110.1 3.4 %copy-start.11 = (bf16[288,1120]{1,0:T(8,128)(2,1)S(1)}, bf16[288,1120]{1,0:T(8,128)(2,1)}, u32[]{:S(2)}) copy-start(bf16[288,1120]{1,0:T(8,128)(2,1)} %copy-done.10) | copy-start | bytes 1935364
  113.6 12.3 %copy-start.27 = (bf16[288,1536]{1,0:T(8,128)(2,1)S(1)}, bf16[288,1536]{1,0:T(8,128)(2,1)}, u32[]{:S(2)}) copy-start(bf16[288,1536]{1,0:T(8,128)(2,1)} %copy-done.26) | copy-start | bytes 2654212
  113.6 12.3 %copy-start.33 = (bf16[288,560]{1,0:T(8,128)(2,1)S(1)}, bf16[288,560]{1,0:T(8,128)(2,1)}, u32[]{:S(2)}) copy-start(bf16[288,560]{1,0:T(8,128)(2,1)} %copy-done.32) | copy-start | bytes 967684
  117.1 12.5 %copy-start.6 = (f32[2,72,1536]{2,1,0:T(8,128)}, f32[2,72,1536]{2,1,0:T(8,128)S(1)}, u32[]{:S(2)}) copy-start(f32[2,72,1536]{2,1,0:T(8,128)S(1)} %get-tuple-element.44.refs_3_.own) | copy-start | bytes 2654212
  122.6 7.1 %copy-start.12 = (bf16[2,72,1536]{2,1,0:T(8,128)(2,1)}, bf16[2,72,1536]{2,1,0:T(8,128)(2,1)S(1)}, u32[]{:S(2)}) copy-start(bf16[2,72,1536]{2,1,0:T(8,128)(2,1)S(1)} %collective-permute-done.19.refs_4_.left) | copy-start | bytes 1327108
  125.9 3.8 %copy-start.14 = (bf16[2,72,1536]{2,1,0:T(8,128)(2,1)}, bf16[2,72,1536]{2,1,0:T(8,128)(2,1)S(1)}, u32[]{:S(2)}) copy-start(bf16[2,72,1536]{2,1,0:T(8,128)(2,1)S(1)} %collective-permute-done.20.refs_5_.right) | copy-start | bytes 1327108
  125.9 3.8 %copy-start.16 = (bf16[2,72,1536]{2,1,0:T(8,128)(2,1)}, bf16[2,72,1536]{2,1,0:T(8,128)(2,1)S(1)}, u32[]{:S(2)}) copy-start(bf16[2,72,1536]{2,1,0:T(8,128)(2,1)S(1)} %collective-permute-done.21.refs_6_.far) | copy-start | bytes 1327108
  129.7 13.4 %collective-permute-start.22 = (bf16[4,2,96,560]{3,2,1,0:T(8,128)(2,1)}, bf16[4,2,96,560]{3,2,1,0:T(8,128)(2,1)S(1)}, u32[]{:S(2)}, u32[]{:S(2)}) collective-permute-start(bf16[4,2,96,560]{3,2,1,0:T(8,128)(2,1)} %get-tuple-element.59), channel_id=1, source_target_pairs={{0,16},{16,0},{32,48},{48,32},{64,80},{80,64},{96,112},{112,96},{1... | collective-permute-start | bytes 2580488 | tf_op jit(solution)/shard_map/ppermute | solution.py:40
  129.8 13.3 %collective-permute-start.16 = (bf16[2,72,1536]{2,1,0:T(8,128)(2,1)}, bf16[2,72,1536]{2,1,0:T(8,128)(2,1)S(1)}, u32[]{:S(2)}, u32[]{:S(2)}) collective-permute-start(bf16[2,72,1536]{2,1,0:T(8,128)(2,1)} %get-tuple-element.45), channel_id=1, source_target_pairs={{0,3},{1,0},{2,1},{3,2},{4,7},{5,4},{6,5},{7,6},{8,11},{9,8},{10,9... | collective-permute-start | bytes 1327112 | tf_op jit(solution)/shard_map/ppermute | solution.py:24
  130.1 23.6 %collective-permute-start.17 = (bf16[2,72,1536]{2,1,0:T(8,128)(2,1)}, bf16[2,72,1536]{2,1,0:T(8,128)(2,1)}, u32[]{:S(2)}, u32[]{:S(2)}) collective-permute-start(bf16[2,72,1536]{2,1,0:T(8,128)(2,1)} %get-tuple-element.46), channel_id=1, source_target_pairs={{0,1},{1,2},{2,3},{3,0},{4,5},{5,6},{6,7},{7,4},{8,9},{9,10},{10,1... | collective-permute-start | bytes 1327112 | tf_op jit(solution)/shard_map/ppermute | solution.py:24
  131.9 21.9 %collective-permute-start.18 = (bf16[2,72,1536]{2,1,0:T(8,128)(2,1)}, bf16[2,72,1536]{2,1,0:T(8,128)(2,1)}, u32[]{:S(2)}, u32[]{:S(2)}) collective-permute-start(bf16[2,72,1536]{2,1,0:T(8,128)(2,1)} %get-tuple-element.47), channel_id=1, source_target_pairs={{0,2},{1,3},{2,0},{3,1},{4,6},{5,7},{6,4},{7,5},{8,10},{9,11},{10,... | collective-permute-start | bytes 1327112 | tf_op jit(solution)/shard_map/ppermute | solution.py:24
  135.5 24.5 %collective-permute-start.26 = (bf16[96,1120]{1,0:T(8,128)(2,1)}, bf16[96,1120]{1,0:T(8,128)(2,1)}, u32[]{:S(2)}, u32[]{:S(2)}) collective-permute-start(bf16[96,1120]{1,0:T(8,128)(2,1)} %get-tuple-element.65), channel_id=1, source_target_pairs={{0,32},{16,48},{32,0},{48,16},{64,96},{80,112},{96,64},{112,80},{1... | collective-permute-start | bytes 645128 | tf_op jit(solution)/shard_map/ppermute | solution.py:36
  144.6 5.0 %copy-start.13 = (bf16[2,72,1536]{2,1,0:T(8,128)(2,1)S(1)}, bf16[2,72,1536]{2,1,0:T(8,128)(2,1)}, u32[]{:S(2)}) copy-start(bf16[2,72,1536]{2,1,0:T(8,128)(2,1)} %copy-done.12) | copy-start | bytes 1327108
  144.6 5.0 %copy-start.15 = (bf16[2,72,1536]{2,1,0:T(8,128)(2,1)S(1)}, bf16[2,72,1536]{2,1,0:T(8,128)(2,1)}, u32[]{:S(2)}) copy-start(bf16[2,72,1536]{2,1,0:T(8,128)(2,1)} %copy-done.14) | copy-start | bytes 1327108
  144.6 5.0 %copy-start.17 = (bf16[2,72,1536]{2,1,0:T(8,128)(2,1)S(1)}, bf16[2,72,1536]{2,1,0:T(8,128)(2,1)}, u32[]{:S(2)}) copy-start(bf16[2,72,1536]{2,1,0:T(8,128)(2,1)} %copy-done.16) | copy-start | bytes 1327108
  144.6 17.3 %all-to-all-start.1 = ((bf16[4,2,96,560]{3,2,1,0:T(8,128)(2,1)}), bf16[4,2,96,560]{3,2,1,0:T(8,128)(2,1)S(1)}, u32[]{:S(2)}, u32[]{:S(2)}) async-start(bf16[4,2,96,560]{3,2,1,0:T(8,128)(2,1)} %over_cores.3.refs_0_), calls=%async_computation.1 | async-start | bytes 1966080 | tf_op jit(solution)/shard_map/all_to_all | solution.py:235
  149.6 4.2 %copy-start.7 = (f32[2,72,1536]{2,1,0:T(8,128)S(1)}, f32[2,72,1536]{2,1,0:T(8,128)}, u32[]{:S(2)}) copy-start(f32[2,72,1536]{2,1,0:T(8,128)} %copy-done.6) | copy-start | bytes 2654212
  149.6 1.2 copy-start.23
  151.1 8.9 %copy-start.31 = (f32[96,1120]{1,0:T(8,128)S(1)}, f32[96,1120]{1,0:T(8,128)}, u32[]{:S(2)}) copy-start(f32[96,1120]{1,0:T(8,128)} %copy-done.30) | copy-start | bytes 1290244
  151.1 29.2 %collective-permute-start.24 = (bf16[72,1536]{1,0:T(8,128)(2,1)S(1)}, bf16[72,1536]{1,0:T(8,128)(2,1)S(1)}, u32[]{:S(2)}, u32[]{:S(2)}) collective-permute-start(bf16[72,1536]{1,0:T(8,128)(2,1)S(1)} %get-tuple-element.60.refs_0_), channel_id=1, source_target_pairs={{0,12},{1,13},{2,14},{3,15},{4,0},{5,1},{6,2},{7,3},{8,4},{9,5},{1... | collective-permute-start | bytes 663560 | tf_op jit(solution)/shard_map/ppermute | solution.py:28
  155.1 15.9 %collective-permute-start.25 = (bf16[72,1536]{1,0:T(8,128)(2,1)S(1)}, bf16[72,1536]{1,0:T(8,128)(2,1)S(1)}, u32[]{:S(2)}, u32[]{:S(2)}) collective-permute-start(bf16[72,1536]{1,0:T(8,128)(2,1)S(1)} %get-tuple-element.63), channel_id=1, source_target_pairs={{0,8},{1,9},{2,10},{3,11},{4,12},{5,13},{6,14},{7,15},{8,0},{9,1},... | collective-permute-start | bytes 663560 | tf_op jit(solution)/shard_map/ppermute | solution.py:28
  160.0 20.4 %collective-permute-start.23 = (bf16[72,1536]{1,0:T(8,128)(2,1)S(1)}, bf16[72,1536]{1,0:T(8,128)(2,1)S(1)}, u32[]{:S(2)}, u32[]{:S(2)}) collective-permute-start(bf16[72,1536]{1,0:T(8,128)(2,1)S(1)} %get-tuple-element.62), channel_id=1, source_target_pairs={{0,4},{1,5},{2,6},{3,7},{4,8},{5,9},{6,10},{7,11},{8,12},{9,13},{1... | collective-permute-start | bytes 663560 | tf_op jit(solution)/shard_map/ppermute | solution.py:28
  162.6 18.5 %collective-permute-start.27 = (bf16[96,560]{1,0:T(8,128)(2,1)S(1)}, bf16[96,560]{1,0:T(8,128)(2,1)S(1)}, u32[]{:S(2)}, u32[]{:S(2)}) collective-permute-start(bf16[96,560]{1,0:T(8,128)(2,1)S(1)} %get-tuple-element.67), channel_id=1, source_target_pairs={{0,32},{16,48},{32,0},{48,16},{64,96},{80,112},{96,64},{112,80},{1... | collective-permute-start | bytes 322568 | tf_op jit(solution)/shard_map/ppermute | solution.py:36
  (5 other events, 3.9 us)
